TPU v7x, 32 devices: a whole 2x2x4 slice. The times are simulated.
32 devices in a mesh: row: 8 (over z, x), col: 4 (over y, core).
Axes of the slice: x: 2, y: 2, z: 4, core: 2. Of those that a mesh axis runs over, the one named last changes fastest.
Arguments:
- kernel_tiles: float32 [1, 8, 2, 4, 1024, 1024], P(None, 'row', None, 'col'), may hold values from 0 to 2.5, as said below
- profile: int32 [2, 8], replicated, may hold values from 0 to 7, as said below
Outputs:
- factored: float32 [1, 8, 2, 4, 1024, 1024], P(None, 'row', None, 'col')
Inputs may be any that keep to these rules, and one draw needn't show every extreme that they name: profile[0] never falls along the tile rows; profile[0, i] >= i - 5, and profile[0, i] = 0 for i <= 5; profile[1, i] is the last j with profile[0, j] <= i. `kernel_tiles`: symmetric; every tile outside the pattern is zero; the matrix restricted to the pattern is positive definite.
All inputs are finite; a program needn't handle non-finite values.
Results may differ from a plain program's by a relative error of at most 0.0001.
Values sent between devices are 32-bit elements; how exact they have to be, the bound alone decides.
No kernel may reach another device: no remote copies, remote signals or barrier semaphores. Data moves between devices by JAX's collectives and lax.ppermute only.
A program may use at most 256 MiB of HBM per device.

v0:
```python
import jax
import jax.numpy as jnp
from jax import lax
from jax.sharding import PartitionSpec as P

STEPS = 2


def from_root(value, axis, root):
    mine = lax.axis_index(axis) == root
    return lax.psum(jnp.where(mine, value, jnp.zeros_like(value)), axis)


def solve_right(block_tile, lower_factor):
    return lax.linalg.triangular_solve(
        lower_factor, block_tile, left_side=False, lower=True, transpose_a=True
    )


def zero_like(block_tile, lower_factor):
    return jnp.zeros_like(block_tile)


def zero_factor(block_tile):
    return jnp.zeros_like(block_tile)


def subtract_outer(target, left_tile, right_tile):
    product = lax.dot_general(
        left_tile,
        right_tile,
        (((1,), (1,)), ((), ())),
        precision=lax.Precision.HIGHEST,
        preferred_element_type=jnp.float32,
    )
    return target - product


def keep_target(target, left_tile, right_tile):
    return target


def on_device(kernel_tiles, profile):
    rows_here = kernel_tiles.shape[0]
    cols_here = kernel_tiles.shape[2]
    order = kernel_tiles.shape[-1]
    blocks = kernel_tiles.reshape(rows_here, cols_here, order, order)
    row_count = lax.axis_size("row")
    col_count = lax.axis_size("col")
    row_index = lax.axis_index("row")
    col_index = lax.axis_index("col")
    global_row = jnp.arange(rows_here, dtype=jnp.int32) * row_count + row_index
    global_col = jnp.arange(cols_here, dtype=jnp.int32) * col_count + col_index
    first_col = profile[0]
    last_col = profile[1]
    row_first = first_col[global_row]
    row_last = last_col[global_row]
    col_first = first_col[global_col]
    in_pattern = jnp.where(
        global_row[:, None] >= global_col[None, :],
        row_first[:, None] <= global_col[None, :],
        global_col[None, :] <= row_last[:, None],
    )
    blocks = jnp.where(in_pattern[:, :, None, None], blocks, jnp.float32(0.0))
    for step in range(STEPS):
        owner_row = step % row_count
        owner_col = step % col_count
        local_row = step // row_count
        local_col = step // col_count
        live_row = (global_row > step) & (row_first <= step)
        live_col = (global_col > step) & (col_first <= step)
        diag_tile = from_root(blocks[local_row, local_col], "row", owner_row)
        diag_factor = lax.cond(col_index == owner_col, jnp.linalg.cholesky, zero_factor, diag_tile)
        solved = jnp.stack(
            [
                lax.cond(
                    live_row[0] & (col_index == owner_col),
                    solve_right,
                    zero_like,
                    blocks[0, local_col],
                    diag_factor,
                )
            ]
        )
        panel_here = from_root(solved, "col", owner_col)
        copies = []
        for slot in range(cols_here):
            wanted = global_col[slot]
            source = lax.dynamic_index_in_dim(panel_here, wanted // row_count, 0, keepdims=False)
            copies.append(from_root(source, "row", wanted % row_count))
        across = jnp.stack(copies)
        updated = []
        for col_slot in range(cols_here):
            active = live_row[0] & live_col[col_slot]
            target = lax.cond(
                active,
                subtract_outer,
                keep_target,
                blocks[0, col_slot],
                panel_here[0],
                across[col_slot],
            )
            is_col = global_col[col_slot] == step
            target = jnp.where(is_col & (global_row[0] > step), panel_here[0], target)
            target = jnp.where(is_col & (global_row[0] == step), diag_factor, target)
            target = jnp.where(
                (global_row[0] == step) & (global_col[col_slot] > step), jnp.float32(0.0), target
            )
            updated.append(target)
        updated_rows = [jnp.stack(updated)]
        blocks = jnp.stack(updated_rows)
    return blocks.reshape(kernel_tiles.shape)


def solution(mesh):
    placed = (P(None, "row", None, "col", None, None), P())
    return jax.shard_map(
        on_device,
        mesh=mesh,
        in_specs=placed,
        out_specs=P(None, "row", None, "col", None, None),
        check_vma=False,
    )
```

profile of v0, /device:TPU:12, one launch (start us, length us, event | category | flops | bytes accessed | tf_op | source)
XLA Modules:
  0.0 1919.4 jit_solution(4113088891274238499)
XLA Ops:
  9.9 4.4 bitcast_select_fusion
  14.4 3.4 copy-done.3
  20.9 8.8 slice_bitcast_fusion.34
  29.7 146.3 %all-reduce.10.cloned.1.call-done = f32[1024,1024]{1,0:T(8,128)} async-done(((f32[1024,1024]{1,0:T(8,128)}), f32[1024,1024]{1,0:T(8,128)}) %all-reduce.10.cloned.1.call-update) | async-done | bytes 4194320 | tf_op jit(solution)/shard_map/psum | solution.py:11
  176.0 5.4 conditional.8
  181.4 14.9 conditional.9
  203.8 440.1 %all-reduce.12.cloned.1.call-done = f32[1024,1024]{1,0:T(8,128)} async-done(((f32[1024,1024]{1,0:T(8,128)}), f32[1024,1024]{1,0:T(8,128)}) %all-reduce.12.cloned.1.call-update) | async-done | bytes 4194320 | tf_op jit(solution)/shard_map/psum | solution.py:11
  643.9 7.0 broadcast_select_fusion.5
  656.0 265.3 %all-reduce.20.cloned.1.call-done = (f32[1024,1024]{1,0:T(8,128)}, f32[1024,1024]{1,0:T(8,128)}) async-done(((f32[1024,1024]{1,0:T(8,128)}, f32[1024,1024]{1,0:T(8,128)}), (f32[1024,1024]{1,0:T(8,128)}, f32[1024,1024]{1,0:T(8,128)})) %all-reduce.20.cloned.1.call-update) | async-done | bytes 8388624 | tf_op jit(solution)/shard_map/psum | solution.py:11
  921.3 18.5 conditional.10
  921.5 18.3 convolution_subtract_fusion.7
  939.8 10.4 select_bitcast_fusion.17
  953.3 3.4 copy-done.2
  959.7 8.3 slice_bitcast_fusion.32
  968.0 163.2 %all-reduce.14.cloned.1.call-done = f32[1024,1024]{1,0:T(8,128)} async-done(((f32[1024,1024]{1,0:T(8,128)}), f32[1024,1024]{1,0:T(8,128)}) %all-reduce.14.cloned.1.call-update) | async-done | bytes 4194320 | tf_op jit(solution)/shard_map/psum | solution.py:11
  1131.3 5.6 conditional.12
  1136.9 14.6 conditional.13
  1154.4 444.5 %all-reduce.16.cloned.1.call-done = f32[1024,1024]{1,0:T(8,128)} async-done(((f32[1024,1024]{1,0:T(8,128)}), f32[1024,1024]{1,0:T(8,128)}) %all-reduce.16.cloned.1.call-update) | async-done | bytes 4194320 | tf_op jit(solution)/shard_map/psum | solution.py:11
  1598.9 7.0 broadcast_select_fusion.1
  1609.8 266.5 %all-reduce.18.cloned.1.call-done = (f32[1024,1024]{1,0:T(8,128)}, f32[1024,1024]{1,0:T(8,128)}) async-done(((f32[1024,1024]{1,0:T(8,128)}, f32[1024,1024]{1,0:T(8,128)}), (f32[1024,1024]{1,0:T(8,128)}, f32[1024,1024]{1,0:T(8,128)})) %all-reduce.18.cloned.1.call-update) | async-done | bytes 8388624 | tf_op jit(solution)/shard_map/psum | solution.py:11
  1876.3 18.5 conditional.14
  1876.6 18.3 convolution_subtract_fusion.9
  1894.9 10.4 select_bitcast_fusion.15
  1905.2 6.8 maximum_bitcast_fusion.1
  (36 shorter events, 29.1 us)
Async XLA Ops:
  6.5 169.5 %all-reduce.10.cloned.1.call-start = ((), (), s32[]{:S(2)}) async-start(), calls=%async_computation | async-start | bytes 8388608 | tf_op jit(solution)/shard_map/psum | solution.py:11
  14.4 3.4 copy-start.3
  20.2 623.7 %all-reduce.12.cloned.1.call-start = ((), (), s32[]{:S(2)}) async-start(), calls=%async_computation.1 | async-start | bytes 8388608 | tf_op jit(solution)/shard_map/psum | solution.py:11
  199.2 722.2 %all-reduce.20.cloned.1.call-start = ((), (), s32[]{:S(2)}) async-start(), calls=%async_computation.5 | async-start | bytes 16777216 | tf_op jit(solution)/shard_map/psum | solution.py:11
  650.9 480.4 %all-reduce.14.cloned.1.call-start = ((), (), s32[]{:S(2)}) async-start(), calls=%async_computation.2 | async-start | bytes 8388608 | tf_op jit(solution)/shard_map/psum | solution.py:11
  953.2 3.4 copy-start.2
  959.1 639.8 %all-reduce.16.cloned.1.call-start = ((), (), s32[]{:S(2)}) async-start(), calls=%async_computation.3 | async-start | bytes 8388608 | tf_op jit(solution)/shard_map/psum | solution.py:11
  1154.3 722.0 %all-reduce.18.cloned.1.call-start = ((), (), s32[]{:S(2)}) async-start(), calls=%async_computation.4 | async-start | bytes 16777216 | tf_op jit(solution)/shard_map/psum | solution.py:11
Sparse Core Ops, SparseCore 0:
  20.3 155.6 all-reduce.9
  199.3 444.5 all-reduce.11
  651.0 270.2 all-reduce.19
  959.2 172.0 all-reduce.13
  1154.4 444.4 all-reduce.15
  1606.0 270.2 all-reduce.17
where the time goes:
time: 1920 us
  waiting for transfers between devices  1730 us (90%)
  other arithmetic  61.4 us (3%)
  local copies, waits for them, and re-layouts  37.3 us (2%)
  matrix products  36.5 us (2%)
  loops' own time  30.9 us (2%)
  between operations  27 us (1%)
    psum x6, waiting for transfers between devices, from_root(): return lax.psum(jnp.where(mine, value, jnp.zeros_like(value)), axis)  1730 us
  transfers between devices with their start and end apart: 6, of which 6 were waited for; matrix products, arithmetic and copies ran while one was open for 1% of the time, Pallas kernels for 0%

commit v1 on v0

v1 whole, which is shorter than its diff:
```python
import jax
import jax.numpy as jnp
from jax import lax
from jax.experimental import pallas as pl
from jax.experimental.pallas import tpu as pltpu
from jax.sharding import PartitionSpec as P

SUB = 8
BASE = 128
BLOCK = 256
FIRST = (2, 4)
SECOND = (5, 7)
THIRD = (8,)
NN = ((1,), (0,))
NT = ((1,), (1,))
TN = ((0,), (0,))
ANY = pl.BlockSpec(memory_space=pl.ANY)
SMEM = pl.BlockSpec(memory_space=pltpu.SMEM)
DMA = pltpu.SemaphoreType.DMA
F32 = jnp.float32


def dot(a, b, dims, precision=lax.Precision.HIGHEST):
    return lax.dot_general(
        a, b, (dims, ((), ())), precision=precision, preferred_element_type=jnp.float32
    )


def down(x, j):
    return jnp.broadcast_to(x[j : j + 1, :], x.shape)


def along(x, j):
    return jnp.broadcast_to(x[:, j : j + 1], x.shape)


def factor_base(diag):
    sub = lax.broadcasted_iota(jnp.int32, (SUB, BASE), 0)
    lane = lax.broadcasted_iota(jnp.int32, (SUB, BASE), 1)
    count = BASE // SUB
    left = [diag[SUB * t : SUB * t + SUB, :] for t in range(count)]
    right = [(lane == sub + SUB * t).astype(jnp.float32) for t in range(count)]
    upper, inverse = [], []
    for t in range(count):
        a, b = left[t], right[t]
        cols = [along(a, SUB * t + j) for j in range(SUB)]
        ua, ub, pivots = a, b, None
        for j in range(SUB):
            mine = sub == j
            pivot = down(cols[j], j)
            recip = 1.0 / pivot
            if j:
                ua = jnp.where(sub >= j, a, ua)
                ub = jnp.where(sub >= j, b, ub)
                pivots = jnp.where(sub >= j, pivot, pivots)
            else:
                pivots = pivot
            mult = cols[j]
            row = down(a, j) * recip
            a = jnp.where(mine, row, a - mult * row)
            row = down(b, j) * recip
            b = jnp.where(mine, row, b - mult * row)
            for k in range(j + 1, SUB):
                row = down(cols[k], j) * recip
                cols[k] = jnp.where(mine, row, cols[k] - mult * row)
        scale = lax.rsqrt(pivots)
        upper.append(jnp.where(lane >= sub + SUB * t, ua * scale, 0.0))
        inverse.append(ub * scale)
        if t + 1 < count:
            va = [down(a, j) for j in range(SUB)]
            vb = [down(b, j) for j in range(SUB)]
            for i in range(t + 1, count):
                mult = [along(left[i], SUB * t + j) for j in range(SUB)]
                for j in range(SUB):
                    left[i] = left[i] - mult[j] * va[j]
                    right[i] = right[i] - mult[j] * vb[j]
    return jnp.concatenate(upper, 0), jnp.concatenate(inverse, 0)


def params(limit_mib=48):
    return pltpu.CompilerParams(vmem_limit_bytes=limit_mib << 20)


def shape(*dims):
    return jax.ShapeDtypeStruct(dims, F32)


def factor_kernel(kind, flag_ref, *refs):
    refs = list(refs)
    sources = [refs.pop(0) for _ in range({"first": 3, "next": 1, "schur": 6}[kind])]
    a_ref, f_ref, sems = refs[-3:]
    f_out = refs[0]
    rest_out = refs[1] if len(refs) > 4 else None
    n, m = a_ref.shape
    top, below = pl.ds(0, BLOCK), pl.ds(BLOCK, n - BLOCK)

    @pl.when(flag_ref[0] == 1)
    def _():
        copies = []

        def load(source, target):
            copies.append(pltpu.make_async_copy(source, target, sems.at[len(copies)]))
            copies[-1].start()

        if kind == "first":
            left, right, cut = pl.ds(0, n), pl.ds(n, n), n // 2 - BLOCK
            load(sources[0].at[0, top], a_ref.at[top, left])
            load(sources[1].at[top], a_ref.at[top, right])
            load(sources[0].at[0, below], a_ref.at[below, left])
            load(sources[1].at[pl.ds(BLOCK, cut)], a_ref.at[pl.ds(BLOCK, cut), right])
            load(sources[2], a_ref.at[pl.ds(n // 2, n // 2), right])
            needed = 2
        elif kind == "next":
            load(sources[0].at[top], a_ref.at[top])
            if n > BLOCK:
                load(sources[0].at[below], a_ref.at[below])
            needed = 1
        else:
            parts = refs[-4]
            for h in range(2):
                load(sources[h], a_ref.at[pl.ds(h * n // 2, n // 2)])
            for p, part in enumerate(sources[2:]):
                load(
                    part.at[:, pl.ds(part.shape[1] - n, n)],
                    parts.at[pl.ds(p * BLOCK, BLOCK)],
                )
            needed = len(copies)
        for copy in copies[:needed]:
            copy.wait()
        if kind == "schur":
            for r in range(0, n, BLOCK):
                lhs = parts[:, r : r + BLOCK].T
                for c in range(r, n, BLOCK):
                    a_ref[r : r + BLOCK, c : c + BLOCK] -= dot(lhs, parts[:, c : c + BLOCK], NN)

        first, second = pl.ds(0, BASE), pl.ds(BASE, BASE)
        sub = lax.broadcasted_iota(jnp.int32, (BASE, BASE), 0)
        lane = lax.broadcasted_iota(jnp.int32, (BASE, BASE), 1)
        x_ref = refs[-4] if kind != "schur" else refs[-5]

        def base(b, carry):
            rows = pl.ds(pl.multiple_of(b * BASE, BASE), BASE)
            u, x = factor_base(a_ref[rows, rows])
            f_ref[rows, rows] = jnp.where(sub <= lane, u, x)
            x_ref[rows, rows] = x

            @pl.when(b == 0)
            def _():
                u12 = dot(x, a_ref[first, second], NN)
                f_ref[first, second] = u12
                a_ref[second, second] -= dot(u12, u12, TN)

            return carry

        lax.fori_loop(0, BLOCK // BASE, base, 0)
        x21 = -dot(x_ref[second, second], dot(f_ref[first, second], x_ref[first, first], TN), NN)
        f_ref[second, first] = x21
        x_ref[second, first] = x21
        x_ref[first, second] = jnp.zeros((BASE, BASE), F32)
        x = x_ref[...]
        for c in range(BLOCK, m, BLOCK):
            f_ref[:, c : c + BLOCK] = dot(x, a_ref[top, c : c + BLOCK], NN)
        leaving = [pltpu.make_async_copy(f_ref, f_out, sems.at[len(copies)])]
        leaving[0].start()
        for copy in copies[needed:]:
            copy.wait()
        for r in range(BLOCK, n, BLOCK):
            lhs = f_ref[:, r : r + BLOCK].T
            for c in range(r, m, BLOCK):
                a_ref[r : r + BLOCK, c : c + BLOCK] -= dot(lhs, f_ref[:, c : c + BLOCK], NN)
            rows = pl.ds(r, BLOCK)
            leaving.append(
                pltpu.make_async_copy(
                    a_ref.at[rows, pl.ds(BLOCK, m - BLOCK)],
                    rest_out.at[pl.ds(r - BLOCK, BLOCK)],
                    sems.at[len(copies) + len(leaving)],
                )
            )
            leaving[-1].start()
        for copy in leaving:
            copy.wait()


def factor_block(kind, flag, n, m, *sources):
    shapes = [shape(BLOCK, m)]
    if n > BLOCK:
        shapes.append(shape(n - BLOCK, m - BLOCK))
    scratch = [pltpu.VMEM((BLOCK, BLOCK), F32)]
    if kind == "schur":
        scratch.append(pltpu.VMEM((n, n), F32))
    scratch += [pltpu.VMEM((n, m), F32), pltpu.VMEM((BLOCK, m), F32), DMA((12,))]
    out = pl.pallas_call(
        lambda *refs: factor_kernel(kind, *refs),
        out_shape=shapes,
        in_specs=[SMEM] + [ANY] * len(sources),
        out_specs=[ANY] * len(shapes),
        scratch_shapes=scratch,
        cost_estimate=pl.CostEstimate(
            flops=2_000_000_000, bytes_accessed=8 * n * m, transcendentals=0
        ),
        compiler_params=params(),
    )(flag, *sources)
    return out if n > BLOCK else (out[0], None)


def choose(index, options):
    def kernel(index_ref, *refs):
        *bufs, out_ref, sem = refs
        for k, buf in enumerate(bufs):

            @pl.when(index_ref[0] == k)
            def _():
                copy = pltpu.make_async_copy(buf, out_ref, sem)
                copy.start()
                copy.wait()

    return pl.pallas_call(
        kernel,
        out_shape=shape(*options[0].shape),
        in_specs=[SMEM] + [ANY] * len(options),
        out_specs=ANY,
        scratch_shapes=[DMA(())],
    )(index, *options)


def unset(like):
    return pl.pallas_call(
        lambda out_ref: None, out_shape=shape(*like.shape), in_specs=[], out_specs=ANY
    )()


def patch(flags, result, parts):
    def kernel(flags_ref, result_ref, *refs):
        *bufs, out_ref, sems = refs
        for k, buf in enumerate(bufs):

            @pl.when(flags_ref[k] == 1)
            def _():
                copy = pltpu.make_async_copy(buf, out_ref.at[k], sems.at[k])
                copy.start()
                copy.wait()

    return pl.pallas_call(
        kernel,
        out_shape=shape(*result.shape),
        in_specs=[SMEM] + [ANY] * (1 + len(parts)),
        out_specs=ANY,
        scratch_shapes=[DMA((len(parts),))],
        input_output_aliases={1: 0},
    )(flags, result, *parts)


def split(x):
    high = x.astype(jnp.bfloat16)
    return high, (x - high.astype(F32)).astype(jnp.bfloat16)


def dot3(a, b, dims):
    total = None
    for x, y in ((a[1], b[0]), (a[0], b[1]), (a[0], b[0])):
        part = lax.dot_general(x, y, (dims, ((), ())), preferred_element_type=F32)
        total = part if total is None else total + part
    return total


PASS, WORK, ZERO, LOWER0, PANEL0, LOWER1 = range(6)


def finish_kernel(n_raw, n_sets, meta_ref, *refs):
    tiles_ref, raws, refs = refs[0], refs[1 : 1 + n_raw], refs[1 + n_raw :]
    order = tiles_ref.shape[-1]
    steps = order // BLOCK
    count = 2 * steps
    sets = [refs[k * count : (k + 1) * count] for k in range(n_sets)]
    out_ref, p1_ref, z, t, high, low, *fs, sems = refs[n_sets * count :]
    role, transposed, which, col, edge = (meta_ref[k] for k in (0, 5, 6, 7, 8))
    half = pl.ds(0, order), pl.ds(order, order)
    mid = order // 2
    sources = [
        [tiles_ref.at[0, pl.ds(h * mid, mid)]] + [raws[2 * k + h] for k in range(n_raw // 2)]
        for h in range(2)
    ]

    def load_pieces(pieces):
        for k in range(n_sets):

            @pl.when(which == k)
            def _():
                for p in pieces:
                    pltpu.make_async_copy(sets[k][p], fs[p], sems.at[8 + p]).start()

    def await_piece(p):
        pltpu.make_async_copy(sets[0][p], fs[p], sems.at[8 + p]).wait()

    def move_out(source, target, sem):
        copy = pltpu.make_async_copy(source, target, sems.at[sem])
        copy.start()
        return copy

    @pl.when(role == PASS)
    def _():
        copies = [move_out(tiles_ref.at[k], out_ref.at[k], k) for k in range(2)]
        for copy in copies:
            copy.wait()

    @pl.when(role >= ZERO)
    def _():
        t[...] = jnp.zeros((order, order), F32)
        move_out(t, out_ref.at[1], 1).wait()

        def upper_block(p, q, lead):
            base = lead + (q - p) * BLOCK
            return fs[p][:, base : base + BLOCK].T

        def triangle(offset):
            sub = lax.broadcasted_iota(jnp.int32, (BLOCK, BLOCK), 0)
            lane = lax.broadcasted_iota(jnp.int32, (BLOCK, BLOCK), 1)
            for p in range(steps):
                for q in range(p, steps):
                    block = fs[offset + p][:, (q - p) * BLOCK : (q - p + 1) * BLOCK]
                    if p == q:
                        block = jnp.where(sub <= lane, block, 0.0)
                    t[q * BLOCK : (q + 1) * BLOCK, p * BLOCK : (p + 1) * BLOCK] = block.T

        for kind, pieces in (
            (LOWER0, range(steps)),
            (PANEL0, range(steps)),
            (LOWER1, range(steps, count)),
        ):

            @pl.when(role == kind)
            def _():
                load_pieces(pieces)
                for p in pieces:
                    await_piece(p)
                if kind == PANEL0:
                    for p in range(steps):
                        for q in range(steps):
                            t[q * BLOCK : (q + 1) * BLOCK, p * BLOCK : (p + 1) * BLOCK] = (
                                upper_block(p, q, order - p * BLOCK + p * BLOCK)
                            )
                else:
                    triangle(pieces[0])

        move_out(t, out_ref.at[0], 0).wait()

    @pl.when(role == WORK)
    def _():
        places = [
            [z.at[pl.ds(a * order + h * mid, mid), pl.ds(b * order, order)] for h in range(2)]
            for a in range(2)
            for b in range(2)
        ]
        for s, place in enumerate(places):
            for k in range(len(sources[0])):

                @pl.when(meta_ref[1 + s] == k)
                def _():
                    for h in range(2):
                        sem = sems.at[8 + count + 2 * s + h]
                        pltpu.make_async_copy(sources[h][k], place[h], sem).start()

        load_pieces(range(count))
        for slot, taken in ((1, col < 2), (0, col >= 2)):

            @pl.when(taken)
            def _():
                pltpu.make_async_copy(tiles_ref.at[slot], t, sems.at[4]).start()

        @pl.when(col >= 2)
        def _():
            move_out(tiles_ref.at[1], out_ref.at[1], 5)

        for s, place in enumerate(places):
            for h in range(2):
                sem = sems.at[8 + count + 2 * s + h]
                pltpu.make_async_copy(sources[h][1], place[h], sem).wait()

        @pl.when(transposed == 1)
        def _():
            for left in (0, order):
                for a in range(steps):
                    for b in range(a, steps):
                        ra = order + a * BLOCK, left + a * BLOCK
                        rb = order + b * BLOCK, left + b * BLOCK
                        upper = z[ra[0] : ra[0] + BLOCK, rb[1] : rb[1] + BLOCK].T
                        if a != b:
                            z[ra[0] : ra[0] + BLOCK, rb[1] : rb[1] + BLOCK] = z[
                                rb[0] : rb[0] + BLOCK, ra[1] : ra[1] + BLOCK
                            ].T
                        z[rb[0] : rb[0] + BLOCK, ra[1] : ra[1] + BLOCK] = upper

        sub = lax.broadcasted_iota(jnp.int32, (BLOCK, BLOCK), 0)
        lane = lax.broadcasted_iota(jnp.int32, (BLOCK, BLOCK), 1)
        for p in range(count):
            await_piece(p)
            packed = fs[p][:, :BLOCK]
            inverse = jnp.where(
                sub > lane, packed, jnp.where(sub == lane, 1.0 / packed, 0.0)
            )
            inverse = split(inverse)
            for rows in half:
                solved = dot3(
                    split(z[rows, p * BLOCK : (p + 1) * BLOCK]), inverse, NT
                )
                z[rows, p * BLOCK : (p + 1) * BLOCK] = solved
                solved = split(solved)
                high[rows, :] = solved[0]
                low[rows, :] = solved[1]

            def eliminate(q, carry):
                to = pl.ds(pl.multiple_of(q * BLOCK, BLOCK), BLOCK)
                u = split(fs[p][:, pl.ds(pl.multiple_of((q - p) * BLOCK, BLOCK), BLOCK)])
                for rows in half:
                    z[rows, to] -= dot3((high[rows, :], low[rows, :]), u, NN)
                return carry

            lax.fori_loop(p + 1, count, eliminate, 0)
            if p == 0:
                pltpu.make_async_copy(tiles_ref.at[0], t, sems.at[4]).wait()

            def update(r, carry):
                rows = pl.ds(pl.multiple_of(r * BLOCK, BLOCK), BLOCK)
                others = high[half[1], :], low[half[1], :]
                t[rows, :] -= dot3((high[rows, :], low[rows, :]), others, NT)
                return carry

            lax.fori_loop(0, steps, update, 0)

        @pl.when(col == 0)
        def _():
            move_out(z.at[half[0], half[0]], out_ref.at[0], 5)

        @pl.when(col == 1)
        def _():
            move_out(z.at[half[0], half[1]], out_ref.at[0], 5)

        for slot, taken in ((1, col < 2), (0, col >= 2)):

            @pl.when(taken)
            def _():
                move_out(t, out_ref.at[slot], 6)

        @pl.when((col == 2) & (edge == 1))
        def _():
            move_out(z.at[half[0], half[1]], p1_ref, 7).wait()

        pltpu.make_async_copy(t, out_ref.at[0], sems.at[5]).wait()
        pltpu.make_async_copy(t, out_ref.at[0], sems.at[6]).wait()


def finish(meta, tiles, raws, sets):
    order = tiles.shape[-1]
    count = len(sets[0])
    flat = [f for s in sets for f in s]
    scratch = [
        pltpu.VMEM((2 * order, 2 * order), F32),
        pltpu.VMEM((order, order), F32),
        pltpu.VMEM((2 * order, BLOCK), jnp.bfloat16),
        pltpu.VMEM((2 * order, BLOCK), jnp.bfloat16),
    ]
    scratch += [pltpu.VMEM(f.shape, F32) for f in sets[0]] + [DMA((16 + count,))]
    return pl.pallas_call(
        lambda *refs: finish_kernel(len(raws), len(sets), *refs),
        out_shape=[shape(*tiles.shape), shape(order, order)],
        in_specs=[SMEM] + [ANY] * (1 + len(raws) + len(flat)),
        out_specs=[ANY, ANY],
        scratch_shapes=scratch,
        cost_estimate=pl.CostEstimate(
            flops=60_000_000_000, bytes_accessed=64 << 20, transcendentals=0
        ),
        compiler_params=params(56),
    )(meta, tiles, *raws, *flat)


def move(value, pairs, cols):
    if isinstance(value, list):
        return [move(v, pairs, cols) for v in value]
    flat = [(a * cols + b, c * cols + d) for (a, b), (c, d) in pairs]
    return lax.ppermute(value, ("row", "col"), flat)


def doubling(value, axis, root, size):
    place = lax.rem(lax.axis_index(axis) - root + size, size)
    reach = 1
    while reach < size:
        pairs = [
            ((root + i) % size, (root + i + reach) % size) for i in range(min(reach, size - reach))
        ]
        value = jnp.where(place >= reach, lax.ppermute(value, axis, pairs), value)
        reach *= 2
    return value


def both_ways(pairs):
    return pairs + [(b, a) for a, b in pairs]


def eliminate_last(panel, pieces):
    done = []
    for f in pieces:
        packed = f[:, :BLOCK]
        inverse = jnp.tril(packed, -1) + jnp.diag(1.0 / jnp.diagonal(packed))
        part = dot(panel[:, :BLOCK], inverse, NT, lax.Precision.HIGH)
        done.append(part)
        if f.shape[1] > BLOCK:
            panel = panel[:, BLOCK:] - dot(part, f[:, BLOCK:], NN, lax.Precision.HIGH)
    return jnp.concatenate(done, 1)


def on_device(kernel_tiles, profile):
    order = kernel_tiles.shape[-1]
    rows, cols = lax.axis_size("row"), lax.axis_size("col")
    row, col = lax.axis_index("row"), lax.axis_index("col")
    tiles = kernel_tiles.reshape(2, order, order)
    near = [tiles[0, h * order // 2 : (h + 1) * order // 2] for h in range(2)]
    steps = order // BLOCK
    count = 2 * steps
    edge = cols + 2
    edge_live = profile[0, edge] <= 1
    owner = jnp.reshape(((row == 0) & (col == 0)).astype(jnp.int32), (1,))
    workers = range(2, edge)
    routed = cols == 4

    plan = [[[PASS, 0, 0, 0, 0, 0, 0, 0, 0, -1, -1, -1] for _ in range(cols)] for _ in range(rows)]
    for r in range(rows):
        for c in range(cols):
            plan[r][c][7] = c
            if r < 2:
                plan[r][c][0] = ZERO
            elif r < edge:
                plan[r][c][0] = WORK
    plan[0][0][0], plan[1][0][0], plan[1][1][0] = LOWER0, PANEL0, LOWER1

    if routed:
        r1 = move(near, both_ways([((r, 0), (r, 1)) for r in (0,) + tuple(workers)]), cols)
        r2 = move(
            near,
            [((r, c), (r, c + 2)) for r in workers for c in (0, 1)]
            + [((1, 1), (0, 0)), ((edge, 1), (edge, 3))],
            cols,
        )
        r3 = move(
            near,
            both_ways([((4, c), (5, c)) for c in (0, 1)])
            + [((r, c), (r + 4, c)) for r in (0, 1) for c in (2, 3)],
            cols,
        )
        r4 = move(near, [((r, c), (r - 2, c)) for r in (4, 5) for c in (0, 1)], cols)
        tile01 = r1
        for r in workers:
            plan[r][0][1:3] = [0, 1]
            plan[r][1][1:3] = [1, 0]
            plan[r][2][1:3] = [2, 5]
            plan[r][3][1:3] = [5, 2]
            for c in range(4):
                plan[r][c][3:5] = plan[r][c][1:3]
        for place, pair in {
            (2, 0): (4, 10), (2, 1): (11, 6), (3, 0): (6, 11), (3, 1): (10, 4),
            (4, 1): (9, 3), (5, 0): (3, 9), (2, 3): (12, 7), (3, 2): (7, 12),
            (4, 2): (3, 8), (4, 3): (3, 8), (5, 2): (8, 3), (5, 3): (8, 3),
        }.items():
            plan[place[0]][place[1]][3:5] = pair
        for r in (4, 5):
            for c in (2, 3):
                plan[r][c][5] = 1
        plan[1][1][6] = 1
        for r in workers:
            plan[r][1][6] = plan[r][3][6] = 2 if r < 4 else 3
            plan[r][3][6] = 4
        for r in (1,) + tuple(workers):
            plan[r][0][6] = plan[r][2][6] = 5
        plan[0][1][9], plan[1][1][9] = 0, 1
        for r in workers:
            plan[r][1][10] = 0 if r < 4 else 1
            plan[r][1][11] = 1 if r < 4 else 2
            plan[r][3][11] = 3
        plan[1][1][11] = 0
    else:
        mine = jnp.where(col < 2, tiles[1], tiles[0])
        mine = [mine[: order // 2], mine[order // 2 :]]
        left0 = [doubling(v, "col", 0, cols) for v in near]
        left1 = [doubling(v, "col", 1, cols) for v in near]
        top0 = [doubling(v, "row", 0, rows) for v in mine]
        top1 = [doubling(v, "row", 1, rows) for v in mine]
        tile01 = move(near, [((0, 1), (0, 0))], cols)
        tile11 = move(near, [((1, 1), (0, 0))], cols)
        raws = left0 + left1 + top0 + top1
        for r in range(rows):
            for c in range(cols):
                plan[r][c][1:6] = [1, 2, 3, 4, 1]
    meta = jnp.array(plan, jnp.int32)[row, col]
    meta = meta.at[8].set(edge_live.astype(jnp.int32))

    pieces, copies, state = [], [], None
    r5, r6a, r6b, r6c, e1, r7a, r7b, r7c, r7d = ([] for _ in range(9))
    stages = 6 if routed else 0
    late = []
    for slot in range(count + stages):
        arrived = []
        if slot < count:
            step, local = divmod(slot, steps)
            n = order - local * BLOCK
            if slot == 0:
                args = ("first", owner, n, 2 * n, tiles, *tile01)
            elif local == 0:
                args = ("schur", owner, n, n, *(r2 if routed else tile11), *pieces)
            else:
                args = ("next", owner, n, n + (1 - step) * order, state)
            piece, state = factor_block(*args)
            pieces.append(piece)
            copies.append([])
            if not routed:
                copies[-1].append(doubling(doubling(piece, "row", 0, rows), "col", 0, cols))
        if not routed:
            continue
        for k in range(1, stages + 1):
            p = slot - k
            if not 0 <= p < count:
                continue
            got = copies[p]
            if k == 1:
                got.append(move(pieces[p], [((0, 0), (0, 1))], cols))
            elif k == 2:
                got.append(move(got[0], [((0, 1), (1, 1))], cols))
            elif k == 3:
                via = choose(meta[9:10], [got[0], got[1]])
                got.append(move(via, [((r, 1), (r + 2, 1)) for r in (0, 1)], cols))
            elif k == 4:
                got.append(move(got[2], [((r, 1), (r + 2, 1)) for r in (2, 3)], cols))
            elif k == 5:
                via = choose(meta[10:11], [got[2], got[3]])
                got.append(move(via, [((r, 1), (r, 3)) for r in workers], cols))
            else:
                via = choose(meta[11:12], [got[1], got[2], got[3], got[4]])
                got.append(
                    move(
                        via,
                        [((r, c), (r, c - 1)) for r in workers for c in (1, 3)]
                        + [((1, 1), (1, 0))],
                        cols,
                    )
                )
            arrived.append(p)
        late = {
            FIRST[0]: lambda: [r2[0], r3[0], r4[0]],
            FIRST[1]: lambda: [r2[1], r3[1], r4[1]],
            SECOND[0]: lambda: [r5[0], r6a[0], r6b[0], r6c[0], e1[0]],
            SECOND[1]: lambda: [r5[1], r6a[1], r6b[1], r6c[1], e1[1]],
            THIRD[0]: lambda: [r7a[0], r7b[0], r7c[0], r7d[0]],
        }.get(slot, list)()
        last = [copies[p][-1] for p in arrived]
        flowing = ([pieces[slot]] if slot < count else []) + ([] if state is None else [state])
        flowing, last, late = lax.optimization_barrier((flowing, last, late))
        if slot < count:
            pieces[slot] = flowing[0]
        if state is not None:
            state = flowing[-1]
        for p, value in zip(arrived, last):
            copies[p][-1] = value
        for h in range(2):
            if slot == FIRST[h]:
                r2[h], r3[h], r4[h] = late
                r5.append(move(r2[h], both_ways([((r, 2), (r, 3)) for r in workers]), cols))
                r6a.append(move(r4[h], both_ways([((2, c), (3, c)) for c in (0, 1)]), cols))
                r6b.append(move(r2[h], both_ways([((2, c), (3, c)) for c in (2, 3)]), cols))
                r6c.append(move(r3[h], both_ways([((4, c), (5, c)) for c in (2, 3)]), cols))
                e1.append(move(r2[h], [((edge, 3), (edge - 2, 2))], cols))
            elif slot == SECOND[h]:
                r5[h], r6a[h], r6b[h], r6c[h], e1[h] = late
                r7a.append(move(r3[h], [((4, 0), (4, 1)), ((5, 1), (5, 0))], cols))
                r7b.append(move(r4[h], [((2, 1), (2, 0)), ((3, 0), (3, 1))], cols))
                r7c.append(move(r6a[h], [((2, 0), (2, 1)), ((3, 1), (3, 0))], cols))
                r7d.append(move(r6b[h], [((2, 2), (2, 3)), ((3, 3), (3, 2))], cols))
        if slot == THIRD[0]:
            r7a[0], r7b[0], r7c[0], r7d[0] = late

    if routed:
        sets = [pieces] + [[got[k] for got in copies] for k in (1, 2, 3, 4, 5)]
        raws = r1 + r2 + r3 + r4 + r5 + r6a + r6b + r6c + r7a + r7b + r7c + r7d
    else:
        sets = [[got[0] for got in copies]]

    def fetch(tile):
        if routed:
            e2 = move(tile, [((edge - 2, 2), (edge - 4, 2))], cols)
            e3 = move(tile + e2, [((r, 2), (r + 1, 2)) for r in (2, 4)], cols)
            return tile + e2 + e3
        total = jnp.zeros_like(tile)
        for r in workers:
            total = total + move(tile, [((edge, 1), (r, 2))], cols)
        return total

    result, panel1 = finish(meta, tiles, raws, sets)

    def edge_parts(args):
        panel1, edge_tile, last_pieces = args
        far = tiles[1]
        edge_tile = fetch(jnp.concatenate(edge_tile, 0))
        last = eliminate_last(edge_tile, last_pieces)
        column = far - dot(panel1, last, NT, lax.Precision.HIGH)
        sent = move(column, [((r, 2), (edge, r % cols)) for r in workers], cols).T
        solved = move(last, [((edge - 2, 2), (edge, 1)), ((edge - 1, 2), (edge, 2))], cols)
        corner = far - dot(solved, solved, NT, lax.Precision.HIGH)
        part0 = jnp.where(col == 1, solved, sent)
        part1 = jnp.where(row == edge, jnp.where(col == 2, corner, sent), column)
        return part0, part1

    def no_edge(args):
        return unset(tiles[0]), unset(tiles[0])

    parts = lax.cond(edge_live, edge_parts, no_edge, (panel1, e1 if routed else near, sets[-1][steps:]))
    at_edge = edge_live & (row == edge)
    flags = jnp.stack(
        [
            at_edge & (col >= 1),
            (at_edge & (col <= 2)) | (edge_live & (row >= 2) & (row < edge) & (col == 2)),
        ]
    ).astype(jnp.int32)
    return patch(flags, result, parts).reshape(kernel_tiles.shape)


def solution(mesh):
    placed = (P(None, "row", None, "col", None, None), P())
    return jax.shard_map(
        on_device,
        mesh=mesh,
        in_specs=placed,
        out_specs=P(None, "row", None, "col", None, None),
        check_vma=False,
    )
```

time: 1920 us -> 1160 us (0.60)
  waiting for transfers between devices: 1730 us -> 654 us
  starting transfers between devices: 0.21 us -> 305 us
  Pallas kernels: 0 us -> 153 us
  other arithmetic: 61.4 us -> 0.61 us
  matrix products: 36.5 us -> 0 us
  loops' own time: 30.9 us -> 5.86 us
  between operations: 27 us -> 2.37 us
    psum x6 -> x0, waiting for transfers between devices: 1730 us -> none  [from_root(): return lax.psum(jnp.where(mine, value, jnp.zeros_like(value)), axis)]
    ppermute x0 -> x74, waiting for transfers between devices: none -> 654 us  [move(): return lax.ppermute(value, ('row', 'col'), flat)]
    ppermute x0 -> x74, starting transfers between devices: none -> 305 us  [move(): return lax.ppermute(value, ('row', 'col'), flat)]
    pallas_call x0 -> x36, Pallas kernels: none -> 153 us  [the longest x1 130 us: finish(): pl.pallas_call(lambda *refs: finish_kernel(len(raws), len(sets), *refs),...]
    dot_general x2 -> x0, matrix products: 36.5 us -> none  [subtract_outer(): lax.dot_general(left_tile, right_tile, (((1,), (1,)), ((), ())), precisio...]
    another operation x4 -> x0, other arithmetic: 30.7 us -> none  [the longest x2 20.8 us: on_device(): updated_rows = [jnp.stack(updated)]]
    select_n x9 -> x0, other arithmetic: 30.1 us -> none  [the longest x6 24.3 us: from_root(): return lax.psum(jnp.where(mine, value, jnp.zeros_like(value)), axis)]
    another operation x8 -> x1, loops' own time: 30.9 us -> 5.86 us  [on_device(): lax.cond(edge_live, edge_parts, no_edge, (panel1, e1 if routed else near,...]
  transfers between devices with their start and end apart: 6 -> 74, of which waited for: 6 -> 10; matrix products, arithmetic and copies ran while one was open for 1% -> 0% of each run, Pallas kernels for 0% -> 2%
where the time goes in v1:
time: 1160 us; the launch traced here: 1140 us
  waiting for transfers between devices  654 us (56%)
  starting transfers between devices  305 us (26%)
  Pallas kernels  153 us (13%)
  local copies, waits for them, and re-layouts  19.9 us (2%)
    ppermute x74, waiting for transfers between devices, move(): return lax.ppermute(value, ('row', 'col'), flat)  654 us
    ppermute x74, starting transfers between devices, move(): return lax.ppermute(value, ('row', 'col'), flat)  305 us
    pallas_call x1, Pallas kernels, finish(): pl.pallas_call(lambda *refs: finish_kernel(len(raws), len(sets), *refs),...  130 us
  transfers between devices with their start and end apart: 74, of which 10 were waited for; matrix products, arithmetic and copies ran while one was open for 0% of the time, Pallas kernels for 2%

profile of v1, /device:TPU:12, one launch (start us, length us, event | category | flops | bytes accessed | tf_op | source)
XLA Modules:
  0.0 1140.7 jit_solution(3398537255920364420)
XLA Ops:
  0.0 4.9 slice_bitcast_fusion.1
  9.8 2.0 collective-permute-start.11
  18.4 5.8 shard_map.39
  25.2 42.3 %collective-permute-done.9.refs_1_.refs_4_ = f32[512,1024]{1,0:T(8,128)S(1)} collective-permute-done((f32[512,1024]{1,0:T(8,128)}, f32[512,1024]{1,0:T(8,128)S(1)}, u32[]{:S(2)}, u32[]{:S(2)}) %collective-permute-start.9) | collective-permute-done | bytes 2097184 | tf_op jit(solution)/shard_map/ppermute | solution.py:480
  90.1 41.7 %collective-permute-done.12.refs_2_.refs_5_ = f32[512,1024]{1,0:T(8,128)} collective-permute-done((f32[512,1024]{1,0:T(8,128)}, f32[512,1024]{1,0:T(8,128)}, u32[]{:S(2)}, u32[]{:S(2)}) %collective-permute-start.12) | collective-permute-done | bytes 2097184 | tf_op jit(solution)/shard_map/ppermute | solution.py:480
  135.8 2.1 collective-permute-start.31
  137.8 3.4 collective-permute-start.29
  148.0 2.1 collective-permute-start.26
  150.2 2.1 collective-permute-start.25
  154.6 31.6 %collective-permute-done.29.refs_14_ = f32[512,1024]{1,0:T(8,128)} collective-permute-done((f32[512,1024]{1,0:T(8,128)}, f32[512,1024]{1,0:T(8,128)}, u32[]{:S(2)}, u32[]{:S(2)}) %collective-permute-start.29) | collective-permute-done | bytes 2097184 | tf_op jit(solution)/shard_map/ppermute | solution.py:480
  206.0 3.4 collective-permute-start.46
  209.4 213.8 %collective-permute-done.37.refs_66_ = f32[256,2048]{1,0:T(8,128)} collective-permute-done((f32[256,2048]{1,0:T(8,128)}, f32[256,2048]{1,0:T(8,128)}, u32[]{:S(2)}, u32[]{:S(2)}) %collective-permute-start.37) | collective-permute-done | bytes 2097184 | tf_op jit(solution)/shard_map/ppermute | solution.py:480
  423.2 83.3 %collective-permute-start.44 = (f32[512,1024]{1,0:T(8,128)}, f32[512,1024]{1,0:T(8,128)}, u32[]{:S(2)}, u32[]{:S(2)}) collective-permute-start(f32[512,1024]{1,0:T(8,128)} %collective-permute-done.12.refs_2_.refs_5_), channel_id=1, source_target_pairs={{10,11},{14,15},{18,19},{22,23},{11,10},{15,14},{19,18},{23,22}} | collective-permute-start | bytes 6291464 | tf_op jit(solution)/shard_map/ppermute | solution.py:480
  523.6 78.3 %collective-permute-start.58 = (f32[512,1024]{1,0:T(8,128)}, f32[512,1024]{1,0:T(8,128)}, u32[]{:S(2)}, u32[]{:S(2)}) collective-permute-start(f32[512,1024]{1,0:T(8,128)} %collective-permute-done.29.refs_14_), channel_id=1, source_target_pairs={{10,11},{15,14}} | collective-permute-start | bytes 6291464 | tf_op jit(solution)/shard_map/ppermute | solution.py:480
  610.9 43.3 %collective-permute-done.54.refs_68_ = f32[256,1536]{1,0:T(8,128)} collective-permute-done((f32[256,1536]{1,0:T(8,128)}, f32[256,1536]{1,0:T(8,128)}, u32[]{:S(2)}, u32[]{:S(2)}) %collective-permute-start.54) | collective-permute-done | bytes 1572896 | tf_op jit(solution)/shard_map/ppermute | solution.py:480
  661.3 133.5 %collective-permute-done.67.refs_69_ = f32[256,1280]{1,0:T(8,128)} collective-permute-done((f32[256,1280]{1,0:T(8,128)}, f32[256,1280]{1,0:T(8,128)}, u32[]{:S(2)}, u32[]{:S(2)}) %collective-permute-start.67) | collective-permute-done | bytes 1310752 | tf_op jit(solution)/shard_map/ppermute | solution.py:480
  801.1 77.8 %collective-permute-done.71.refs_70_ = f32[256,1024]{1,0:T(8,128)S(1)} collective-permute-done((f32[256,1024]{1,0:T(8,128)}, f32[256,1024]{1,0:T(8,128)S(1)}, u32[]{:S(2)}, u32[]{:S(2)}) %collective-permute-start.71) | collective-permute-done | bytes 1048608 | tf_op jit(solution)/shard_map/ppermute | solution.py:480
  885.0 2.0 collective-permute-start.61
  887.1 38.8 %collective-permute-start.62 = (f32[512,1024]{1,0:T(8,128)}, f32[512,1024]{1,0:T(8,128)}, u32[]{:S(2)}, u32[]{:S(2)}) collective-permute-start(f32[512,1024]{1,0:T(8,128)} %collective-permute-done.46.refs_15_), channel_id=1, source_target_pairs={{10,11},{15,14}} | collective-permute-start | bytes 6291464 | tf_op jit(solution)/shard_map/ppermute | solution.py:480
  927.9 24.9 %collective-permute-done.74.refs_71_ = f32[256,768]{1,0:T(8,128)S(1)} collective-permute-done((f32[256,768]{1,0:T(8,128)}, f32[256,768]{1,0:T(8,128)S(1)}, u32[]{:S(2)}, u32[]{:S(2)}) %collective-permute-start.74) | collective-permute-done | bytes 786464 | tf_op jit(solution)/shard_map/ppermute | solution.py:480
  956.2 35.5 %collective-permute-done.76.refs_72_ = f32[256,512]{1,0:T(8,128)S(1)} collective-permute-done((f32[256,512]{1,0:T(8,128)}, f32[256,512]{1,0:T(8,128)S(1)}, u32[]{:S(2)}, u32[]{:S(2)}) %collective-permute-start.76) | collective-permute-done | bytes 524320 | tf_op jit(solution)/shard_map/ppermute | solution.py:480
  994.3 9.7 collective-permute-done.77.refs_73_
  1004.1 129.6 %shard_map.69 = (f32[2,1024,1024]{2,1,0:T(8,128)}, f32[1024,1024]{1,0:T(8,128)}) custom-call(s32[12]{0:T(128)} %copy-done.42, f32[2,1024,1024]{2,1,0:T(8,128)} %bitcast.41, f32[512,1024]{1,0:T(8,128)} %copy-done, f32[512,1024]{1,0:T(8,128)} %collective-permute-done.5.refs_3_, f32[512,1024]{1,0:T(8,128)} %copy-done.33, ...), custom_call_target="tpu_custom_call" | custom-call | flops 60000002048 | bytes 67108864 | tf_op jit(solution)/shard_map/pallas_call | solution.py:463
  1133.7 5.9 conditional.1
  (253 shorter events, 120.6 us)
Async XLA Ops:
  13.8 53.6 %collective-permute-start.9 = (f32[512,1024]{1,0:T(8,128)}, f32[512,1024]{1,0:T(8,128)S(1)}, u32[]{:S(2)}, u32[]{:S(2)}) collective-permute-start(f32[512,1024]{1,0:T(8,128)} %get-tuple-element.264), channel_id=1, source_target_pairs={{8,10},{9,11},{12,14},{13,15},{16,18},{17,19},{20,22},{21,23},{5,0... | collective-permute-start | bytes 6291464 | tf_op jit(solution)/shard_map/ppermute | solution.py:480
  15.5 52.0 %collective-permute-start.8 = (f32[256,2048]{1,0:T(8,128)S(1)}, f32[256,2048]{1,0:T(8,128)S(1)}, u32[]{:S(2)}, u32[]{:S(2)}) collective-permute-start(f32[256,2048]{1,0:T(8,128)S(1)} %collective-permute-done.6.refs_0_), channel_id=1, source_target_pairs={{1,5}} | collective-permute-start | bytes 6291464 | tf_op jit(solution)/shard_map/ppermute | solution.py:480
  16.4 51.0 %collective-permute-start.7 = (f32[256,1792]{1,0:T(8,128)S(1)}, f32[256,1792]{1,0:T(8,128)}, u32[]{:S(2)}, u32[]{:S(2)}) collective-permute-start(f32[256,1792]{1,0:T(8,128)S(1)} %get-tuple-element.149.refs_4_.refs_27_), channel_id=1, source_target_pairs={{0,1}} | collective-permute-start | bytes 5505032 | tf_op jit(solution)/shard_map/ppermute | solution.py:480
  82.4 49.4 %collective-permute-start.12 = (f32[512,1024]{1,0:T(8,128)}, f32[512,1024]{1,0:T(8,128)}, u32[]{:S(2)}, u32[]{:S(2)}) collective-permute-start(f32[512,1024]{1,0:T(8,128)} %get-tuple-element.263), channel_id=1, source_target_pairs={{8,10},{9,11},{12,14},{13,15},{16,18},{17,19},{20,22},{21,23},{5,0... | collective-permute-start | bytes 6291464 | tf_op jit(solution)/shard_map/ppermute | solution.py:480
  87.6 50.2 %collective-permute-start.18 = (f32[256,1792]{1,0:T(8,128)}, f32[256,1792]{1,0:T(8,128)S(1)}, u32[]{:S(2)}, u32[]{:S(2)}) collective-permute-start(f32[256,1792]{1,0:T(8,128)} %shard_map.43), channel_id=1, source_target_pairs={{1,9},{5,13}} | collective-permute-start | bytes 5505032 | tf_op jit(solution)/shard_map/ppermute | solution.py:480
  88.4 52.8 %collective-permute-start.19 = (f32[256,2048]{1,0:T(8,128)}, f32[256,2048]{1,0:T(8,128)S(1)}, u32[]{:S(2)}, u32[]{:S(2)}) collective-permute-start(f32[256,2048]{1,0:T(8,128)} %collective-permute-done.15.refs_0_.refs_1_.refs_42_), channel_id=1, source_target_pairs={{9,17},{13,21}} | collective-permute-start | bytes 6291464 | tf_op jit(solution)/shard_map/ppermute | solution.py:480
  193.2 230.0 %collective-permute-start.37 = (f32[256,2048]{1,0:T(8,128)}, f32[256,2048]{1,0:T(8,128)}, u32[]{:S(2)}, u32[]{:S(2)}) collective-permute-start(f32[256,2048]{1,0:T(8,128)} %shard_map.50), channel_id=1, source_target_pairs={{9,8},{11,10},{13,12},{15,14},{17,16},{19,18},{21,20},{23,22},{5,4}} | collective-permute-start | bytes 6291464 | tf_op jit(solution)/shard_map/ppermute | solution.py:480
  200.1 307.4 %collective-permute-start.47 = (f32[512,1024]{1,0:T(8,128)}, f32[512,1024]{1,0:T(8,128)}, u32[]{:S(2)}, u32[]{:S(2)}) collective-permute-start(f32[512,1024]{1,0:T(8,128)} %collective-permute-done.20.refs_7_), channel_id=1, source_target_pairs={{18,22},{19,23},{22,18},{23,19}} | collective-permute-start | bytes 6291464 | tf_op jit(solution)/shard_map/ppermute | solution.py:480
  202.1 307.3 %collective-permute-start.45 = (f32[512,1024]{1,0:T(8,128)}, f32[512,1024]{1,0:T(8,128)}, u32[]{:S(2)}, u32[]{:S(2)}) collective-permute-start(f32[512,1024]{1,0:T(8,128)} %collective-permute-done.21.refs_9_), channel_id=1, source_target_pairs={{8,12},{9,13},{12,8},{13,9}} | collective-permute-start | bytes 6291464 | tf_op jit(solution)/shard_map/ppermute | solution.py:480
  204.1 307.8 %collective-permute-start.48 = (f32[512,1024]{1,0:T(8,128)}, f32[512,1024]{1,0:T(8,128)}, u32[]{:S(2)}, u32[]{:S(2)}) collective-permute-start(f32[512,1024]{1,0:T(8,128)} %collective-permute-done.12.refs_2_.refs_5_), channel_id=1, source_target_pairs={{27,18}} | collective-permute-start | bytes 6291464 | tf_op jit(solution)/shard_map/ppermute | solution.py:480
  206.0 306.5 %collective-permute-start.46 = (f32[512,1024]{1,0:T(8,128)}, f32[512,1024]{1,0:T(8,128)}, u32[]{:S(2)}, u32[]{:S(2)}) collective-permute-start(f32[512,1024]{1,0:T(8,128)} %collective-permute-done.12.refs_2_.refs_5_), channel_id=1, source_target_pairs={{10,14},{11,15},{14,10},{15,11}} | collective-permute-start | bytes 6291464 | tf_op jit(solution)/shard_map/ppermute | solution.py:480
  423.2 90.9 %collective-permute-start.44 = (f32[512,1024]{1,0:T(8,128)}, f32[512,1024]{1,0:T(8,128)}, u32[]{:S(2)}, u32[]{:S(2)}) collective-permute-start(f32[512,1024]{1,0:T(8,128)} %collective-permute-done.12.refs_2_.refs_5_), channel_id=1, source_target_pairs={{10,11},{14,15},{18,19},{22,23},{11,10},{15,14},{19,18},{23,22}} | collective-permute-start | bytes 6291464 | tf_op jit(solution)/shard_map/ppermute | solution.py:480
  516.3 85.7 %collective-permute-start.43 = (f32[256,1792]{1,0:T(8,128)}, f32[256,1792]{1,0:T(8,128)}, u32[]{:S(2)}, u32[]{:S(2)}) collective-permute-start(f32[256,1792]{1,0:T(8,128)} %shard_map.54), channel_id=1, source_target_pairs={{9,8},{11,10},{13,12},{15,14},{17,16},{19,18},{21,20},{23,22},{5,4}} | collective-permute-start | bytes 5505032 | tf_op jit(solution)/shard_map/ppermute | solution.py:480
  517.6 87.3 %collective-permute-start.55 = (f32[512,1024]{1,0:T(8,128)}, f32[512,1024]{1,0:T(8,128)}, u32[]{:S(2)}, u32[]{:S(2)}) collective-permute-start(f32[512,1024]{1,0:T(8,128)} %collective-permute-done.10.refs_6_), channel_id=1, source_target_pairs={{16,17},{21,20}} | collective-permute-start | bytes 6291464 | tf_op jit(solution)/shard_map/ppermute | solution.py:480
  519.6 87.0 %collective-permute-start.56 = (f32[512,1024]{1,0:T(8,128)}, f32[512,1024]{1,0:T(8,128)}, u32[]{:S(2)}, u32[]{:S(2)}) collective-permute-start(f32[512,1024]{1,0:T(8,128)} %collective-permute-done.11.refs_8_), channel_id=1, source_target_pairs={{9,8},{12,13}} | collective-permute-start | bytes 6291464 | tf_op jit(solution)/shard_map/ppermute | solution.py:480
  521.6 85.7 %collective-permute-start.57 = (f32[512,1024]{1,0:T(8,128)}, f32[512,1024]{1,0:T(8,128)}, u32[]{:S(2)}, u32[]{:S(2)}) collective-permute-start(f32[512,1024]{1,0:T(8,128)} %collective-permute-done.28.refs_12_), channel_id=1, source_target_pairs={{8,9},{13,12}} | collective-permute-start | bytes 6291464 | tf_op jit(solution)/shard_map/ppermute | solution.py:480
  523.6 85.0 %collective-permute-start.58 = (f32[512,1024]{1,0:T(8,128)}, f32[512,1024]{1,0:T(8,128)}, u32[]{:S(2)}, u32[]{:S(2)}) collective-permute-start(f32[512,1024]{1,0:T(8,128)} %collective-permute-done.29.refs_14_), channel_id=1, source_target_pairs={{10,11},{15,14}} | collective-permute-start | bytes 6291464 | tf_op jit(solution)/shard_map/ppermute | solution.py:480
  602.7 51.5 %collective-permute-start.54 = (f32[256,1536]{1,0:T(8,128)}, f32[256,1536]{1,0:T(8,128)}, u32[]{:S(2)}, u32[]{:S(2)}) collective-permute-start(f32[256,1536]{1,0:T(8,128)} %shard_map.57), channel_id=1, source_target_pairs={{9,8},{11,10},{13,12},{15,14},{17,16},{19,18},{21,20},{23,22},{5,4}} | collective-permute-start | bytes 4718600 | tf_op jit(solution)/shard_map/ppermute | solution.py:480
  654.9 140.0 %collective-permute-start.67 = (f32[256,1280]{1,0:T(8,128)}, f32[256,1280]{1,0:T(8,128)}, u32[]{:S(2)}, u32[]{:S(2)}) collective-permute-start(f32[256,1280]{1,0:T(8,128)} %shard_map.60), channel_id=1, source_target_pairs={{9,8},{11,10},{13,12},{15,14},{17,16},{19,18},{21,20},{23,22},{5,4}} | collective-permute-start | bytes 3932168 | tf_op jit(solution)/shard_map/ppermute | solution.py:480
  795.5 83.4 %collective-permute-start.71 = (f32[256,1024]{1,0:T(8,128)}, f32[256,1024]{1,0:T(8,128)S(1)}, u32[]{:S(2)}, u32[]{:S(2)}) collective-permute-start(f32[256,1024]{1,0:T(8,128)} %shard_map.63), channel_id=1, source_target_pairs={{9,8},{11,10},{13,12},{15,14},{17,16},{19,18},{21,20},{23,22},{5,4}} | collective-permute-start | bytes 3145736 | tf_op jit(solution)/shard_map/ppermute | solution.py:480
  881.1 123.0 %collective-permute-start.59 = (f32[512,1024]{1,0:T(8,128)}, f32[512,1024]{1,0:T(8,128)}, u32[]{:S(2)}, u32[]{:S(2)}) collective-permute-start(f32[512,1024]{1,0:T(8,128)} %collective-permute-done.20.refs_7_), channel_id=1, source_target_pairs={{16,17},{21,20}} | collective-permute-start | bytes 6291464 | tf_op jit(solution)/shard_map/ppermute | solution.py:480
  883.1 121.0 %collective-permute-start.60 = (f32[512,1024]{1,0:T(8,128)}, f32[512,1024]{1,0:T(8,128)}, u32[]{:S(2)}, u32[]{:S(2)}) collective-permute-start(f32[512,1024]{1,0:T(8,128)} %collective-permute-done.21.refs_9_), channel_id=1, source_target_pairs={{9,8},{12,13}} | collective-permute-start | bytes 6291464 | tf_op jit(solution)/shard_map/ppermute | solution.py:480
  885.0 119.0 %collective-permute-start.61 = (f32[512,1024]{1,0:T(8,128)}, f32[512,1024]{1,0:T(8,128)}, u32[]{:S(2)}, u32[]{:S(2)}) collective-permute-start(f32[512,1024]{1,0:T(8,128)} %collective-permute-done.45.refs_13_), channel_id=1, source_target_pairs={{8,9},{13,12}} | collective-permute-start | bytes 6291464 | tf_op jit(solution)/shard_map/ppermute | solution.py:480
  887.1 117.0 %collective-permute-start.62 = (f32[512,1024]{1,0:T(8,128)}, f32[512,1024]{1,0:T(8,128)}, u32[]{:S(2)}, u32[]{:S(2)}) collective-permute-start(f32[512,1024]{1,0:T(8,128)} %collective-permute-done.46.refs_15_), channel_id=1, source_target_pairs={{10,11},{15,14}} | collective-permute-start | bytes 6291464 | tf_op jit(solution)/shard_map/ppermute | solution.py:480
  (93 other events, 3112.4 us)

commit v2 on v1

--- a/solution.py
+++ b/solution.py
@@ -8,9 +8,9 @@
 SUB = 8
 BASE = 128
 BLOCK = 256
-FIRST = (2, 4)
-SECOND = (5, 7)
-THIRD = (8,)
+FIRST = 3
+SECOND = 6
+THIRD = 8
 NN = ((1,), (0,))
 NT = ((1,), (1,))
 TN = ((0,), (0,))
@@ -87,7 +87,7 @@
 
 def factor_kernel(kind, flag_ref, *refs):
     refs = list(refs)
-    sources = [refs.pop(0) for _ in range({"first": 3, "next": 1, "schur": 6}[kind])]
+    sources = [refs.pop(0) for _ in range({"first": 2, "next": 1, "schur": 5}[kind])]
     a_ref, f_ref, sems = refs[-3:]
     f_out = refs[0]
     rest_out = refs[1] if len(refs) > 4 else None
@@ -103,12 +103,9 @@
             copies[-1].start()
 
         if kind == "first":
-            left, right, cut = pl.ds(0, n), pl.ds(n, n), n // 2 - BLOCK
-            load(sources[0].at[0, top], a_ref.at[top, left])
-            load(sources[1].at[top], a_ref.at[top, right])
-            load(sources[0].at[0, below], a_ref.at[below, left])
-            load(sources[1].at[pl.ds(BLOCK, cut)], a_ref.at[pl.ds(BLOCK, cut), right])
-            load(sources[2], a_ref.at[pl.ds(n // 2, n // 2), right])
+            for rows in (top, below):
+                load(sources[0].at[0, rows], a_ref.at[rows, pl.ds(0, n)])
+                load(sources[1].at[rows], a_ref.at[rows, pl.ds(n, n)])
             needed = 2
         elif kind == "next":
             load(sources[0].at[top], a_ref.at[top])
@@ -117,9 +114,8 @@
             needed = 1
         else:
             parts = refs[-4]
-            for h in range(2):
-                load(sources[h], a_ref.at[pl.ds(h * n // 2, n // 2)])
-            for p, part in enumerate(sources[2:]):
+            load(sources[0], a_ref)
+            for p, part in enumerate(sources[1:]):
                 load(
                     part.at[:, pl.ds(part.shape[1] - n, n)],
                     parts.at[pl.ds(p * BLOCK, BLOCK)],
@@ -205,21 +201,28 @@
 
 def choose(index, options):
     def kernel(index_ref, *refs):
-        *bufs, out_ref, sem = refs
+        *bufs, out_ref, held, sem = refs
         for k, buf in enumerate(bufs):
 
             @pl.when(index_ref[0] == k)
             def _():
-                copy = pltpu.make_async_copy(buf, out_ref, sem)
+                copy = pltpu.make_async_copy(buf, held, sem)
                 copy.start()
                 copy.wait()
+
+        @pl.when(index_ref[0] >= 0)
+        def _():
+            copy = pltpu.make_async_copy(held, out_ref, sem)
+            copy.start()
+            copy.wait()
 
     return pl.pallas_call(
         kernel,
         out_shape=shape(*options[0].shape),
         in_specs=[SMEM] + [ANY] * len(options),
         out_specs=ANY,
-        scratch_shapes=[DMA(())],
+        scratch_shapes=[pltpu.VMEM(options[0].shape, F32), DMA(())],
+        compiler_params=params(8),
     )(index, *options)
 
 
@@ -231,22 +234,24 @@
 
 def patch(flags, result, parts):
     def kernel(flags_ref, result_ref, *refs):
-        *bufs, out_ref, sems = refs
+        *bufs, out_ref, held, sem = refs
         for k, buf in enumerate(bufs):
 
             @pl.when(flags_ref[k] == 1)
             def _():
-                copy = pltpu.make_async_copy(buf, out_ref.at[k], sems.at[k])
-                copy.start()
-                copy.wait()
+                for source, target in ((buf, held), (held, out_ref.at[k])):
+                    copy = pltpu.make_async_copy(source, target, sem)
+                    copy.start()
+                    copy.wait()
 
     return pl.pallas_call(
         kernel,
         out_shape=shape(*result.shape),
         in_specs=[SMEM] + [ANY] * (1 + len(parts)),
         out_specs=ANY,
-        scratch_shapes=[DMA((len(parts),))],
+        scratch_shapes=[pltpu.VMEM(parts[0].shape, F32), DMA(())],
         input_output_aliases={1: 0},
+        compiler_params=params(8),
     )(flags, result, *parts)
 
 
@@ -272,14 +277,10 @@
     steps = order // BLOCK
     count = 2 * steps
     sets = [refs[k * count : (k + 1) * count] for k in range(n_sets)]
-    out_ref, p1_ref, z, t, high, low, *fs, sems = refs[n_sets * count :]
+    out_ref, p1_ref, z, t, spare, high, low, *fs, sems = refs[n_sets * count :]
     role, transposed, which, col, edge = (meta_ref[k] for k in (0, 5, 6, 7, 8))
     half = pl.ds(0, order), pl.ds(order, order)
-    mid = order // 2
-    sources = [
-        [tiles_ref.at[0, pl.ds(h * mid, mid)]] + [raws[2 * k + h] for k in range(n_raw // 2)]
-        for h in range(2)
-    ]
+    sources = [tiles_ref.at[0]] + list(raws)
 
     def load_pieces(pieces):
         for k in range(n_sets):
@@ -299,7 +300,11 @@
 
     @pl.when(role == PASS)
     def _():
-        copies = [move_out(tiles_ref.at[k], out_ref.at[k], k) for k in range(2)]
+        held = (t, spare)
+        copies = [move_out(tiles_ref.at[k], held[k], k) for k in range(2)]
+        for k in range(2):
+            copies[k].wait()
+            copies[k] = move_out(held[k], out_ref.at[k], k)
         for copy in copies:
             copy.wait()
 
@@ -346,19 +351,13 @@
 
     @pl.when(role == WORK)
     def _():
-        places = [
-            [z.at[pl.ds(a * order + h * mid, mid), pl.ds(b * order, order)] for h in range(2)]
-            for a in range(2)
-            for b in range(2)
-        ]
+        places = [z.at[half[a], half[b]] for a in range(2) for b in range(2)]
         for s, place in enumerate(places):
-            for k in range(len(sources[0])):
+            for k, source in enumerate(sources):
 
                 @pl.when(meta_ref[1 + s] == k)
                 def _():
-                    for h in range(2):
-                        sem = sems.at[8 + count + 2 * s + h]
-                        pltpu.make_async_copy(sources[h][k], place[h], sem).start()
+                    pltpu.make_async_copy(source, place, sems.at[s]).start()
 
         load_pieces(range(count))
         for slot, taken in ((1, col < 2), (0, col >= 2)):
@@ -369,12 +368,10 @@
 
         @pl.when(col >= 2)
         def _():
-            move_out(tiles_ref.at[1], out_ref.at[1], 5)
+            move_out(tiles_ref.at[1], spare, 5)
 
         for s, place in enumerate(places):
-            for h in range(2):
-                sem = sems.at[8 + count + 2 * s + h]
-                pltpu.make_async_copy(sources[h][1], place[h], sem).wait()
+            pltpu.make_async_copy(sources[1], place, sems.at[s]).wait()
 
         @pl.when(transposed == 1)
         def _():
@@ -427,6 +424,11 @@
 
             lax.fori_loop(0, steps, update, 0)
 
+        @pl.when(col >= 2)
+        def _():
+            pltpu.make_async_copy(tiles_ref.at[1], spare, sems.at[5]).wait()
+            move_out(spare, out_ref.at[1], 5)
+
         @pl.when(col == 0)
         def _():
             move_out(z.at[half[0], half[0]], out_ref.at[0], 5)
@@ -456,10 +458,11 @@
     scratch = [
         pltpu.VMEM((2 * order, 2 * order), F32),
         pltpu.VMEM((order, order), F32),
+        pltpu.VMEM((order, order), F32),
         pltpu.VMEM((2 * order, BLOCK), jnp.bfloat16),
         pltpu.VMEM((2 * order, BLOCK), jnp.bfloat16),
     ]
-    scratch += [pltpu.VMEM(f.shape, F32) for f in sets[0]] + [DMA((16 + count,))]
+    scratch += [pltpu.VMEM(f.shape, F32) for f in sets[0]] + [DMA((8 + count,))]
     return pl.pallas_call(
         lambda *refs: finish_kernel(len(raws), len(sets), *refs),
         out_shape=[shape(*tiles.shape), shape(order, order)],
@@ -474,8 +477,6 @@
 
 
 def move(value, pairs, cols):
-    if isinstance(value, list):
-        return [move(v, pairs, cols) for v in value]
     flat = [(a * cols + b, c * cols + d) for (a, b), (c, d) in pairs]
     return lax.ppermute(value, ("row", "col"), flat)
 
@@ -513,7 +514,7 @@
     rows, cols = lax.axis_size("row"), lax.axis_size("col")
     row, col = lax.axis_index("row"), lax.axis_index("col")
     tiles = kernel_tiles.reshape(2, order, order)
-    near = [tiles[0, h * order // 2 : (h + 1) * order // 2] for h in range(2)]
+    near = tiles[0]
     steps = order // BLOCK
     count = 2 * steps
     edge = cols + 2
@@ -522,7 +523,7 @@
     workers = range(2, edge)
     routed = cols == 4
 
-    plan = [[[PASS, 0, 0, 0, 0, 0, 0, 0, 0, -1, -1, -1] for _ in range(cols)] for _ in range(rows)]
+    plan = [[[PASS] + [0] * 8 + [-1] * 5 for _ in range(cols)] for _ in range(rows)]
     for r in range(rows):
         for c in range(cols):
             plan[r][c][7] = c
@@ -556,11 +557,19 @@
             for c in range(4):
                 plan[r][c][3:5] = plan[r][c][1:3]
         for place, pair in {
-            (2, 0): (4, 10), (2, 1): (11, 6), (3, 0): (6, 11), (3, 1): (10, 4),
-            (4, 1): (9, 3), (5, 0): (3, 9), (2, 3): (12, 7), (3, 2): (7, 12),
-            (4, 2): (3, 8), (4, 3): (3, 8), (5, 2): (8, 3), (5, 3): (8, 3),
+            (2, 0): (4, 7), (2, 1): (7, 6), (3, 0): (6, 7), (3, 1): (7, 4),
+            (4, 1): (7, 3), (5, 0): (3, 7), (2, 3): (7, 6), (3, 2): (6, 7),
+            (4, 2): (3, 6), (4, 3): (3, 6), (5, 2): (6, 3), (5, 3): (6, 3),
         }.items():
             plan[place[0]][place[1]][3:5] = pair
+        for c in (0, 1):
+            plan[2][c][12] = plan[3][c][12] = 2
+        for c in (2, 3):
+            plan[2][c][12] = plan[3][c][12] = 0
+            plan[4][c][12] = plan[5][c][12] = 1
+        plan[4][0][13] = plan[5][1][13] = 0
+        plan[2][1][13] = plan[3][0][13] = 1
+        plan[2][0][13] = plan[3][1][13] = plan[2][2][13] = plan[3][3][13] = 2
         for r in (4, 5):
             for c in (2, 3):
                 plan[r][c][5] = 1
@@ -577,15 +586,14 @@
             plan[r][3][11] = 3
         plan[1][1][11] = 0
     else:
-        mine = jnp.where(col < 2, tiles[1], tiles[0])
-        mine = [mine[: order // 2], mine[order // 2 :]]
-        left0 = [doubling(v, "col", 0, cols) for v in near]
-        left1 = [doubling(v, "col", 1, cols) for v in near]
-        top0 = [doubling(v, "row", 0, rows) for v in mine]
-        top1 = [doubling(v, "row", 1, rows) for v in mine]
+        mine = jnp.where(col < 2, tiles[1], near)
+        left0 = doubling(near, "col", 0, cols)
+        left1 = doubling(near, "col", 1, cols)
+        top0 = doubling(mine, "row", 0, rows)
+        top1 = doubling(mine, "row", 1, rows)
         tile01 = move(near, [((0, 1), (0, 0))], cols)
         tile11 = move(near, [((1, 1), (0, 0))], cols)
-        raws = left0 + left1 + top0 + top1
+        raws = [left0, left1, top0, top1]
         for r in range(rows):
             for c in range(cols):
                 plan[r][c][1:6] = [1, 2, 3, 4, 1]
@@ -593,7 +601,6 @@
     meta = meta.at[8].set(edge_live.astype(jnp.int32))
 
     pieces, copies, state = [], [], None
-    r5, r6a, r6b, r6c, e1, r7a, r7b, r7c, r7d = ([] for _ in range(9))
     stages = 6 if routed else 0
     late = []
     for slot in range(count + stages):
@@ -602,9 +609,9 @@
             step, local = divmod(slot, steps)
             n = order - local * BLOCK
             if slot == 0:
-                args = ("first", owner, n, 2 * n, tiles, *tile01)
+                args = ("first", owner, n, 2 * n, tiles, tile01)
             elif local == 0:
-                args = ("schur", owner, n, n, *(r2 if routed else tile11), *pieces)
+                args = ("schur", owner, n, n, r2 if routed else tile11, *pieces)
             else:
                 args = ("next", owner, n, n + (1 - step) * order, state)
             piece, state = factor_block(*args)
@@ -642,13 +649,13 @@
                     )
                 )
             arrived.append(p)
-        late = {
-            FIRST[0]: lambda: [r2[0], r3[0], r4[0]],
-            FIRST[1]: lambda: [r2[1], r3[1], r4[1]],
-            SECOND[0]: lambda: [r5[0], r6a[0], r6b[0], r6c[0], e1[0]],
-            SECOND[1]: lambda: [r5[1], r6a[1], r6b[1], r6c[1], e1[1]],
-            THIRD[0]: lambda: [r7a[0], r7b[0], r7c[0], r7d[0]],
-        }.get(slot, list)()
+        late = []
+        if slot == FIRST:
+            late = [r2, r3, r4]
+        elif slot == SECOND:
+            late = [r5, r6, e1]
+        elif slot == THIRD:
+            late = [r7]
         last = [copies[p][-1] for p in arrived]
         flowing = ([pieces[slot]] if slot < count else []) + ([] if state is None else [state])
         flowing, last, late = lax.optimization_barrier((flowing, last, late))
@@ -658,26 +665,29 @@
             state = flowing[-1]
         for p, value in zip(arrived, last):
             copies[p][-1] = value
-        for h in range(2):
-            if slot == FIRST[h]:
-                r2[h], r3[h], r4[h] = late
-                r5.append(move(r2[h], both_ways([((r, 2), (r, 3)) for r in workers]), cols))
-                r6a.append(move(r4[h], both_ways([((2, c), (3, c)) for c in (0, 1)]), cols))
-                r6b.append(move(r2[h], both_ways([((2, c), (3, c)) for c in (2, 3)]), cols))
-                r6c.append(move(r3[h], both_ways([((4, c), (5, c)) for c in (2, 3)]), cols))
-                e1.append(move(r2[h], [((edge, 3), (edge - 2, 2))], cols))
-            elif slot == SECOND[h]:
-                r5[h], r6a[h], r6b[h], r6c[h], e1[h] = late
-                r7a.append(move(r3[h], [((4, 0), (4, 1)), ((5, 1), (5, 0))], cols))
-                r7b.append(move(r4[h], [((2, 1), (2, 0)), ((3, 0), (3, 1))], cols))
-                r7c.append(move(r6a[h], [((2, 0), (2, 1)), ((3, 1), (3, 0))], cols))
-                r7d.append(move(r6b[h], [((2, 2), (2, 3)), ((3, 3), (3, 2))], cols))
-        if slot == THIRD[0]:
-            r7a[0], r7b[0], r7c[0], r7d[0] = late
+        if slot == FIRST:
+            r2, r3, r4 = late
+            r5 = move(r2, both_ways([((r, 2), (r, 3)) for r in workers]), cols)
+            r6 = move(
+                choose(meta[12:13], [r2, r3, r4]),
+                both_ways([((2, c), (3, c)) for c in range(4)] + [((4, c), (5, c)) for c in (2, 3)]),
+                cols,
+            )
+            e1 = move(r2, [((edge, 3), (edge - 2, 2))], cols)
+        elif slot == SECOND:
+            r5, r6, e1 = late
+            r7 = move(
+                choose(meta[13:14], [r3, r4, r6]),
+                [((4, 0), (4, 1)), ((5, 1), (5, 0)), ((2, 1), (2, 0)), ((3, 0), (3, 1))]
+                + [((2, 0), (2, 1)), ((3, 1), (3, 0)), ((2, 2), (2, 3)), ((3, 3), (3, 2))],
+                cols,
+            )
+        elif slot == THIRD:
+            (r7,) = late
 
     if routed:
         sets = [pieces] + [[got[k] for got in copies] for k in (1, 2, 3, 4, 5)]
-        raws = r1 + r2 + r3 + r4 + r5 + r6a + r6b + r6c + r7a + r7b + r7c + r7d
+        raws = [r1, r2, r3, r4, r5, r6, r7]
     else:
         sets = [[got[0] for got in copies]]
 
@@ -696,7 +706,7 @@
     def edge_parts(args):
         panel1, edge_tile, last_pieces = args
         far = tiles[1]
-        edge_tile = fetch(jnp.concatenate(edge_tile, 0))
+        edge_tile = fetch(edge_tile)
         last = eliminate_last(edge_tile, last_pieces)
         column = far - dot(panel1, last, NT, lax.Precision.HIGH)
         sent = move(column, [((r, 2), (edge, r % cols)) for r in workers], cols).T
@@ -707,7 +717,7 @@
         return part0, part1
 
     def no_edge(args):
-        return unset(tiles[0]), unset(tiles[0])
+        return unset(near), unset(near)
 
     parts = lax.cond(edge_live, edge_parts, no_edge, (panel1, e1 if routed else near, sets[-1][steps:]))
     at_edge = edge_live & (row == edge)

time: 1160 us -> 465 us (0.40)
  waiting for transfers between devices: 654 us -> 242 us
  starting transfers between devices: 305 us -> 87.5 us
  Pallas kernels: 153 us -> 103 us
    ppermute x74 -> x56, waiting for transfers between devices: 654 us -> 242 us  [move(): return lax.ppermute(value, ('row', 'col'), flat)]
    ppermute x74 -> x56, starting transfers between devices: 305 us -> 87.5 us  [move(): return lax.ppermute(value, ('row', 'col'), flat)]
    pallas_call x1, Pallas kernels: 130 us -> 70.4 us  [finish(): pl.pallas_call(lambda *refs: finish_kernel(len(raws), len(sets), *refs),...]
    pallas_call x24 -> x26, Pallas kernels: 15.6 us -> 24.6 us  [choose(): pl.pallas_call(kernel, out_shape=shape(*options[0].shape), in_specs=[SMEM...]
  transfers between devices with their start and end apart: 74 -> 56, of which waited for: 10 -> 8; matrix products, arithmetic and copies ran while one was open for 0% -> 0% of each run, Pallas kernels for 2% -> 6%
where the time goes in v2:
time: 465 us; the launch traced here: 456 us
  waiting for transfers between devices  242 us (52%)
  Pallas kernels  103 us (22%)
  starting transfers between devices  87.5 us (19%)
  local copies, waits for them, and re-layouts  14.2 us (3%)
  loops' own time  5.92 us (1%)
    ppermute x56, waiting for transfers between devices, move(): return lax.ppermute(value, ('row', 'col'), flat)  242 us
    ppermute x56, starting transfers between devices, move(): return lax.ppermute(value, ('row', 'col'), flat)  87.5 us
    pallas_call x1, Pallas kernels, finish(): pl.pallas_call(lambda *refs: finish_kernel(len(raws), len(sets), *refs),...  70.4 us
    pallas_call x26, Pallas kernels, choose(): pl.pallas_call(kernel, out_shape=shape(*options[0].shape), in_specs=[SMEM...  24.6 us
  transfers between devices with their start and end apart: 56, of which 8 were waited for; matrix products, arithmetic and copies ran while one was open for 0% of the time, Pallas kernels for 6%

profile of v2, /device:TPU:12, one launch (start us, length us, event | category | flops | bytes accessed | tf_op | source)
XLA Modules:
  0.0 455.6 jit_solution(16401921353776885535)
XLA Ops:
  0.0 4.8 %slice_bitcast_fusion.1 = f32[1024,1024]{1,0:T(8,128)} fusion(f32[1,1,2,1,1024,1024]{5,4,3,2,1,0:T(8,128)} %param.7), kind=kLoop, calls=%fused_computation.65 | loop fusion | bytes 8388608 | tf_op jit(solution)/shard_map/squeeze | solution.py:517
  4.8 2.7 collective-permute-start.4
  7.6 2.1 collective-permute-start.5
  9.7 2.6 collective-permute-start.13
  15.5 2.6 collective-permute-start.12
  30.2 86.2 %collective-permute-done.11.refs_1_.refs_0_.refs_3_ = f32[1024,1024]{1,0:T(8,128)} collective-permute-done((f32[1024,1024]{1,0:T(8,128)}, f32[1024,1024]{1,0:T(8,128)}, u32[]{:S(2)}, u32[]{:S(2)}) %collective-permute-start.11) | collective-permute-done | bytes 4194336 | tf_op jit(solution)/shard_map/ppermute | solution.py:481
  118.0 2.0 collective-permute-start.16
  122.9 6.2 %shard_map.42 = (f32[256,1024]{1,0:T(8,128)}, f32[768,768]{1,0:T(8,128)}) custom-call(s32[1]{0:T(128)} %bitcast.11.refs_0_, f32[1024,1024]{1,0:T(8,128)} %collective-permute-done.11.refs_1_.refs_0_.refs_3_, f32[256,2048]{1,0:T(8,128)} %copy-done.19, f32[256,1792]{1,0:T(8,128)} %get-tuple-element.133.refs_3_.refs_10_, f32[256,1536]{1,0:T(8,128)S(1)} %copy-done.23, ...), custom_call_target="tpu_custom_call" | custom-call | flops 2000000000 | bytes 8388608 | tf_op jit(solution)/shard_map/pallas_call | solution.py:188
  130.7 4.8 %shard_map.51 = f32[1024,1024]{1,0:T(8,128)} custom-call(s32[1]{0:T(128)} %get-tuple-element.233.index_ref, f32[1024,1024]{1,0:T(8,128)} %collective-permute-done.11.refs_1_.refs_0_.refs_3_, f32[1024,1024]{1,0:T(8,128)} %collective-permute-done.12.refs_1_.refs_0_.refs_4_, f32[1024,1024]{1,0:T(8,128)} %collective-permute-done.13.refs_2_.refs_1_.refs_5_), custom_call_target="tpu_custom_call" | custom-call | tf_op jit(solution)/shard_map/pallas_call | solution.py:219
  135.6 3.4 collective-permute-start.30
  139.0 2.7 collective-permute-start.31
  143.9 1.9 collective-permute-start.29
  146.6 2.0 collective-permute-start.22
  155.2 74.7 %collective-permute-done.30.refs_2_.refs_7_ = f32[1024,1024]{1,0:T(8,128)} collective-permute-done((f32[1024,1024]{1,0:T(8,128)}, f32[1024,1024]{1,0:T(8,128)}, u32[]{:S(2)}, u32[]{:S(2)}) %collective-permute-start.30) | collective-permute-done | bytes 4194336 | tf_op jit(solution)/shard_map/ppermute | solution.py:481
  236.5 3.2 shard_map.59
  239.7 18.8 %collective-permute-start.44 = (f32[1024,1024]{1,0:T(8,128)S(1)}, f32[1024,1024]{1,0:T(8,128)}, u32[]{:S(2)}, u32[]{:S(2)}) collective-permute-start(f32[1024,1024]{1,0:T(8,128)S(1)} %shard_map.59), channel_id=1, source_target_pairs={{16,17},{21,20},{9,8},{12,13},{8,9},{13,12},{10,11},{15,14}} | collective-permute-start | bytes 12582920 | tf_op jit(solution)/shard_map/ppermute | solution.py:481
  275.5 23.0 %collective-permute-done.43.refs_51_ = f32[256,1536]{1,0:T(8,128)S(1)} collective-permute-done((f32[256,1536]{1,0:T(8,128)S(1)}, f32[256,1536]{1,0:T(8,128)S(1)}, u32[]{:S(2)}, u32[]{:S(2)}) %collective-permute-start.43) | collective-permute-done | bytes 1572896 | tf_op jit(solution)/shard_map/ppermute | solution.py:481
  304.8 16.2 %collective-permute-done.49.refs_52_ = f32[256,1280]{1,0:T(8,128)S(1)} collective-permute-done((f32[256,1280]{1,0:T(8,128)S(1)}, f32[256,1280]{1,0:T(8,128)S(1)}, u32[]{:S(2)}, u32[]{:S(2)}) %collective-permute-start.49) | collective-permute-done | bytes 1310752 | tf_op jit(solution)/shard_map/ppermute | solution.py:481
  326.9 13.2 %collective-permute-done.53.refs_53_ = f32[256,1024]{1,0:T(8,128)S(1)} collective-permute-done((f32[256,1024]{1,0:T(8,128)S(1)}, f32[256,1024]{1,0:T(8,128)S(1)}, u32[]{:S(2)}, u32[]{:S(2)}) %collective-permute-start.53) | collective-permute-done | bytes 1048608 | tf_op jit(solution)/shard_map/ppermute | solution.py:481
  344.2 11.1 %collective-permute-done.56.refs_54_ = f32[256,768]{1,0:T(8,128)S(1)} collective-permute-done((f32[256,768]{1,0:T(8,128)S(1)}, f32[256,768]{1,0:T(8,128)S(1)}, u32[]{:S(2)}, u32[]{:S(2)}) %collective-permute-start.56) | collective-permute-done | bytes 786464 | tf_op jit(solution)/shard_map/ppermute | solution.py:481
  358.8 9.1 %collective-permute-done.58.refs_55_ = f32[256,512]{1,0:T(8,128)} collective-permute-done((f32[256,512]{1,0:T(8,128)S(1)}, f32[256,512]{1,0:T(8,128)}, u32[]{:S(2)}, u32[]{:S(2)}) %collective-permute-start.58) | collective-permute-done | bytes 524320 | tf_op jit(solution)/shard_map/ppermute | solution.py:481
  370.0 8.1 %collective-permute-done.59.refs_56_ = f32[256,256]{1,0:T(8,128)S(1)} collective-permute-done((f32[256,256]{1,0:T(8,128)S(1)}, f32[256,256]{1,0:T(8,128)S(1)}, u32[]{:S(2)}, u32[]{:S(2)}) %collective-permute-start.59) | collective-permute-done | bytes 262176 | tf_op jit(solution)/shard_map/ppermute | solution.py:481
  378.1 70.4 %shard_map.71 = (f32[2,1024,1024]{2,1,0:T(8,128)}, f32[1024,1024]{1,0:T(8,128)}) custom-call(s32[14]{0:T(128)} %copy-done.49, f32[2,1024,1024]{2,1,0:T(8,128)} %bitcast.38, f32[1024,1024]{1,0:T(8,128)} %collective-permute-done.4.refs_2_, f32[1024,1024]{1,0:T(8,128)} %collective-permute-done.11.refs_1_.refs_0_.refs_3_, ...), custom_call_target="tpu_custom_call" | custom-call | flops 60000002048 | bytes 67108864 | tf_op jit(solution)/shard_map/pallas_call | solution.py:466
  448.6 5.9 %conditional.1 = (f32[1024,1024]{1,0:T(8,128)}, f32[1024,1024]{1,0:T(8,128)}) conditional(s32[]{:T(128)} %convert_element_type.9, () %tuple.41, (s32[]{:T(128)}, f32[1024,1024]{1,0:T(8,128)}, f32[256,1024]{1,0:T(8,128)S(1)}, f32[256,768]{1,0:T(8,128)}, f32[256,512]{1,0:T(8,128)}, /*index=5*/f32[256,256]{1,0:T(8,128)S(1)}, f32[2,1024,1024]{2,1,0:T(8,128)}, ...), branch_computations={%region_0.0_spmd, %region_1.0_spmd} | conditional | flops 16927950848 | bytes 270567744 | solution.py:722
  (235 shorter events, 75.0 us)
Async XLA Ops:
  9.7 18.6 %collective-permute-start.13 = (f32[1024,1024]{1,0:T(8,128)}, f32[1024,1024]{1,0:T(8,128)}, u32[]{:S(2)}, u32[]{:S(2)}) collective-permute-start(f32[1024,1024]{1,0:T(8,128)} %slice_bitcast_fusion.1), channel_id=1, source_target_pairs={{16,8},{17,9},{20,12},{21,13}} | collective-permute-start | bytes 12582920 | tf_op jit(solution)/shard_map/ppermute | solution.py:481
  14.7 11.4 %collective-permute-start.7 = (f32[256,2048]{1,0:T(8,128)}, f32[256,2048]{1,0:T(8,128)S(1)}, u32[]{:S(2)}, u32[]{:S(2)}) collective-permute-start(f32[256,2048]{1,0:T(8,128)} %collective-permute-done.5.refs_0_), channel_id=1, source_target_pairs={{1,5}} | collective-permute-start | bytes 6291464 | tf_op jit(solution)/shard_map/ppermute | solution.py:481
  15.5 14.7 %collective-permute-start.12 = (f32[1024,1024]{1,0:T(8,128)}, f32[1024,1024]{1,0:T(8,128)}, u32[]{:S(2)}, u32[]{:S(2)}) collective-permute-start(f32[1024,1024]{1,0:T(8,128)} %slice_bitcast_fusion.1), channel_id=1, source_target_pairs={{16,20},{17,21},{20,16},{21,17},{2,18},{3,19},{6,22},{7,23}} | collective-permute-start | bytes 12582920 | tf_op jit(solution)/shard_map/ppermute | solution.py:481
  18.1 98.4 %collective-permute-start.11 = (f32[1024,1024]{1,0:T(8,128)}, f32[1024,1024]{1,0:T(8,128)}, u32[]{:S(2)}, u32[]{:S(2)}) collective-permute-start(f32[1024,1024]{1,0:T(8,128)} %slice_bitcast_fusion.1), channel_id=1, source_target_pairs={{8,10},{9,11},{12,14},{13,15},{16,18},{17,19},{20,22},{21,23},{5,0... | collective-permute-start | bytes 12582920 | tf_op jit(solution)/shard_map/ppermute | solution.py:481
  26.7 89.8 %collective-permute-start.10 = (f32[256,2048]{1,0:T(8,128)S(1)}, f32[256,2048]{1,0:T(8,128)S(1)}, u32[]{:S(2)}, u32[]{:S(2)}) collective-permute-start(f32[256,2048]{1,0:T(8,128)S(1)} %shard_map.41), channel_id=1, source_target_pairs={{1,9},{5,13}} | collective-permute-start | bytes 6291464 | tf_op jit(solution)/shard_map/ppermute | solution.py:481
  27.5 89.0 %collective-permute-start.9 = (f32[256,1792]{1,0:T(8,128)}, f32[256,1792]{1,0:T(8,128)S(1)}, u32[]{:S(2)}, u32[]{:S(2)}) collective-permute-start(f32[256,1792]{1,0:T(8,128)} %collective-permute-done.6.refs_0_), channel_id=1, source_target_pairs={{1,5}} | collective-permute-start | bytes 5505032 | tf_op jit(solution)/shard_map/ppermute | solution.py:481
  28.3 88.2 %collective-permute-start.8 = (f32[256,1536]{1,0:T(8,128)S(1)}, f32[256,1536]{1,0:T(8,128)}, u32[]{:S(2)}, u32[]{:S(2)}) collective-permute-start(f32[256,1536]{1,0:T(8,128)S(1)} %get-tuple-element.136.refs_4_.refs_11_), channel_id=1, source_target_pairs={{0,1}} | collective-permute-start | bytes 4718600 | tf_op jit(solution)/shard_map/ppermute | solution.py:481
  116.5 12.6 %collective-permute-start.17 = (f32[256,2048]{1,0:T(8,128)S(1)}, f32[256,2048]{1,0:T(8,128)S(1)}, u32[]{:S(2)}, u32[]{:S(2)}) collective-permute-start(f32[256,2048]{1,0:T(8,128)S(1)} %collective-permute-done.10.refs_0_.refs_1_.refs_25_), channel_id=1, source_target_pairs={{9,17},{13,21}} | collective-permute-start | bytes 6291464 | tf_op jit(solution)/shard_map/ppermute | solution.py:481
  118.0 11.0 %collective-permute-start.16 = (f32[256,1792]{1,0:T(8,128)}, f32[256,1792]{1,0:T(8,128)}, u32[]{:S(2)}, u32[]{:S(2)}) collective-permute-start(f32[256,1792]{1,0:T(8,128)} %shard_map.43), channel_id=1, source_target_pairs={{1,9},{5,13}} | collective-permute-start | bytes 5505032 | tf_op jit(solution)/shard_map/ppermute | solution.py:481
  120.1 9.0 %collective-permute-start.15 = (f32[256,1536]{1,0:T(8,128)}, f32[256,1536]{1,0:T(8,128)}, u32[]{:S(2)}, u32[]{:S(2)}) collective-permute-start(f32[256,1536]{1,0:T(8,128)} %collective-permute-done.8.refs_0_), channel_id=1, source_target_pairs={{1,5}} | collective-permute-start | bytes 4718600 | tf_op jit(solution)/shard_map/ppermute | solution.py:481
  129.1 14.8 %collective-permute-start.18 = (f32[256,1024]{1,0:T(8,128)}, f32[256,1024]{1,0:T(8,128)}, u32[]{:S(2)}, u32[]{:S(2)}) collective-permute-start(f32[256,1024]{1,0:T(8,128)} %get-tuple-element.151.refs_13_), channel_id=1, source_target_pairs={{0,1}} | collective-permute-start | bytes 3145736 | tf_op jit(solution)/shard_map/ppermute | solution.py:481
  135.6 94.3 %collective-permute-start.30 = (f32[1024,1024]{1,0:T(8,128)}, f32[1024,1024]{1,0:T(8,128)}, u32[]{:S(2)}, u32[]{:S(2)}) collective-permute-start(f32[1024,1024]{1,0:T(8,128)} %shard_map.51), channel_id=1, source_target_pairs={{8,12},{9,13},{10,14},{11,15},{18,22},{19,23},{12,8},{13,9},{14,10... | collective-permute-start | bytes 12582920 | tf_op jit(solution)/shard_map/ppermute | solution.py:481
  139.0 91.7 %collective-permute-start.31 = (f32[1024,1024]{1,0:T(8,128)}, f32[1024,1024]{1,0:T(8,128)}, u32[]{:S(2)}, u32[]{:S(2)}) collective-permute-start(f32[1024,1024]{1,0:T(8,128)} %collective-permute-done.11.refs_1_.refs_0_.refs_3_), channel_id=1, source_target_pairs={{27,18}} | collective-permute-start | bytes 12582920 | tf_op jit(solution)/shard_map/ppermute | solution.py:481
  143.9 88.1 %collective-permute-start.29 = (f32[1024,1024]{1,0:T(8,128)}, f32[1024,1024]{1,0:T(8,128)}, u32[]{:S(2)}, u32[]{:S(2)}) collective-permute-start(f32[1024,1024]{1,0:T(8,128)} %collective-permute-done.11.refs_1_.refs_0_.refs_3_), channel_id=1, source_target_pairs={{10,11},{14,15},{18,19},{22,23},{11,10},{15,14},{19,18},{23,22}} | collective-permute-start | bytes 12582920 | tf_op jit(solution)/shard_map/ppermute | solution.py:481
  151.5 84.9 %collective-permute-start.28 = (f32[256,2048]{1,0:T(8,128)}, f32[256,2048]{1,0:T(8,128)}, u32[]{:S(2)}, u32[]{:S(2)}) collective-permute-start(f32[256,2048]{1,0:T(8,128)} %shard_map.50), channel_id=1, source_target_pairs={{9,8},{11,10},{13,12},{15,14},{17,16},{19,18},{21,20},{23,22},{5,4}} | collective-permute-start | bytes 6291464 | tf_op jit(solution)/shard_map/ppermute | solution.py:481
  152.8 80.0 %collective-permute-start.23 = (f32[256,768]{1,0:T(8,128)}, f32[256,768]{1,0:T(8,128)}, u32[]{:S(2)}, u32[]{:S(2)}) collective-permute-start(f32[256,768]{1,0:T(8,128)} %get-tuple-element.159.refs_14_), channel_id=1, source_target_pairs={{0,1}} | collective-permute-start | bytes 2359304 | tf_op jit(solution)/shard_map/ppermute | solution.py:481
  239.7 58.8 %collective-permute-start.44 = (f32[1024,1024]{1,0:T(8,128)S(1)}, f32[1024,1024]{1,0:T(8,128)}, u32[]{:S(2)}, u32[]{:S(2)}) collective-permute-start(f32[1024,1024]{1,0:T(8,128)S(1)} %shard_map.59), channel_id=1, source_target_pairs={{16,17},{21,20},{9,8},{12,13},{8,9},{13,12},{10,11},{15,14}} | collective-permute-start | bytes 12582920 | tf_op jit(solution)/shard_map/ppermute | solution.py:481
  260.7 7.2 %collective-permute-start.37 = (f32[256,1792]{1,0:T(8,128)}, f32[256,1792]{1,0:T(8,128)}, u32[]{:S(2)}, u32[]{:S(2)}) collective-permute-start(f32[256,1792]{1,0:T(8,128)} %shard_map.55), channel_id=1, source_target_pairs={{9,8},{11,10},{13,12},{15,14},{17,16},{19,18},{21,20},{23,22},{5,4}} | collective-permute-start | bytes 5505032 | tf_op jit(solution)/shard_map/ppermute | solution.py:481
  269.1 29.4 %collective-permute-start.43 = (f32[256,1536]{1,0:T(8,128)S(1)}, f32[256,1536]{1,0:T(8,128)S(1)}, u32[]{:S(2)}, u32[]{:S(2)}) collective-permute-start(f32[256,1536]{1,0:T(8,128)S(1)} %shard_map.58), channel_id=1, source_target_pairs={{9,8},{11,10},{13,12},{15,14},{17,16},{19,18},{21,20},{23,22},{5,4}} | collective-permute-start | bytes 4718600 | tf_op jit(solution)/shard_map/ppermute | solution.py:481
  299.3 21.7 %collective-permute-start.49 = (f32[256,1280]{1,0:T(8,128)S(1)}, f32[256,1280]{1,0:T(8,128)S(1)}, u32[]{:S(2)}, u32[]{:S(2)}) collective-permute-start(f32[256,1280]{1,0:T(8,128)S(1)} %shard_map.62), channel_id=1, source_target_pairs={{9,8},{11,10},{13,12},{15,14},{17,16},{19,18},{21,20},{23,22},{5,4}} | collective-permute-start | bytes 3932168 | tf_op jit(solution)/shard_map/ppermute | solution.py:481
  322.2 17.9 %collective-permute-start.53 = (f32[256,1024]{1,0:T(8,128)S(1)}, f32[256,1024]{1,0:T(8,128)S(1)}, u32[]{:S(2)}, u32[]{:S(2)}) collective-permute-start(f32[256,1024]{1,0:T(8,128)S(1)} %shard_map.65), channel_id=1, source_target_pairs={{9,8},{11,10},{13,12},{15,14},{17,16},{19,18},{21,20},{23,22},{5,4}} | collective-permute-start | bytes 3145736 | tf_op jit(solution)/shard_map/ppermute | solution.py:481
  340.8 14.5 %collective-permute-start.56 = (f32[256,768]{1,0:T(8,128)S(1)}, f32[256,768]{1,0:T(8,128)S(1)}, u32[]{:S(2)}, u32[]{:S(2)}) collective-permute-start(f32[256,768]{1,0:T(8,128)S(1)} %shard_map.67), channel_id=1, source_target_pairs={{9,8},{11,10},{13,12},{15,14},{17,16},{19,18},{21,20},{23,22},{5,4}} | collective-permute-start | bytes 2359304 | tf_op jit(solution)/shard_map/ppermute | solution.py:481
  356.1 11.8 %collective-permute-start.58 = (f32[256,512]{1,0:T(8,128)S(1)}, f32[256,512]{1,0:T(8,128)}, u32[]{:S(2)}, u32[]{:S(2)}) collective-permute-start(f32[256,512]{1,0:T(8,128)S(1)} %shard_map.69), channel_id=1, source_target_pairs={{9,8},{11,10},{13,12},{15,14},{17,16},{19,18},{21,20},{23,22},{5,4}} | collective-permute-start | bytes 1572872 | tf_op jit(solution)/shard_map/ppermute | solution.py:481
  368.6 9.5 %collective-permute-start.59 = (f32[256,256]{1,0:T(8,128)S(1)}, f32[256,256]{1,0:T(8,128)S(1)}, u32[]{:S(2)}, u32[]{:S(2)}) collective-permute-start(f32[256,256]{1,0:T(8,128)S(1)} %shard_map.70), channel_id=1, source_target_pairs={{9,8},{11,10},{13,12},{15,14},{17,16},{19,18},{21,20},{23,22},{5,4}} | collective-permute-start | bytes 786440 | tf_op jit(solution)/shard_map/ppermute | solution.py:481
  (83 other events, 2052.5 us)

commit v3 on v2

--- a/solution.py
+++ b/solution.py
@@ -8,9 +8,10 @@
 SUB = 8
 BASE = 128
 BLOCK = 256
-FIRST = 3
-SECOND = 6
-THIRD = 8
+STAGES = (6, 3)
+FIRST = 2
+SECOND = 5
+THIRD = 7
 NN = ((1,), (0,))
 NT = ((1,), (1,))
 TN = ((0,), (0,))
@@ -278,17 +279,20 @@
     count = 2 * steps
     sets = [refs[k * count : (k + 1) * count] for k in range(n_sets)]
     out_ref, p1_ref, z, t, spare, high, low, *fs, sems = refs[n_sets * count :]
-    role, transposed, which, col, edge = (meta_ref[k] for k in (0, 5, 6, 7, 8))
+    role, transposed, col, edge = (meta_ref[k] for k in (0, 5, 7, 8))
+    which = meta_ref[6], meta_ref[14]
     half = pl.ds(0, order), pl.ds(order, order)
     sources = [tiles_ref.at[0]] + list(raws)
 
     def load_pieces(pieces):
         for k in range(n_sets):
-
-            @pl.when(which == k)
-            def _():
-                for p in pieces:
-                    pltpu.make_async_copy(sets[k][p], fs[p], sems.at[8 + p]).start()
+            for step in range(2):
+
+                @pl.when(which[step] == k)
+                def _():
+                    for p in pieces:
+                        if p // steps == step:
+                            pltpu.make_async_copy(sets[k][p], fs[p], sems.at[8 + p]).start()
 
     def await_piece(p):
         pltpu.make_async_copy(sets[0][p], fs[p], sems.at[8 + p]).wait()
@@ -523,7 +527,7 @@
     workers = range(2, edge)
     routed = cols == 4
 
-    plan = [[[PASS] + [0] * 8 + [-1] * 5 for _ in range(cols)] for _ in range(rows)]
+    plan = [[[PASS] + [0] * 8 + [-1] * 5 + [0, -1, -1] for _ in range(cols)] for _ in range(rows)]
     for r in range(rows):
         for c in range(cols):
             plan[r][c][7] = c
@@ -537,8 +541,7 @@
         r1 = move(near, both_ways([((r, 0), (r, 1)) for r in (0,) + tuple(workers)]), cols)
         r2 = move(
             near,
-            [((r, c), (r, c + 2)) for r in workers for c in (0, 1)]
-            + [((1, 1), (0, 0)), ((edge, 1), (edge, 3))],
+            [((r, c), (r, c + 2)) for r in workers for c in (0, 1)],
             cols,
         )
         r3 = move(
@@ -548,7 +551,7 @@
             cols,
         )
         r4 = move(near, [((r, c), (r - 2, c)) for r in (4, 5) for c in (0, 1)], cols)
-        tile01 = r1
+        tile01, tile11 = r1, move(near, [((1, 1), (0, 0))], cols)
         for r in workers:
             plan[r][0][1:3] = [0, 1]
             plan[r][1][1:3] = [1, 0]
@@ -579,6 +582,11 @@
             plan[r][3][6] = 4
         for r in (1,) + tuple(workers):
             plan[r][0][6] = plan[r][2][6] = 5
+        plan[1][1][14] = 4
+        plan[0][0][15], plan[1][0][15], plan[1][0][16] = 0, 1, 0
+        for r in workers:
+            plan[r][0][14:17] = [1, -1, 1] if r < 4 else [2, -1, 2]
+            plan[r][1][14], plan[r][2][14], plan[r][3][14] = 4, 3, 5
         plan[0][1][9], plan[1][1][9] = 0, 1
         for r in workers:
             plan[r][1][10] = 0 if r < 4 else 1
@@ -601,17 +609,15 @@
     meta = meta.at[8].set(edge_live.astype(jnp.int32))
 
     pieces, copies, state = [], [], None
-    stages = 6 if routed else 0
-    late = []
-    for slot in range(count + stages):
-        arrived = []
+    drain = max(STAGES[0], steps + STAGES[1]) - steps if routed else 0
+    for slot in range(count + drain):
         if slot < count:
             step, local = divmod(slot, steps)
             n = order - local * BLOCK
             if slot == 0:
                 args = ("first", owner, n, 2 * n, tiles, tile01)
             elif local == 0:
-                args = ("schur", owner, n, n, r2 if routed else tile11, *pieces)
+                args = ("schur", owner, n, n, tile11, *pieces)
             else:
                 args = ("next", owner, n, n + (1 - step) * order, state)
             piece, state = factor_block(*args)
@@ -621,61 +627,67 @@
                 copies[-1].append(doubling(doubling(piece, "row", 0, rows), "col", 0, cols))
         if not routed:
             continue
-        for k in range(1, stages + 1):
-            p = slot - k
-            if not 0 <= p < count:
+        arrived = {}
+        for p in range(max(0, slot - max(STAGES)), min(slot, count)):
+            got, k = copies[p], slot - p
+            if k > STAGES[p // steps]:
                 continue
-            got = copies[p]
-            if k == 1:
-                got.append(move(pieces[p], [((0, 0), (0, 1))], cols))
+            if p < steps:
+                if k == 1:
+                    new = [move(pieces[p], [((0, 0), (0, 1))], cols)]
+                elif k == 2:
+                    new = [move(got[0], [((0, 1), (1, 1))], cols)]
+                elif k == 3:
+                    via = choose(meta[9:10], [got[0], got[1]])
+                    new = [move(via, [((r, 1), (r + 2, 1)) for r in (0, 1)], cols)]
+                elif k == 4:
+                    new = [move(got[2], [((r, 1), (r + 2, 1)) for r in (2, 3)], cols)]
+                elif k == 5:
+                    via = choose(meta[10:11], [got[2], got[3]])
+                    new = [move(via, [((r, 1), (r, 3)) for r in workers], cols)]
+                else:
+                    via = choose(meta[11:12], [got[1], got[2], got[3], got[4]])
+                    pairs = [((r, c), (r, c - 1)) for r in workers for c in (1, 3)]
+                    new = [move(via, pairs + [((1, 1), (1, 0))], cols)]
+            elif k == 1:
+                new = [move(pieces[p], [((0, 0), (1, 0))], cols)]
             elif k == 2:
-                got.append(move(got[0], [((0, 1), (1, 1))], cols))
-            elif k == 3:
-                via = choose(meta[9:10], [got[0], got[1]])
-                got.append(move(via, [((r, 1), (r + 2, 1)) for r in (0, 1)], cols))
-            elif k == 4:
-                got.append(move(got[2], [((r, 1), (r + 2, 1)) for r in (2, 3)], cols))
-            elif k == 5:
-                via = choose(meta[10:11], [got[2], got[3]])
-                got.append(move(via, [((r, 1), (r, 3)) for r in workers], cols))
+                via = choose(meta[15:16], [pieces[p], got[0]])
+                new = [
+                    move(via, [((r, 0), (r + far, 0)) for r in (0, 1)], cols) for far in (2, 4)
+                ]
             else:
-                via = choose(meta[11:12], [got[1], got[2], got[3], got[4]])
-                got.append(
-                    move(
-                        via,
-                        [((r, c), (r, c - 1)) for r in workers for c in (1, 3)]
-                        + [((1, 1), (1, 0))],
-                        cols,
-                    )
-                )
-            arrived.append(p)
+                via = choose(meta[16:17], got)
+                new = [
+                    move(via, [((r, 0), (r, c)) for r in workers] + also, cols)
+                    for c, also in ((2, []), (1, [((1, 0), (1, 1))]), (3, []))
+                ]
+            arrived[p] = new
         late = []
         if slot == FIRST:
-            late = [r2, r3, r4]
+            late = [r2, r3, r4, tile11]
         elif slot == SECOND:
-            late = [r5, r6, e1]
+            late = [r5, r6]
         elif slot == THIRD:
             late = [r7]
-        last = [copies[p][-1] for p in arrived]
         flowing = ([pieces[slot]] if slot < count else []) + ([] if state is None else [state])
-        flowing, last, late = lax.optimization_barrier((flowing, last, late))
+        flowing, arrived, late = lax.optimization_barrier((flowing, arrived, late))
         if slot < count:
             pieces[slot] = flowing[0]
         if state is not None:
             state = flowing[-1]
-        for p, value in zip(arrived, last):
-            copies[p][-1] = value
+        for p, new in arrived.items():
+            copies[p] += new
         if slot == FIRST:
-            r2, r3, r4 = late
+            r2, r3, r4, tile11 = late
             r5 = move(r2, both_ways([((r, 2), (r, 3)) for r in workers]), cols)
             r6 = move(
                 choose(meta[12:13], [r2, r3, r4]),
                 both_ways([((2, c), (3, c)) for c in range(4)] + [((4, c), (5, c)) for c in (2, 3)]),
                 cols,
             )
-            e1 = move(r2, [((edge, 3), (edge - 2, 2))], cols)
         elif slot == SECOND:
-            r5, r6, e1 = late
+            r5, r6 = late
             r7 = move(
                 choose(meta[13:14], [r3, r4, r6]),
                 [((4, 0), (4, 1)), ((5, 1), (5, 0)), ((2, 1), (2, 0)), ((3, 0), (3, 1))]
@@ -687,27 +699,36 @@
 
     if routed:
         sets = [pieces] + [[got[k] for got in copies] for k in (1, 2, 3, 4, 5)]
+        last_pieces = sets[3][steps:]
         raws = [r1, r2, r3, r4, r5, r6, r7]
     else:
         sets = [[got[0] for got in copies]]
-
-    def fetch(tile):
+        last_pieces = sets[0][steps:]
+
+    def fetch():
         if routed:
-            e2 = move(tile, [((edge - 2, 2), (edge - 4, 2))], cols)
-            e3 = move(tile + e2, [((r, 2), (r + 1, 2)) for r in (2, 4)], cols)
-            return tile + e2 + e3
-        total = jnp.zeros_like(tile)
+            e0 = move(near, [((edge, 1), (edge - 2, 2))], cols)
+            e1 = move(e0, [((edge - 2, 2), (edge - 4, 2))], cols)
+            e2 = move(e0 + e1, [((r, 2), (r + 1, 2)) for r in (2, 4)], cols)
+            return e0 + e1 + e2
+        total = jnp.zeros_like(near)
         for r in workers:
-            total = total + move(tile, [((edge, 1), (r, 2))], cols)
+            total = total + move(near, [((edge, 1), (r, 2))], cols)
         return total
 
     result, panel1 = finish(meta, tiles, raws, sets)
+    at_edge = edge_live & (row == edge)
+    flags = jnp.stack(
+        [
+            at_edge & (col >= 1),
+            (at_edge & (col <= 2)) | (edge_live & (row >= 2) & (row < edge) & (col == 2)),
+        ]
+    ).astype(jnp.int32)
 
     def edge_parts(args):
-        panel1, edge_tile, last_pieces = args
+        panel1, last_pieces = args
         far = tiles[1]
-        edge_tile = fetch(edge_tile)
-        last = eliminate_last(edge_tile, last_pieces)
+        last = eliminate_last(fetch(), last_pieces)
         column = far - dot(panel1, last, NT, lax.Precision.HIGH)
         sent = move(column, [((r, 2), (edge, r % cols)) for r in workers], cols).T
         solved = move(last, [((edge - 2, 2), (edge, 1)), ((edge - 1, 2), (edge, 2))], cols)
@@ -719,14 +740,7 @@
     def no_edge(args):
         return unset(near), unset(near)
 
-    parts = lax.cond(edge_live, edge_parts, no_edge, (panel1, e1 if routed else near, sets[-1][steps:]))
-    at_edge = edge_live & (row == edge)
-    flags = jnp.stack(
-        [
-            at_edge & (col >= 1),
-            (at_edge & (col <= 2)) | (edge_live & (row >= 2) & (row < edge) & (col == 2)),
-        ]
-    ).astype(jnp.int32)
+    parts = lax.cond(edge_live, edge_parts, no_edge, (panel1, last_pieces))
     return patch(flags, result, parts).reshape(kernel_tiles.shape)
 
 

time: 465 us -> 480 us (1.032)
  waiting for transfers between devices: 242 us -> 271 us
  starting transfers between devices: 87.5 us -> 73.5 us
  local copies, waits for them, and re-layouts: 14.2 us -> 22.1 us
  Pallas kernels: 103 us -> 96.9 us
    ppermute x56, waiting for transfers between devices: 242 us -> 271 us  [move(): return lax.ppermute(value, ('row', 'col'), flat)]
    ppermute x56, starting transfers between devices: 87.5 us -> 73.5 us  [move(): return lax.ppermute(value, ('row', 'col'), flat)]
    unnamed x102 -> x104, local copies, waits for them, and re-layouts: 7.4 us -> 15.3 us
    pallas_call x26 -> x22, Pallas kernels: 24.6 us -> 21.1 us  [choose(): pl.pallas_call(kernel, out_shape=shape(*options[0].shape), in_specs=[SMEM...]
  transfers between devices with their start and end apart: 56 -> 56, of which waited for: 8 -> 6; matrix products, arithmetic and copies ran while one was open for 0% -> 0% of each run, Pallas kernels for 6% -> 5%
where the time goes in v3:
time: 480 us; the launch traced here: 472 us
  waiting for transfers between devices  271 us (56%)
  Pallas kernels  96.9 us (20%)
  starting transfers between devices  73.5 us (15%)
  local copies, waits for them, and re-layouts  22.1 us (5%)
  loops' own time  5.89 us (1%)
    ppermute x56, waiting for transfers between devices, move(): return lax.ppermute(value, ('row', 'col'), flat)  271 us
    ppermute x56, starting transfers between devices, move(): return lax.ppermute(value, ('row', 'col'), flat)  73.5 us
    pallas_call x1, Pallas kernels, finish(): pl.pallas_call(lambda *refs: finish_kernel(len(raws), len(sets), *refs),...  70.9 us
    pallas_call x22, Pallas kernels, choose(): pl.pallas_call(kernel, out_shape=shape(*options[0].shape), in_specs=[SMEM...  21.1 us
    unnamed x104, local copies, waits for them, and re-layouts  15.3 us
  transfers between devices with their start and end apart: 56, of which 6 were waited for; matrix products, arithmetic and copies ran while one was open for 0% of the time, Pallas kernels for 5%

profile of v3, /device:TPU:12, one launch (start us, length us, event | category | flops | bytes accessed | tf_op | source)
XLA Modules:
  0.0 471.6 jit_solution(426296257421713436)
XLA Ops:
  0.0 4.9 %slice_bitcast_fusion.1 = f32[1024,1024]{1,0:T(8,128)} fusion(f32[1,1,2,1,1024,1024]{5,4,3,2,1,0:T(8,128)} %param.7), kind=kLoop, calls=%fused_computation.65 | loop fusion | bytes 8388608 | tf_op jit(solution)/shard_map/squeeze | solution.py:521
  4.9 2.7 collective-permute-start.5
  7.5 2.6 collective-permute-start.12
  10.3 2.2 collective-permute-start.6
  12.5 2.7 collective-permute-start.11
  15.2 2.6 collective-permute-start.10
  28.5 85.0 %collective-permute-done.9.refs_0_.refs_3_ = f32[1024,1024]{1,0:T(8,128)} collective-permute-done((f32[1024,1024]{1,0:T(8,128)}, f32[1024,1024]{1,0:T(8,128)}, u32[]{:S(2)}, u32[]{:S(2)}) %collective-permute-start.9) | collective-permute-done | bytes 4194336 | tf_op jit(solution)/shard_map/ppermute | solution.py:485
  117.6 4.8 %shard_map.47 = f32[1024,1024]{1,0:T(8,128)} custom-call(s32[1]{0:T(128)} %get-tuple-element.238.index_ref, f32[1024,1024]{1,0:T(8,128)} %collective-permute-done.9.refs_0_.refs_3_, f32[1024,1024]{1,0:T(8,128)} %collective-permute-done.10.refs_1_.refs_0_.refs_4_, f32[1024,1024]{1,0:T(8,128)} %collective-permute-done.11.refs_2_.refs_1_.refs_5_), custom_call_target="tpu_custom_call" | custom-call | tf_op jit(solution)/shard_map/pallas_call | solution.py:220
  122.3 3.4 collective-permute-start.26
  131.2 2.3 collective-permute-start.17
  135.3 2.8 shard_map.42
  138.9 2.0 collective-permute-start.20
  140.9 1.9 collective-permute-start.21
  144.3 72.4 %collective-permute-done.26.refs_2_.refs_7_ = f32[1024,1024]{1,0:T(8,128)} collective-permute-done((f32[1024,1024]{1,0:T(8,128)}, f32[1024,1024]{1,0:T(8,128)}, u32[]{:S(2)}, u32[]{:S(2)}) %collective-permute-start.26) | collective-permute-done | bytes 4194336 | tf_op jit(solution)/shard_map/ppermute | solution.py:485
  220.9 2.0 copy-done.21
  228.4 1.9 collective-permute-start.28
  231.1 3.2 shard_map.58
  234.4 3.7 collective-permute-start.43
  259.0 56.0 %collective-permute-done.37.refs_37_ = f32[256,1024]{1,0:T(8,128)} collective-permute-done((f32[256,1024]{1,0:T(8,128)}, f32[256,1024]{1,0:T(8,128)}, u32[]{:S(2)}, u32[]{:S(2)}) %collective-permute-start.37) | collective-permute-done | bytes 1048608 | tf_op jit(solution)/shard_map/ppermute | solution.py:485
  324.8 36.2 %collective-permute-done.46.refs_38_ = f32[256,768]{1,0:T(8,128)S(1)} collective-permute-done((f32[256,768]{1,0:T(8,128)S(1)}, f32[256,768]{1,0:T(8,128)S(1)}, u32[]{:S(2)}, u32[]{:S(2)}) %collective-permute-start.46) | collective-permute-done | bytes 786464 | tf_op jit(solution)/shard_map/ppermute | solution.py:485
  368.7 14.0 %collective-permute-done.53.refs_39_ = f32[256,512]{1,0:T(8,128)S(1)} collective-permute-done((f32[256,512]{1,0:T(8,128)S(1)}, f32[256,512]{1,0:T(8,128)S(1)}, u32[]{:S(2)}, u32[]{:S(2)}) %collective-permute-start.53) | collective-permute-done | bytes 524320 | tf_op jit(solution)/shard_map/ppermute | solution.py:485
  386.8 6.8 %collective-permute-done.58.refs_40_ = f32[256,256]{1,0:T(8,128)S(1)} collective-permute-done((f32[256,256]{1,0:T(8,128)S(1)}, f32[256,256]{1,0:T(8,128)S(1)}, u32[]{:S(2)}, u32[]{:S(2)}) %collective-permute-start.58) | collective-permute-done | bytes 262176 | tf_op jit(solution)/shard_map/ppermute | solution.py:485
  393.7 70.9 %shard_map.67 = (f32[2,1024,1024]{2,1,0:T(8,128)}, f32[1024,1024]{1,0:T(8,128)}) custom-call(s32[17]{0:T(128)} %copy-done.42, f32[2,1024,1024]{2,1,0:T(8,128)} %bitcast.38, f32[1024,1024]{1,0:T(8,128)} %collective-permute-done.5.refs_2_, f32[1024,1024]{1,0:T(8,128)} %collective-permute-done.9.refs_0_.refs_3_, ...), custom_call_target="tpu_custom_call" | custom-call | flops 60000002048 | bytes 67108864 | tf_op jit(solution)/shard_map/pallas_call | solution.py:470
  464.6 5.9 %conditional.1 = (f32[1024,1024]{1,0:T(8,128)}, f32[1024,1024]{1,0:T(8,128)}) conditional(s32[]{:T(128)} %convert_element_type.9, () %tuple.37, (s32[]{:T(128)}, f32[1024,1024]{1,0:T(8,128)}, f32[256,1024]{1,0:T(8,128)}, f32[256,768]{1,0:T(8,128)S(1)}, f32[256,512]{1,0:T(8,128)S(1)}, /*index=5*/f32[256,256]{1,0:T(8,128)S(1)}, ...), branch_computations={%region_0.0_spmd, %region_1.0_spmd} | conditional | flops 16927950848 | bytes 284199296 | solution.py:743
  (233 shorter events, 76.2 us)
Async XLA Ops:
  7.5 14.3 %collective-permute-start.12 = (f32[1024,1024]{1,0:T(8,128)}, f32[1024,1024]{1,0:T(8,128)}, u32[]{:S(2)}, u32[]{:S(2)}) collective-permute-start(f32[1024,1024]{1,0:T(8,128)} %slice_bitcast_fusion.1), channel_id=1, source_target_pairs={{5,0}} | collective-permute-start | bytes 12582920 | tf_op jit(solution)/shard_map/ppermute | solution.py:485
  12.5 16.0 %collective-permute-start.11 = (f32[1024,1024]{1,0:T(8,128)}, f32[1024,1024]{1,0:T(8,128)}, u32[]{:S(2)}, u32[]{:S(2)}) collective-permute-start(f32[1024,1024]{1,0:T(8,128)} %slice_bitcast_fusion.1), channel_id=1, source_target_pairs={{16,8},{17,9},{20,12},{21,13}} | collective-permute-start | bytes 12582920 | tf_op jit(solution)/shard_map/ppermute | solution.py:485
  17.8 95.6 %collective-permute-start.9 = (f32[1024,1024]{1,0:T(8,128)}, f32[1024,1024]{1,0:T(8,128)}, u32[]{:S(2)}, u32[]{:S(2)}) collective-permute-start(f32[1024,1024]{1,0:T(8,128)} %slice_bitcast_fusion.1), channel_id=1, source_target_pairs={{8,10},{9,11},{12,14},{13,15},{16,18},{17,19},{20,22},{21,23}} | collective-permute-start | bytes 12582920 | tf_op jit(solution)/shard_map/ppermute | solution.py:485
  21.1 92.4 %collective-permute-start.7 = (f32[256,2048]{1,0:T(8,128)}, f32[256,2048]{1,0:T(8,128)S(1)}, u32[]{:S(2)}, u32[]{:S(2)}) collective-permute-start(f32[256,2048]{1,0:T(8,128)} %collective-permute-done.6.refs_0_), channel_id=1, source_target_pairs={{1,5}} | collective-permute-start | bytes 6291464 | tf_op jit(solution)/shard_map/ppermute | solution.py:485
  21.9 91.6 %collective-permute-start.8 = (f32[256,1792]{1,0:T(8,128)}, f32[256,1792]{1,0:T(8,128)}, u32[]{:S(2)}, u32[]{:S(2)}) collective-permute-start(f32[256,1792]{1,0:T(8,128)} %get-tuple-element.135.refs_3_.refs_10_), channel_id=1, source_target_pairs={{0,1}} | collective-permute-start | bytes 5505032 | tf_op jit(solution)/shard_map/ppermute | solution.py:485
  114.2 13.7 %collective-permute-start.13 = (f32[256,2048]{1,0:T(8,128)S(1)}, f32[256,2048]{1,0:T(8,128)S(1)}, u32[]{:S(2)}, u32[]{:S(2)}) collective-permute-start(f32[256,2048]{1,0:T(8,128)S(1)} %shard_map.41), channel_id=1, source_target_pairs={{1,9},{5,13}} | collective-permute-start | bytes 6291464 | tf_op jit(solution)/shard_map/ppermute | solution.py:485
  122.3 94.3 %collective-permute-start.26 = (f32[1024,1024]{1,0:T(8,128)}, f32[1024,1024]{1,0:T(8,128)}, u32[]{:S(2)}, u32[]{:S(2)}) collective-permute-start(f32[1024,1024]{1,0:T(8,128)} %shard_map.47), channel_id=1, source_target_pairs={{8,12},{9,13},{10,14},{11,15},{18,22},{19,23},{12,8},{13,9},{14,10... | collective-permute-start | bytes 12582920 | tf_op jit(solution)/shard_map/ppermute | solution.py:485
  125.7 91.7 %collective-permute-start.25 = (f32[1024,1024]{1,0:T(8,128)}, f32[1024,1024]{1,0:T(8,128)}, u32[]{:S(2)}, u32[]{:S(2)}) collective-permute-start(f32[1024,1024]{1,0:T(8,128)} %collective-permute-done.9.refs_0_.refs_3_), channel_id=1, source_target_pairs={{10,11},{14,15},{18,19},{22,23},{11,10},{15,14},{19,18},{23,22}} | collective-permute-start | bytes 12582920 | tf_op jit(solution)/shard_map/ppermute | solution.py:485
  138.9 82.0 %collective-permute-start.20 = (f32[256,2048]{1,0:T(8,128)}, f32[256,2048]{1,0:T(8,128)}, u32[]{:S(2)}, u32[]{:S(2)}) collective-permute-start(f32[256,2048]{1,0:T(8,128)} %shard_map.45), channel_id=1, source_target_pairs={{9,11},{13,15},{17,19},{21,23}} | collective-permute-start | bytes 6291464 | tf_op jit(solution)/shard_map/ppermute | solution.py:485
  140.9 80.0 %collective-permute-start.21 = (f32[256,1792]{1,0:T(8,128)}, f32[256,1792]{1,0:T(8,128)}, u32[]{:S(2)}, u32[]{:S(2)}) collective-permute-start(f32[256,1792]{1,0:T(8,128)} %collective-permute-done.17.refs_0_.refs_1_.refs_26_), channel_id=1, source_target_pairs={{9,17},{13,21}} | collective-permute-start | bytes 5505032 | tf_op jit(solution)/shard_map/ppermute | solution.py:485
  143.5 77.3 %collective-permute-start.22 = (f32[256,1536]{1,0:T(8,128)}, f32[256,1536]{1,0:T(8,128)S(1)}, u32[]{:S(2)}, u32[]{:S(2)}) collective-permute-start(f32[256,1536]{1,0:T(8,128)} %shard_map.46), channel_id=1, source_target_pairs={{1,9},{5,13}} | collective-permute-start | bytes 4718600 | tf_op jit(solution)/shard_map/ppermute | solution.py:485
  225.0 13.8 %collective-permute-start.31 = (f32[256,1024]{1,0:T(8,128)S(1)}, f32[256,1024]{1,0:T(8,128)S(1)}, u32[]{:S(2)}, u32[]{:S(2)}) collective-permute-start(f32[256,1024]{1,0:T(8,128)S(1)} %shard_map.52), channel_id=1, source_target_pairs={{0,8},{4,12}} | collective-permute-start | bytes 3145736 | tf_op jit(solution)/shard_map/ppermute | solution.py:485
  226.5 16.2 %collective-permute-start.27 = (f32[256,2048]{1,0:T(8,128)}, f32[256,2048]{1,0:T(8,128)}, u32[]{:S(2)}, u32[]{:S(2)}) collective-permute-start(f32[256,2048]{1,0:T(8,128)} %shard_map.49), channel_id=1, source_target_pairs={{9,8},{11,10},{13,12},{15,14},{17,16},{19,18},{21,20},{23,22},{5,4}} | collective-permute-start | bytes 6291464 | tf_op jit(solution)/shard_map/ppermute | solution.py:485
  228.4 14.2 %collective-permute-start.28 = (f32[256,1792]{1,0:T(8,128)}, f32[256,1792]{1,0:T(8,128)}, u32[]{:S(2)}, u32[]{:S(2)}) collective-permute-start(f32[256,1792]{1,0:T(8,128)} %shard_map.50), channel_id=1, source_target_pairs={{9,11},{13,15},{17,19},{21,23}} | collective-permute-start | bytes 5505032 | tf_op jit(solution)/shard_map/ppermute | solution.py:485
  234.4 80.6 %collective-permute-start.43 = (f32[1024,1024]{1,0:T(8,128)S(1)}, f32[1024,1024]{1,0:T(8,128)}, u32[]{:S(2)}, u32[]{:S(2)}) collective-permute-start(f32[1024,1024]{1,0:T(8,128)S(1)} %shard_map.58), channel_id=1, source_target_pairs={{16,17},{21,20},{9,8},{12,13},{8,9},{13,12},{10,11},{15,14}} | collective-permute-start | bytes 12582920 | tf_op jit(solution)/shard_map/ppermute | solution.py:485
  250.7 64.2 %collective-permute-start.34 = (f32[256,1792]{1,0:T(8,128)}, f32[256,1792]{1,0:T(8,128)}, u32[]{:S(2)}, u32[]{:S(2)}) collective-permute-start(f32[256,1792]{1,0:T(8,128)} %shard_map.54), channel_id=1, source_target_pairs={{9,8},{11,10},{13,12},{15,14},{17,16},{19,18},{21,20},{23,22},{5,4}} | collective-permute-start | bytes 5505032 | tf_op jit(solution)/shard_map/ppermute | solution.py:485
  253.7 61.2 %collective-permute-start.35 = (f32[256,1536]{1,0:T(8,128)S(1)}, f32[256,1536]{1,0:T(8,128)}, u32[]{:S(2)}, u32[]{:S(2)}) collective-permute-start(f32[256,1536]{1,0:T(8,128)S(1)} %shard_map.55), channel_id=1, source_target_pairs={{9,11},{13,15},{17,19},{21,23}} | collective-permute-start | bytes 4718600 | tf_op jit(solution)/shard_map/ppermute | solution.py:485
  255.6 59.4 %collective-permute-start.36 = (f32[256,1280]{1,0:T(8,128)S(1)}, f32[256,1280]{1,0:T(8,128)S(1)}, u32[]{:S(2)}, u32[]{:S(2)}) collective-permute-start(f32[256,1280]{1,0:T(8,128)S(1)} %collective-permute-done.30.refs_0_.refs_1_.refs_28_), channel_id=1, source_target_pairs={{9,17},{13,21}} | collective-permute-start | bytes 3932168 | tf_op jit(solution)/shard_map/ppermute | solution.py:485
  257.6 57.4 %collective-permute-start.37 = (f32[256,1024]{1,0:T(8,128)}, f32[256,1024]{1,0:T(8,128)}, u32[]{:S(2)}, u32[]{:S(2)}) collective-permute-start(f32[256,1024]{1,0:T(8,128)} %shard_map.56), channel_id=1, source_target_pairs={{8,10},{12,14},{16,18},{20,22}} | collective-permute-start | bytes 3145736 | tf_op jit(solution)/shard_map/ppermute | solution.py:485
  315.7 45.3 %collective-permute-start.44 = (f32[256,1536]{1,0:T(8,128)S(1)}, f32[256,1536]{1,0:T(8,128)S(1)}, u32[]{:S(2)}, u32[]{:S(2)}) collective-permute-start(f32[256,1536]{1,0:T(8,128)S(1)} %shard_map.59), channel_id=1, source_target_pairs={{9,8},{11,10},{13,12},{15,14},{17,16},{19,18},{21,20},{23,22},{5,4}} | collective-permute-start | bytes 4718600 | tf_op jit(solution)/shard_map/ppermute | solution.py:485
  319.9 41.1 %collective-permute-start.45 = (f32[256,1280]{1,0:T(8,128)S(1)}, f32[256,1280]{1,0:T(8,128)S(1)}, u32[]{:S(2)}, u32[]{:S(2)}) collective-permute-start(f32[256,1280]{1,0:T(8,128)S(1)} %shard_map.60), channel_id=1, source_target_pairs={{9,11},{13,15},{17,19},{21,23}} | collective-permute-start | bytes 3932168 | tf_op jit(solution)/shard_map/ppermute | solution.py:485
  323.5 37.6 %collective-permute-start.46 = (f32[256,768]{1,0:T(8,128)S(1)}, f32[256,768]{1,0:T(8,128)S(1)}, u32[]{:S(2)}, u32[]{:S(2)}) collective-permute-start(f32[256,768]{1,0:T(8,128)S(1)} %shard_map.61), channel_id=1, source_target_pairs={{8,10},{12,14},{16,18},{20,22}} | collective-permute-start | bytes 2359304 | tf_op jit(solution)/shard_map/ppermute | solution.py:485
  361.8 21.0 %collective-permute-start.52 = (f32[256,1280]{1,0:T(8,128)S(1)}, f32[256,1280]{1,0:T(8,128)S(1)}, u32[]{:S(2)}, u32[]{:S(2)}) collective-permute-start(f32[256,1280]{1,0:T(8,128)S(1)} %shard_map.63), channel_id=1, source_target_pairs={{9,8},{11,10},{13,12},{15,14},{17,16},{19,18},{21,20},{23,22},{5,4}} | collective-permute-start | bytes 3932168 | tf_op jit(solution)/shard_map/ppermute | solution.py:485
  366.7 16.1 %collective-permute-start.53 = (f32[256,512]{1,0:T(8,128)S(1)}, f32[256,512]{1,0:T(8,128)S(1)}, u32[]{:S(2)}, u32[]{:S(2)}) collective-permute-start(f32[256,512]{1,0:T(8,128)S(1)} %shard_map.64), channel_id=1, source_target_pairs={{8,10},{12,14},{16,18},{20,22}} | collective-permute-start | bytes 1572872 | tf_op jit(solution)/shard_map/ppermute | solution.py:485
  (84 other events, 1880.8 us)

commit v4 on v3

--- a/solution.py
+++ b/solution.py
@@ -10,8 +10,8 @@
 BLOCK = 256
 STAGES = (6, 3)
 FIRST = 2
-SECOND = 5
-THIRD = 7
+SECOND = (4, 6)
+THIRD = 8
 NN = ((1,), (0,))
 NT = ((1,), (1,))
 TN = ((0,), (0,))
@@ -200,16 +200,27 @@
     return out if n > BLOCK else (out[0], None)
 
 
-def choose(index, options):
+def choose(index, options, rows=None):
+    options = [o if isinstance(o, list) else [o] for o in options]
+    total, width = sum(a.shape[0] for a in options[0]), options[0][0].shape[1]
+    start, size = rows or (0, total)
+
     def kernel(index_ref, *refs):
         *bufs, out_ref, held, sem = refs
-        for k, buf in enumerate(bufs):
+        for k, option in enumerate(options):
+            parts, bufs = bufs[: len(option)], bufs[len(option) :]
 
             @pl.when(index_ref[0] == k)
             def _():
-                copy = pltpu.make_async_copy(buf, held, sem)
-                copy.start()
-                copy.wait()
+                at = 0
+                for part in parts:
+                    high = min(part.shape[0], size)
+                    copy = pltpu.make_async_copy(
+                        part.at[pl.ds(start if rows else 0, high)], held.at[pl.ds(at, high)], sem
+                    )
+                    copy.start()
+                    copy.wait()
+                    at += high
 
         @pl.when(index_ref[0] >= 0)
         def _():
@@ -217,14 +228,15 @@
             copy.start()
             copy.wait()
 
+    flat = [a for option in options for a in option]
     return pl.pallas_call(
         kernel,
-        out_shape=shape(*options[0].shape),
-        in_specs=[SMEM] + [ANY] * len(options),
+        out_shape=shape(size, width),
+        in_specs=[SMEM] + [ANY] * len(flat),
         out_specs=ANY,
-        scratch_shapes=[pltpu.VMEM(options[0].shape, F32), DMA(())],
+        scratch_shapes=[pltpu.VMEM((size, width), F32), DMA(())],
         compiler_params=params(8),
-    )(index, *options)
+    )(index, *flat)
 
 
 def unset(like):
@@ -282,7 +294,12 @@
     role, transposed, col, edge = (meta_ref[k] for k in (0, 5, 7, 8))
     which = meta_ref[6], meta_ref[14]
     half = pl.ds(0, order), pl.ds(order, order)
-    sources = [tiles_ref.at[0]] + list(raws)
+    sources = [[tiles_ref.at[0]]]
+    for ref in raws:
+        if ref.shape[0] < order and len(sources[-1]) == 1 and sources[-1][0].shape[0] < order:
+            sources[-1].append(ref)
+        else:
+            sources.append([ref])
 
     def load_pieces(pieces):
         for k in range(n_sets):
@@ -361,7 +378,11 @@
 
                 @pl.when(meta_ref[1 + s] == k)
                 def _():
-                    pltpu.make_async_copy(source, place, sems.at[s]).start()
+                    high = order // len(source)
+                    for h, part in enumerate(source):
+                        rows = pl.ds((s // 2) * order + h * high, high)
+                        target = z.at[rows, half[s % 2]]
+                        pltpu.make_async_copy(part, target, sems.at[s]).start()
 
         load_pieces(range(count))
         for slot, taken in ((1, col < 2), (0, col >= 2)):
@@ -375,7 +396,7 @@
             move_out(tiles_ref.at[1], spare, 5)
 
         for s, place in enumerate(places):
-            pltpu.make_async_copy(sources[1], place, sems.at[s]).wait()
+            pltpu.make_async_copy(sources[1][0], place, sems.at[s]).wait()
 
         @pl.when(transposed == 1)
         def _():
@@ -578,8 +599,7 @@
                 plan[r][c][5] = 1
         plan[1][1][6] = 1
         for r in workers:
-            plan[r][1][6] = plan[r][3][6] = 2 if r < 4 else 3
-            plan[r][3][6] = 4
+            plan[r][1][6] = plan[r][3][6] = 3 if r < 4 else 4
         for r in (1,) + tuple(workers):
             plan[r][0][6] = plan[r][2][6] = 5
         plan[1][1][14] = 4
@@ -588,11 +608,10 @@
             plan[r][0][14:17] = [1, -1, 1] if r < 4 else [2, -1, 2]
             plan[r][1][14], plan[r][2][14], plan[r][3][14] = 4, 3, 5
         plan[0][1][9], plan[1][1][9] = 0, 1
+        plan[0][1][10:12], plan[1][1][10:12] = [0, -1], [1, 0]
+        plan[0][3][10], plan[1][3][10] = 2, 2
         for r in workers:
-            plan[r][1][10] = 0 if r < 4 else 1
-            plan[r][1][11] = 1 if r < 4 else 2
-            plan[r][3][11] = 3
-        plan[1][1][11] = 0
+            plan[r][1][11] = plan[r][3][11] = 1 if r < 4 else 2
     else:
         mine = jnp.where(col < 2, tiles[1], near)
         left0 = doubling(near, "col", 0, cols)
@@ -638,15 +657,17 @@
                 elif k == 2:
                     new = [move(got[0], [((0, 1), (1, 1))], cols)]
                 elif k == 3:
-                    via = choose(meta[9:10], [got[0], got[1]])
-                    new = [move(via, [((r, 1), (r + 2, 1)) for r in (0, 1)], cols)]
+                    via = choose(meta[9:10], got)
+                    new = [move(via, [((r, 1), (r, 3)) for r in (0, 1)], cols)]
                 elif k == 4:
-                    new = [move(got[2], [((r, 1), (r + 2, 1)) for r in (2, 3)], cols)]
+                    via = choose(meta[10:11], got)
+                    pairs = [((r, c), (r + 2, c)) for r in (0, 1) for c in (1, 3)]
+                    new = [move(via, pairs, cols)]
                 elif k == 5:
-                    via = choose(meta[10:11], [got[2], got[3]])
-                    new = [move(via, [((r, 1), (r, 3)) for r in workers], cols)]
+                    pairs = [((r, c), (r + 2, c)) for r in (2, 3) for c in (1, 3)]
+                    new = [move(got[3], pairs, cols)]
                 else:
-                    via = choose(meta[11:12], [got[1], got[2], got[3], got[4]])
+                    via = choose(meta[11:12], [got[1], got[3], got[4]])
                     pairs = [((r, c), (r, c - 1)) for r in workers for c in (1, 3)]
                     new = [move(via, pairs + [((1, 1), (1, 0))], cols)]
             elif k == 1:
@@ -666,8 +687,10 @@
         late = []
         if slot == FIRST:
             late = [r2, r3, r4, tile11]
-        elif slot == SECOND:
-            late = [r5, r6]
+        elif slot == SECOND[0]:
+            late = [r5, r6[0]]
+        elif slot == SECOND[1]:
+            late = [r6[1]]
         elif slot == THIRD:
             late = [r7]
         flowing = ([pieces[slot]] if slot < count else []) + ([] if state is None else [state])
@@ -681,13 +704,16 @@
         if slot == FIRST:
             r2, r3, r4, tile11 = late
             r5 = move(r2, both_ways([((r, 2), (r, 3)) for r in workers]), cols)
-            r6 = move(
-                choose(meta[12:13], [r2, r3, r4]),
-                both_ways([((2, c), (3, c)) for c in range(4)] + [((4, c), (5, c)) for c in (2, 3)]),
-                cols,
+            across = both_ways(
+                [((2, c), (3, c)) for c in range(4)] + [((4, c), (5, c)) for c in (2, 3)]
             )
-        elif slot == SECOND:
-            r5, r6 = late
+            high = order // 2
+            r6 = [move(choose(meta[12:13], [r2, r3, r4], (0, high)), across, cols), None]
+        elif slot == SECOND[0]:
+            r5, r6[0] = late
+            r6[1] = move(choose(meta[12:13], [r2, r3, r4], (high, high)), across, cols)
+        elif slot == SECOND[1]:
+            (r6[1],) = late
             r7 = move(
                 choose(meta[13:14], [r3, r4, r6]),
                 [((4, 0), (4, 1)), ((5, 1), (5, 0)), ((2, 1), (2, 0)), ((3, 0), (3, 1))]
@@ -700,7 +726,7 @@
     if routed:
         sets = [pieces] + [[got[k] for got in copies] for k in (1, 2, 3, 4, 5)]
         last_pieces = sets[3][steps:]
-        raws = [r1, r2, r3, r4, r5, r6, r7]
+        raws = [r1, r2, r3, r4, r5, *r6, r7]
     else:
         sets = [[got[0] for got in copies]]
         last_pieces = sets[0][steps:]

time: 480 us -> 458 us (0.954)
  waiting for transfers between devices: 271 us -> 232 us
  starting transfers between devices: 73.5 us -> 96.1 us
  local copies, waits for them, and re-layouts: 22.1 us -> 16.4 us
    ppermute x56 -> x57, waiting for transfers between devices: 271 us -> 232 us  [move(): return lax.ppermute(value, ('row', 'col'), flat)]
    ppermute x56 -> x57, starting transfers between devices: 73.5 us -> 96.1 us  [move(): return lax.ppermute(value, ('row', 'col'), flat)]
    unnamed x104 -> x88, local copies, waits for them, and re-layouts: 15.3 us -> 9.5 us
    pallas_call x22 -> x23, Pallas kernels: 21.1 us -> 23.1 us  [choose(): pl.pallas_call(kernel, out_shape=shape(size, width), in_specs=[SMEM] + [A...]
  transfers between devices with their start and end apart: 56 -> 57, of which waited for: 6 -> 7; matrix products, arithmetic and copies ran while one was open for 0% -> 0% of each run, Pallas kernels for 5% -> 5%
where the time goes in v4:
time: 458 us; the launch traced here: 450 us
  waiting for transfers between devices  232 us (51%)
  Pallas kernels  96.7 us (21%)
  starting transfers between devices  96.1 us (21%)
  local copies, waits for them, and re-layouts  16.4 us (4%)
  loops' own time  5.92 us (1%)
    ppermute x57, waiting for transfers between devices, move(): return lax.ppermute(value, ('row', 'col'), flat)  232 us
    ppermute x57, starting transfers between devices, move(): return lax.ppermute(value, ('row', 'col'), flat)  96.1 us
    pallas_call x1, Pallas kernels, finish(): pl.pallas_call(lambda *refs: finish_kernel(len(raws), len(sets), *refs),...  71 us
    pallas_call x23, Pallas kernels, choose(): pl.pallas_call(kernel, out_shape=shape(size, width), in_specs=[SMEM] + [A...  23.1 us
    unnamed x88, local copies, waits for them, and re-layouts  9.5 us
  transfers between devices with their start and end apart: 57, of which 7 were waited for; matrix products, arithmetic and copies ran while one was open for 0% of the time, Pallas kernels for 5%

profile of v4, /device:TPU:12, one launch (start us, length us, event | category | flops | bytes accessed | tf_op | source)
XLA Modules:
  0.0 449.6 jit_solution(3010991782029864391)
XLA Ops:
  0.0 4.8 %slice_bitcast_fusion.1 = f32[1024,1024]{1,0:T(8,128)} fusion(f32[1,1,2,1,1024,1024]{5,4,3,2,1,0:T(8,128)} %param.7), kind=kLoop, calls=%fused_computation.65 | loop fusion | bytes 8388608 | tf_op jit(solution)/shard_map/squeeze | solution.py:542
  4.8 2.7 collective-permute-start.5
  7.5 2.7 collective-permute-start.12
  10.3 2.1 collective-permute-start.6
  12.4 2.7 collective-permute-start.11
  15.1 2.6 collective-permute-start.10
  28.8 84.5 %collective-permute-done.9.refs_0_.refs_3_ = f32[1024,1024]{1,0:T(8,128)} collective-permute-done((f32[1024,1024]{1,0:T(8,128)}, f32[1024,1024]{1,0:T(8,128)}, u32[]{:S(2)}, u32[]{:S(2)}) %collective-permute-start.9) | collective-permute-done | bytes 4194336 | tf_op jit(solution)/shard_map/ppermute | solution.py:506
  119.4 3.6 shard_map.45
  123.1 3.4 collective-permute-start.21
  127.3 2.1 collective-permute-start.16
  133.0 40.2 %collective-permute-done.21.refs_2_.refs_7_ = f32[512,1024]{1,0:T(8,128)S(1)} collective-permute-done((f32[512,1024]{1,0:T(8,128)}, f32[512,1024]{1,0:T(8,128)S(1)}, u32[]{:S(2)}, u32[]{:S(2)}) %collective-permute-start.21) | collective-permute-done | bytes 2097184 | tf_op jit(solution)/shard_map/ppermute | solution.py:506
  176.6 2.0 collective-permute-start.22
  181.9 2.0 collective-permute-start.24
  183.9 3.6 shard_map.54
  187.5 3.4 collective-permute-start.34
  198.8 35.4 %collective-permute-done.34.refs_3_.refs_8_ = f32[512,1024]{1,0:T(8,128)} collective-permute-done((f32[512,1024]{1,0:T(8,128)}, f32[512,1024]{1,0:T(8,128)}, u32[]{:S(2)}, u32[]{:S(2)}) %collective-permute-start.34) | collective-permute-done | bytes 2097184 | tf_op jit(solution)/shard_map/ppermute | solution.py:506
  247.1 2.6 shard_map.63
  249.7 20.5 %collective-permute-start.52 = (f32[1024,1024]{1,0:T(8,128)S(1)}, f32[1024,1024]{1,0:T(8,128)}, u32[]{:S(2)}, u32[]{:S(2)}) collective-permute-start(f32[1024,1024]{1,0:T(8,128)S(1)} %shard_map.63), channel_id=1, source_target_pairs={{16,17},{21,20},{9,8},{12,13},{8,9},{13,12},{10,11},{15,14}} | collective-permute-start | bytes 12582920 | tf_op jit(solution)/shard_map/ppermute | solution.py:506
  277.9 30.2 %collective-permute-done.38.refs_38_ = f32[256,1024]{1,0:T(8,128)} collective-permute-done((f32[256,1024]{1,0:T(8,128)S(1)}, f32[256,1024]{1,0:T(8,128)}, u32[]{:S(2)}, u32[]{:S(2)}) %collective-permute-start.38) | collective-permute-done | bytes 1048608 | tf_op jit(solution)/shard_map/ppermute | solution.py:506
  318.3 20.5 %collective-permute-done.46.refs_39_ = f32[256,768]{1,0:T(8,128)S(1)} collective-permute-done((f32[256,768]{1,0:T(8,128)S(1)}, f32[256,768]{1,0:T(8,128)S(1)}, u32[]{:S(2)}, u32[]{:S(2)}) %collective-permute-start.46) | collective-permute-done | bytes 786464 | tf_op jit(solution)/shard_map/ppermute | solution.py:506
  346.4 14.0 %collective-permute-done.54.refs_40_ = f32[256,512]{1,0:T(8,128)S(1)} collective-permute-done((f32[256,512]{1,0:T(8,128)S(1)}, f32[256,512]{1,0:T(8,128)S(1)}, u32[]{:S(2)}, u32[]{:S(2)}) %collective-permute-start.54) | collective-permute-done | bytes 524320 | tf_op jit(solution)/shard_map/ppermute | solution.py:506
  364.6 6.8 %collective-permute-done.59.refs_41_ = f32[256,256]{1,0:T(8,128)S(1)} collective-permute-done((f32[256,256]{1,0:T(8,128)S(1)}, f32[256,256]{1,0:T(8,128)S(1)}, u32[]{:S(2)}, u32[]{:S(2)}) %collective-permute-start.59) | collective-permute-done | bytes 262176 | tf_op jit(solution)/shard_map/ppermute | solution.py:506
  371.5 71.0 %shard_map.68 = (f32[2,1024,1024]{2,1,0:T(8,128)}, f32[1024,1024]{1,0:T(8,128)}) custom-call(s32[17]{0:T(128)} %copy-done.34, f32[2,1024,1024]{2,1,0:T(8,128)} %bitcast.38, f32[1024,1024]{1,0:T(8,128)} %collective-permute-done.5.refs_2_, f32[1024,1024]{1,0:T(8,128)} %collective-permute-done.9.refs_0_.refs_3_, ...), custom_call_target="tpu_custom_call" | custom-call | flops 60000002048 | bytes 67108864 | tf_op jit(solution)/shard_map/pallas_call | solution.py:491
  442.6 5.9 %conditional.1 = (f32[1024,1024]{1,0:T(8,128)}, f32[1024,1024]{1,0:T(8,128)}) conditional(s32[]{:T(128)} %convert_element_type.9, () %tuple.37, (s32[]{:T(128)}, f32[1024,1024]{1,0:T(8,128)}, f32[256,1024]{1,0:T(8,128)}, f32[256,768]{1,0:T(8,128)S(1)}, f32[256,512]{1,0:T(8,128)S(1)}, /*index=5*/f32[256,256]{1,0:T(8,128)S(1)}, ...), branch_computations={%region_0.0_spmd, %region_1.0_spmd} | conditional | flops 16927950848 | bytes 284199296 | solution.py:769
  (220 shorter events, 77.6 us)
Async XLA Ops:
  17.7 95.6 %collective-permute-start.9 = (f32[1024,1024]{1,0:T(8,128)}, f32[1024,1024]{1,0:T(8,128)}, u32[]{:S(2)}, u32[]{:S(2)}) collective-permute-start(f32[1024,1024]{1,0:T(8,128)} %slice_bitcast_fusion.1), channel_id=1, source_target_pairs={{8,10},{9,11},{12,14},{13,15},{16,18},{17,19},{20,22},{21,23}} | collective-permute-start | bytes 12582920 | tf_op jit(solution)/shard_map/ppermute | solution.py:506
  21.0 92.3 %collective-permute-start.7 = (f32[256,2048]{1,0:T(8,128)}, f32[256,2048]{1,0:T(8,128)S(1)}, u32[]{:S(2)}, u32[]{:S(2)}) collective-permute-start(f32[256,2048]{1,0:T(8,128)} %collective-permute-done.6.refs_0_), channel_id=1, source_target_pairs={{1,5}} | collective-permute-start | bytes 6291464 | tf_op jit(solution)/shard_map/ppermute | solution.py:506
  21.8 91.5 %collective-permute-start.8 = (f32[256,1792]{1,0:T(8,128)}, f32[256,1792]{1,0:T(8,128)}, u32[]{:S(2)}, u32[]{:S(2)}) collective-permute-start(f32[256,1792]{1,0:T(8,128)} %get-tuple-element.136.refs_3_.refs_11_), channel_id=1, source_target_pairs={{0,1}} | collective-permute-start | bytes 5505032 | tf_op jit(solution)/shard_map/ppermute | solution.py:506
  116.0 59.9 %collective-permute-start.20 = (f32[1024,1024]{1,0:T(8,128)}, f32[1024,1024]{1,0:T(8,128)}, u32[]{:S(2)}, u32[]{:S(2)}) collective-permute-start(f32[1024,1024]{1,0:T(8,128)} %collective-permute-done.9.refs_0_.refs_3_), channel_id=1, source_target_pairs={{10,11},{14,15},{18,19},{22,23},{11,10},{15,14},{19,18},{23,22}} | collective-permute-start | bytes 12582920 | tf_op jit(solution)/shard_map/ppermute | solution.py:506
  123.1 50.1 %collective-permute-start.21 = (f32[512,1024]{1,0:T(8,128)}, f32[512,1024]{1,0:T(8,128)S(1)}, u32[]{:S(2)}, u32[]{:S(2)}) collective-permute-start(f32[512,1024]{1,0:T(8,128)} %shard_map.45), channel_id=1, source_target_pairs={{8,12},{9,13},{10,14},{11,15},{18,22},{19,23},{12,8},{13,9},{14,10... | collective-permute-start | bytes 6291464 | tf_op jit(solution)/shard_map/ppermute | solution.py:506
  127.3 48.5 %collective-permute-start.16 = (f32[256,2048]{1,0:T(8,128)}, f32[256,2048]{1,0:T(8,128)}, u32[]{:S(2)}, u32[]{:S(2)}) collective-permute-start(f32[256,2048]{1,0:T(8,128)} %shard_map.43), channel_id=1, source_target_pairs={{1,9},{3,11},{5,13},{7,15}} | collective-permute-start | bytes 6291464 | tf_op jit(solution)/shard_map/ppermute | solution.py:506
  130.1 45.7 %collective-permute-start.17 = (f32[256,1792]{1,0:T(8,128)}, f32[256,1792]{1,0:T(8,128)}, u32[]{:S(2)}, u32[]{:S(2)}) collective-permute-start(f32[256,1792]{1,0:T(8,128)} %shard_map.44), channel_id=1, source_target_pairs={{1,3},{5,7}} | collective-permute-start | bytes 5505032 | tf_op jit(solution)/shard_map/ppermute | solution.py:506
  132.1 43.7 %collective-permute-start.18 = (f32[256,1536]{1,0:T(8,128)S(1)}, f32[256,1536]{1,0:T(8,128)S(1)}, u32[]{:S(2)}, u32[]{:S(2)}) collective-permute-start(f32[256,1536]{1,0:T(8,128)S(1)} %collective-permute-done.15.refs_0_), channel_id=1, source_target_pairs={{1,5}} | collective-permute-start | bytes 4718600 | tf_op jit(solution)/shard_map/ppermute | solution.py:506
  187.5 46.7 %collective-permute-start.34 = (f32[512,1024]{1,0:T(8,128)}, f32[512,1024]{1,0:T(8,128)}, u32[]{:S(2)}, u32[]{:S(2)}) collective-permute-start(f32[512,1024]{1,0:T(8,128)} %shard_map.54), channel_id=1, source_target_pairs={{8,12},{9,13},{10,14},{11,15},{18,22},{19,23},{12,8},{13,9},{14,10... | collective-permute-start | bytes 6291464 | tf_op jit(solution)/shard_map/ppermute | solution.py:506
  192.5 46.0 %collective-permute-start.32 = (f32[256,1024]{1,0:T(8,128)}, f32[256,1024]{1,0:T(8,128)S(1)}, u32[]{:S(2)}, u32[]{:S(2)}) collective-permute-start(f32[256,1024]{1,0:T(8,128)} %shard_map.53), channel_id=1, source_target_pairs={{0,16},{4,20}} | collective-permute-start | bytes 3145736 | tf_op jit(solution)/shard_map/ppermute | solution.py:506
  193.3 43.5 %collective-permute-start.33 = (f32[256,768]{1,0:T(8,128)}, f32[256,768]{1,0:T(8,128)S(1)}, u32[]{:S(2)}, u32[]{:S(2)}) collective-permute-start(f32[256,768]{1,0:T(8,128)} %get-tuple-element.169.refs_0_.refs_15_), channel_id=1, source_target_pairs={{0,4}} | collective-permute-start | bytes 2359304 | tf_op jit(solution)/shard_map/ppermute | solution.py:506
  194.7 46.6 %collective-permute-start.27 = (f32[256,2048]{1,0:T(8,128)S(1)}, f32[256,2048]{1,0:T(8,128)}, u32[]{:S(2)}, u32[]{:S(2)}) collective-permute-start(f32[256,2048]{1,0:T(8,128)S(1)} %shard_map.50), channel_id=1, source_target_pairs={{9,8},{11,10},{13,12},{15,14},{17,16},{19,18},{21,20},{23,22},{5,4}} | collective-permute-start | bytes 6291464 | tf_op jit(solution)/shard_map/ppermute | solution.py:506
  196.1 45.2 %collective-permute-start.28 = (f32[256,1792]{1,0:T(8,128)}, f32[256,1792]{1,0:T(8,128)}, u32[]{:S(2)}, u32[]{:S(2)}) collective-permute-start(f32[256,1792]{1,0:T(8,128)} %collective-permute-done.23.refs_1_.refs_35_), channel_id=1, source_target_pairs={{9,17},{11,19},{13,21},{15,23}} | collective-permute-start | bytes 5505032 | tf_op jit(solution)/shard_map/ppermute | solution.py:506
  241.3 28.8 %collective-permute-start.43 = (f32[256,512]{1,0:T(8,128)}, f32[256,512]{1,0:T(8,128)S(1)}, u32[]{:S(2)}, u32[]{:S(2)}) collective-permute-start(f32[256,512]{1,0:T(8,128)} %get-tuple-element.178.refs_0_.refs_16_), channel_id=1, source_target_pairs={{0,4}} | collective-permute-start | bytes 1572872 | tf_op jit(solution)/shard_map/ppermute | solution.py:506
  242.8 28.8 %collective-permute-start.42 = (f32[256,768]{1,0:T(8,128)S(1)}, f32[256,768]{1,0:T(8,128)S(1)}, u32[]{:S(2)}, u32[]{:S(2)}) collective-permute-start(f32[256,768]{1,0:T(8,128)S(1)} %shard_map.59), channel_id=1, source_target_pairs={{0,16},{4,20}} | collective-permute-start | bytes 2359304 | tf_op jit(solution)/shard_map/ppermute | solution.py:506
  243.7 29.4 %collective-permute-start.41 = (f32[256,768]{1,0:T(8,128)S(1)}, f32[256,768]{1,0:T(8,128)S(1)}, u32[]{:S(2)}, u32[]{:S(2)}) collective-permute-start(f32[256,768]{1,0:T(8,128)S(1)} %shard_map.59), channel_id=1, source_target_pairs={{0,8},{4,12}} | collective-permute-start | bytes 2359304 | tf_op jit(solution)/shard_map/ppermute | solution.py:506
  246.3 28.2 %collective-permute-start.40 = (f32[256,1024]{1,0:T(8,128)S(1)}, f32[256,1024]{1,0:T(8,128)S(1)}, u32[]{:S(2)}, u32[]{:S(2)}) collective-permute-start(f32[256,1024]{1,0:T(8,128)S(1)} %shard_map.58), channel_id=1, source_target_pairs={{8,11},{12,15},{16,19},{20,23}} | collective-permute-start | bytes 3145736 | tf_op jit(solution)/shard_map/ppermute | solution.py:506
  249.7 89.2 %collective-permute-start.52 = (f32[1024,1024]{1,0:T(8,128)S(1)}, f32[1024,1024]{1,0:T(8,128)}, u32[]{:S(2)}, u32[]{:S(2)}) collective-permute-start(f32[1024,1024]{1,0:T(8,128)S(1)} %shard_map.63), channel_id=1, source_target_pairs={{16,17},{21,20},{9,8},{12,13},{8,9},{13,12},{10,11},{15,14}} | collective-permute-start | bytes 12582920 | tf_op jit(solution)/shard_map/ppermute | solution.py:506
  271.6 36.5 %collective-permute-start.35 = (f32[256,1792]{1,0:T(8,128)S(1)}, f32[256,1792]{1,0:T(8,128)}, u32[]{:S(2)}, u32[]{:S(2)}) collective-permute-start(f32[256,1792]{1,0:T(8,128)S(1)} %shard_map.56), channel_id=1, source_target_pairs={{9,8},{11,10},{13,12},{15,14},{17,16},{19,18},{21,20},{23,22},{5,4}} | collective-permute-start | bytes 5505032 | tf_op jit(solution)/shard_map/ppermute | solution.py:506
  273.1 35.1 %collective-permute-start.36 = (f32[256,1536]{1,0:T(8,128)}, f32[256,1536]{1,0:T(8,128)S(1)}, u32[]{:S(2)}, u32[]{:S(2)}) collective-permute-start(f32[256,1536]{1,0:T(8,128)} %collective-permute-done.29.refs_1_.refs_36_), channel_id=1, source_target_pairs={{9,17},{11,19},{13,21},{15,23}} | collective-permute-start | bytes 4718600 | tf_op jit(solution)/shard_map/ppermute | solution.py:506
  274.5 33.6 %collective-permute-start.37 = (f32[256,1280]{1,0:T(8,128)}, f32[256,1280]{1,0:T(8,128)S(1)}, u32[]{:S(2)}, u32[]{:S(2)}) collective-permute-start(f32[256,1280]{1,0:T(8,128)} %shard_map.57), channel_id=1, source_target_pairs={{1,9},{3,11},{5,13},{7,15}} | collective-permute-start | bytes 3932168 | tf_op jit(solution)/shard_map/ppermute | solution.py:506
  276.5 31.6 %collective-permute-start.38 = (f32[256,1024]{1,0:T(8,128)S(1)}, f32[256,1024]{1,0:T(8,128)}, u32[]{:S(2)}, u32[]{:S(2)}) collective-permute-start(f32[256,1024]{1,0:T(8,128)S(1)} %shard_map.58), channel_id=1, source_target_pairs={{8,10},{12,14},{16,18},{20,22}} | collective-permute-start | bytes 3145736 | tf_op jit(solution)/shard_map/ppermute | solution.py:506
  313.5 25.3 %collective-permute-start.44 = (f32[256,1536]{1,0:T(8,128)S(1)}, f32[256,1536]{1,0:T(8,128)S(1)}, u32[]{:S(2)}, u32[]{:S(2)}) collective-permute-start(f32[256,1536]{1,0:T(8,128)S(1)} %shard_map.60), channel_id=1, source_target_pairs={{9,8},{11,10},{13,12},{15,14},{17,16},{19,18},{21,20},{23,22},{5,4}} | collective-permute-start | bytes 4718600 | tf_op jit(solution)/shard_map/ppermute | solution.py:506
  315.5 23.3 %collective-permute-start.45 = (f32[256,1280]{1,0:T(8,128)S(1)}, f32[256,1280]{1,0:T(8,128)S(1)}, u32[]{:S(2)}, u32[]{:S(2)}) collective-permute-start(f32[256,1280]{1,0:T(8,128)S(1)} %collective-permute-done.37.refs_1_.refs_37_), channel_id=1, source_target_pairs={{9,17},{11,19},{13,21},{15,23}} | collective-permute-start | bytes 3932168 | tf_op jit(solution)/shard_map/ppermute | solution.py:506
  (77 other events, 1727.2 us)

commit v5 on v4

--- a/solution.py
+++ b/solution.py
@@ -9,8 +9,8 @@
 BASE = 128
 BLOCK = 256
 STAGES = (6, 3)
-FIRST = 2
-SECOND = (4, 6)
+FIRST = 3
+SECOND = (5, 7)
 THIRD = 8
 NN = ((1,), (0,))
 NT = ((1,), (1,))

time: 458 us -> 464 us (1.013)
  starting transfers between devices: 96.1 us -> 75.2 us
  waiting for transfers between devices: 232 us -> 252 us
  local copies, waits for them, and re-layouts: 16.4 us -> 22.7 us
    ppermute x57, starting transfers between devices: 96.1 us -> 75.2 us  [move(): return lax.ppermute(value, ('row', 'col'), flat)]
    ppermute x57, waiting for transfers between devices: 232 us -> 252 us  [move(): return lax.ppermute(value, ('row', 'col'), flat)]
    unnamed x88 -> x112, local copies, waits for them, and re-layouts: 9.5 us -> 15.8 us
  transfers between devices with their start and end apart: 57 -> 57, of which waited for: 7 -> 7; matrix products, arithmetic and copies ran while one was open for 0% -> 0% of each run, Pallas kernels for 5% -> 4%
where the time goes in v5:
time: 464 us; the launch traced here: 455 us
  waiting for transfers between devices  252 us (54%)
  Pallas kernels  95.7 us (21%)
  starting transfers between devices  75.2 us (16%)
  local copies, waits for them, and re-layouts  22.7 us (5%)
  loops' own time  5.88 us (1%)
    ppermute x57, waiting for transfers between devices, move(): return lax.ppermute(value, ('row', 'col'), flat)  252 us
    ppermute x57, starting transfers between devices, move(): return lax.ppermute(value, ('row', 'col'), flat)  75.2 us
    pallas_call x1, Pallas kernels, finish(): pl.pallas_call(lambda *refs: finish_kernel(len(raws), len(sets), *refs),...  70.8 us
    pallas_call x23, Pallas kernels, choose(): pl.pallas_call(kernel, out_shape=shape(size, width), in_specs=[SMEM] + [A...  22.5 us
    unnamed x112, local copies, waits for them, and re-layouts  15.8 us
  transfers between devices with their start and end apart: 57, of which 7 were waited for; matrix products, arithmetic and copies ran while one was open for 0% of the time, Pallas kernels for 4%

profile of v5, /device:TPU:12, one launch (start us, length us, event | category | flops | bytes accessed | tf_op | source)
XLA Modules:
  0.0 454.6 jit_solution(17473637253134996137)
XLA Ops:
  0.0 4.8 %slice_bitcast_fusion.1 = f32[1024,1024]{1,0:T(8,128)} fusion(f32[1,1,2,1,1024,1024]{5,4,3,2,1,0:T(8,128)} %param.7), kind=kLoop, calls=%fused_computation.65 | loop fusion | bytes 8388608 | tf_op jit(solution)/shard_map/squeeze | solution.py:542
  4.8 2.7 collective-permute-start.5
  7.7 2.1 collective-permute-start.6
  14.9 2.7 collective-permute-start.15
  17.6 2.7 collective-permute-start.14
  21.0 2.6 collective-permute-start.13
  33.1 88.8 %collective-permute-done.12.refs_0_.refs_3_ = f32[1024,1024]{1,0:T(8,128)} collective-permute-done((f32[1024,1024]{1,0:T(8,128)}, f32[1024,1024]{1,0:T(8,128)}, u32[]{:S(2)}, u32[]{:S(2)}) %collective-permute-start.12) | collective-permute-done | bytes 4194336 | tf_op jit(solution)/shard_map/ppermute | solution.py:506
  123.4 2.0 collective-permute-start.16
  126.0 2.3 collective-permute-start.17
  131.0 3.9 shard_map.48
  135.0 3.4 collective-permute-start.26
  139.5 2.0 collective-permute-start.20
  142.2 2.1 collective-permute-start.21
  144.8 40.4 %collective-permute-done.26.refs_2_.refs_7_ = f32[512,1024]{1,0:T(8,128)} collective-permute-done((f32[512,1024]{1,0:T(8,128)}, f32[512,1024]{1,0:T(8,128)}, u32[]{:S(2)}, u32[]{:S(2)}) %collective-permute-start.26) | collective-permute-done | bytes 2097184 | tf_op jit(solution)/shard_map/ppermute | solution.py:506
  194.9 2.4 shard_map.59
  197.3 3.5 collective-permute-start.43
  214.9 24.1 %collective-permute-done.43.refs_3_.refs_8_ = f32[512,1024]{1,0:T(8,128)S(1)} collective-permute-done((f32[512,1024]{1,0:T(8,128)S(1)}, f32[512,1024]{1,0:T(8,128)S(1)}, u32[]{:S(2)}, u32[]{:S(2)}) %collective-permute-start.43) | collective-permute-done | bytes 2097184 | tf_op jit(solution)/shard_map/ppermute | solution.py:506
  248.5 57.4 %collective-permute-done.37.refs_38_ = f32[256,1024]{1,0:T(8,128)S(1)} collective-permute-done((f32[256,1024]{1,0:T(8,128)}, f32[256,1024]{1,0:T(8,128)S(1)}, u32[]{:S(2)}, u32[]{:S(2)}) %collective-permute-start.37) | collective-permute-done | bytes 1048608 | tf_op jit(solution)/shard_map/ppermute | solution.py:506
  308.4 2.8 shard_map.63
  323.1 20.7 %collective-permute-done.46.refs_39_ = f32[256,768]{1,0:T(8,128)S(1)} collective-permute-done((f32[256,768]{1,0:T(8,128)S(1)}, f32[256,768]{1,0:T(8,128)S(1)}, u32[]{:S(2)}, u32[]{:S(2)}) %collective-permute-start.46) | collective-permute-done | bytes 786464 | tf_op jit(solution)/shard_map/ppermute | solution.py:506
  352.3 14.0 %collective-permute-done.54.refs_40_ = f32[256,512]{1,0:T(8,128)S(1)} collective-permute-done((f32[256,512]{1,0:T(8,128)S(1)}, f32[256,512]{1,0:T(8,128)S(1)}, u32[]{:S(2)}, u32[]{:S(2)}) %collective-permute-start.54) | collective-permute-done | bytes 524320 | tf_op jit(solution)/shard_map/ppermute | solution.py:506
  370.0 6.8 %collective-permute-done.59.refs_41_ = f32[256,256]{1,0:T(8,128)S(1)} collective-permute-done((f32[256,256]{1,0:T(8,128)S(1)}, f32[256,256]{1,0:T(8,128)S(1)}, u32[]{:S(2)}, u32[]{:S(2)}) %collective-permute-start.59) | collective-permute-done | bytes 262176 | tf_op jit(solution)/shard_map/ppermute | solution.py:506
  376.8 70.8 %shard_map.68 = (f32[2,1024,1024]{2,1,0:T(8,128)}, f32[1024,1024]{1,0:T(8,128)}) custom-call(s32[17]{0:T(128)} %copy-done.46, f32[2,1024,1024]{2,1,0:T(8,128)} %bitcast.38, f32[1024,1024]{1,0:T(8,128)} %collective-permute-done.5.refs_2_, f32[1024,1024]{1,0:T(8,128)} %collective-permute-done.12.refs_0_.refs_3_, ...), custom_call_target="tpu_custom_call" | custom-call | flops 60000002048 | bytes 67108864 | tf_op jit(solution)/shard_map/pallas_call | solution.py:491
  447.7 5.9 %conditional.1 = (f32[1024,1024]{1,0:T(8,128)}, f32[1024,1024]{1,0:T(8,128)}) conditional(s32[]{:T(128)} %convert_element_type.9, () %tuple.37, (s32[]{:T(128)}, f32[1024,1024]{1,0:T(8,128)}, f32[256,1024]{1,0:T(8,128)}, f32[256,768]{1,0:T(8,128)S(1)}, f32[256,512]{1,0:T(8,128)S(1)}, /*index=5*/f32[256,256]{1,0:T(8,128)S(1)}, ...), branch_computations={%region_0.0_spmd, %region_1.0_spmd} | conditional | flops 16927950848 | bytes 288393600 | solution.py:769
  (244 shorter events, 80.9 us)
Async XLA Ops:
  14.9 16.5 %collective-permute-start.15 = (f32[1024,1024]{1,0:T(8,128)}, f32[1024,1024]{1,0:T(8,128)}, u32[]{:S(2)}, u32[]{:S(2)}) collective-permute-start(f32[1024,1024]{1,0:T(8,128)} %slice_bitcast_fusion.1), channel_id=1, source_target_pairs={{5,0}} | collective-permute-start | bytes 12582920 | tf_op jit(solution)/shard_map/ppermute | solution.py:506
  23.7 98.3 %collective-permute-start.12 = (f32[1024,1024]{1,0:T(8,128)}, f32[1024,1024]{1,0:T(8,128)}, u32[]{:S(2)}, u32[]{:S(2)}) collective-permute-start(f32[1024,1024]{1,0:T(8,128)} %slice_bitcast_fusion.1), channel_id=1, source_target_pairs={{8,10},{9,11},{12,14},{13,15},{16,18},{17,19},{20,22},{21,23}} | collective-permute-start | bytes 12582920 | tf_op jit(solution)/shard_map/ppermute | solution.py:506
  30.6 91.4 %collective-permute-start.9 = (f32[256,2048]{1,0:T(8,128)S(1)}, f32[256,2048]{1,0:T(8,128)S(1)}, u32[]{:S(2)}, u32[]{:S(2)}) collective-permute-start(f32[256,2048]{1,0:T(8,128)S(1)} %shard_map.41), channel_id=1, source_target_pairs={{1,3},{5,7}} | collective-permute-start | bytes 6291464 | tf_op jit(solution)/shard_map/ppermute | solution.py:506
  31.4 90.6 %collective-permute-start.10 = (f32[256,1792]{1,0:T(8,128)}, f32[256,1792]{1,0:T(8,128)S(1)}, u32[]{:S(2)}, u32[]{:S(2)}) collective-permute-start(f32[256,1792]{1,0:T(8,128)} %collective-permute-done.8.refs_0_), channel_id=1, source_target_pairs={{1,5}} | collective-permute-start | bytes 5505032 | tf_op jit(solution)/shard_map/ppermute | solution.py:506
  32.2 89.8 %collective-permute-start.11 = (f32[256,1536]{1,0:T(8,128)S(1)}, f32[256,1536]{1,0:T(8,128)S(1)}, u32[]{:S(2)}, u32[]{:S(2)}) collective-permute-start(f32[256,1536]{1,0:T(8,128)S(1)} %get-tuple-element.140.refs_4_.refs_12_), channel_id=1, source_target_pairs={{0,1}} | collective-permute-start | bytes 4718600 | tf_op jit(solution)/shard_map/ppermute | solution.py:506
  128.3 59.7 %collective-permute-start.25 = (f32[1024,1024]{1,0:T(8,128)}, f32[1024,1024]{1,0:T(8,128)}, u32[]{:S(2)}, u32[]{:S(2)}) collective-permute-start(f32[1024,1024]{1,0:T(8,128)} %collective-permute-done.12.refs_0_.refs_3_), channel_id=1, source_target_pairs={{10,11},{14,15},{18,19},{22,23},{11,10},{15,14},{19,18},{23,22}} | collective-permute-start | bytes 12582920 | tf_op jit(solution)/shard_map/ppermute | solution.py:506
  135.0 50.2 %collective-permute-start.26 = (f32[512,1024]{1,0:T(8,128)}, f32[512,1024]{1,0:T(8,128)}, u32[]{:S(2)}, u32[]{:S(2)}) collective-permute-start(f32[512,1024]{1,0:T(8,128)} %shard_map.48), channel_id=1, source_target_pairs={{8,12},{9,13},{10,14},{11,15},{18,22},{19,23},{12,8},{13,9},{14,10... | collective-permute-start | bytes 6291464 | tf_op jit(solution)/shard_map/ppermute | solution.py:506
  138.8 48.3 %collective-permute-start.24 = (f32[256,1024]{1,0:T(8,128)}, f32[256,1024]{1,0:T(8,128)S(1)}, u32[]{:S(2)}, u32[]{:S(2)}) collective-permute-start(f32[256,1024]{1,0:T(8,128)} %get-tuple-element.158.refs_0_.refs_14_), channel_id=1, source_target_pairs={{0,4}} | collective-permute-start | bytes 3145736 | tf_op jit(solution)/shard_map/ppermute | solution.py:506
  139.5 48.5 %collective-permute-start.20 = (f32[256,2048]{1,0:T(8,128)}, f32[256,2048]{1,0:T(8,128)}, u32[]{:S(2)}, u32[]{:S(2)}) collective-permute-start(f32[256,2048]{1,0:T(8,128)} %collective-permute-done.16.refs_1_.refs_34_), channel_id=1, source_target_pairs={{9,17},{11,19},{13,21},{15,23}} | collective-permute-start | bytes 6291464 | tf_op jit(solution)/shard_map/ppermute | solution.py:506
  142.2 45.8 %collective-permute-start.21 = (f32[256,1792]{1,0:T(8,128)}, f32[256,1792]{1,0:T(8,128)}, u32[]{:S(2)}, u32[]{:S(2)}) collective-permute-start(f32[256,1792]{1,0:T(8,128)} %shard_map.46), channel_id=1, source_target_pairs={{1,9},{3,11},{5,13},{7,15}} | collective-permute-start | bytes 5505032 | tf_op jit(solution)/shard_map/ppermute | solution.py:506
  197.3 41.7 %collective-permute-start.43 = (f32[512,1024]{1,0:T(8,128)S(1)}, f32[512,1024]{1,0:T(8,128)S(1)}, u32[]{:S(2)}, u32[]{:S(2)}) collective-permute-start(f32[512,1024]{1,0:T(8,128)S(1)} %shard_map.59), channel_id=1, source_target_pairs={{8,12},{9,13},{10,14},{11,15},{18,22},{19,23},{12,8},{13,9},{14,10... | collective-permute-start | bytes 6291464 | tf_op jit(solution)/shard_map/ppermute | solution.py:506
  206.3 34.2 %collective-permute-start.42 = (f32[256,512]{1,0:T(8,128)S(1)}, f32[256,512]{1,0:T(8,128)S(1)}, u32[]{:S(2)}, u32[]{:S(2)}) collective-permute-start(f32[256,512]{1,0:T(8,128)S(1)} %get-tuple-element.177.refs_0_.refs_16_), channel_id=1, source_target_pairs={{0,4}} | collective-permute-start | bytes 1572872 | tf_op jit(solution)/shard_map/ppermute | solution.py:506
  212.0 34.1 %collective-permute-start.39 = (f32[256,1024]{1,0:T(8,128)}, f32[256,1024]{1,0:T(8,128)S(1)}, u32[]{:S(2)}, u32[]{:S(2)}) collective-permute-start(f32[256,1024]{1,0:T(8,128)} %shard_map.57), channel_id=1, source_target_pairs={{8,11},{12,15},{16,19},{20,23}} | collective-permute-start | bytes 3145736 | tf_op jit(solution)/shard_map/ppermute | solution.py:506
  212.7 29.2 %collective-permute-start.41 = (f32[256,768]{1,0:T(8,128)S(1)}, f32[256,768]{1,0:T(8,128)S(1)}, u32[]{:S(2)}, u32[]{:S(2)}) collective-permute-start(f32[256,768]{1,0:T(8,128)S(1)} %shard_map.58), channel_id=1, source_target_pairs={{0,16},{4,20}} | collective-permute-start | bytes 2359304 | tf_op jit(solution)/shard_map/ppermute | solution.py:506
  213.4 30.1 %collective-permute-start.40 = (f32[256,768]{1,0:T(8,128)S(1)}, f32[256,768]{1,0:T(8,128)S(1)}, u32[]{:S(2)}, u32[]{:S(2)}) collective-permute-start(f32[256,768]{1,0:T(8,128)S(1)} %shard_map.58), channel_id=1, source_target_pairs={{0,8},{4,12}} | collective-permute-start | bytes 2359304 | tf_op jit(solution)/shard_map/ppermute | solution.py:506
  239.0 66.9 %collective-permute-start.34 = (f32[256,1792]{1,0:T(8,128)}, f32[256,1792]{1,0:T(8,128)S(1)}, u32[]{:S(2)}, u32[]{:S(2)}) collective-permute-start(f32[256,1792]{1,0:T(8,128)} %shard_map.55), channel_id=1, source_target_pairs={{9,8},{11,10},{13,12},{15,14},{17,16},{19,18},{21,20},{23,22},{5,4}} | collective-permute-start | bytes 5505032 | tf_op jit(solution)/shard_map/ppermute | solution.py:506
  240.5 65.4 %collective-permute-start.35 = (f32[256,1536]{1,0:T(8,128)S(1)}, f32[256,1536]{1,0:T(8,128)S(1)}, u32[]{:S(2)}, u32[]{:S(2)}) collective-permute-start(f32[256,1536]{1,0:T(8,128)S(1)} %collective-permute-done.29.refs_1_.refs_36_), channel_id=1, source_target_pairs={{9,17},{11,19},{13,21},{15,23}} | collective-permute-start | bytes 4718600 | tf_op jit(solution)/shard_map/ppermute | solution.py:506
  242.8 63.1 %collective-permute-start.36 = (f32[256,1280]{1,0:T(8,128)S(1)}, f32[256,1280]{1,0:T(8,128)S(1)}, u32[]{:S(2)}, u32[]{:S(2)}) collective-permute-start(f32[256,1280]{1,0:T(8,128)S(1)} %shard_map.56), channel_id=1, source_target_pairs={{1,9},{3,11},{5,13},{7,15}} | collective-permute-start | bytes 3932168 | tf_op jit(solution)/shard_map/ppermute | solution.py:506
  247.1 58.8 %collective-permute-start.37 = (f32[256,1024]{1,0:T(8,128)}, f32[256,1024]{1,0:T(8,128)S(1)}, u32[]{:S(2)}, u32[]{:S(2)}) collective-permute-start(f32[256,1024]{1,0:T(8,128)} %shard_map.57), channel_id=1, source_target_pairs={{8,10},{12,14},{16,18},{20,22}} | collective-permute-start | bytes 3145736 | tf_op jit(solution)/shard_map/ppermute | solution.py:506
  311.2 33.4 %collective-permute-start.52 = (f32[1024,1024]{1,0:T(8,128)S(1)}, f32[1024,1024]{1,0:T(8,128)S(1)}, u32[]{:S(2)}, u32[]{:S(2)}) collective-permute-start(f32[1024,1024]{1,0:T(8,128)S(1)} %shard_map.63), channel_id=1, source_target_pairs={{16,17},{21,20},{9,8},{12,13},{8,9},{13,12},{10,11},{15,14}} | collective-permute-start | bytes 12582920 | tf_op jit(solution)/shard_map/ppermute | solution.py:506
  318.1 25.7 %collective-permute-start.44 = (f32[256,1536]{1,0:T(8,128)S(1)}, f32[256,1536]{1,0:T(8,128)S(1)}, u32[]{:S(2)}, u32[]{:S(2)}) collective-permute-start(f32[256,1536]{1,0:T(8,128)S(1)} %shard_map.60), channel_id=1, source_target_pairs={{9,8},{11,10},{13,12},{15,14},{17,16},{19,18},{21,20},{23,22},{5,4}} | collective-permute-start | bytes 4718600 | tf_op jit(solution)/shard_map/ppermute | solution.py:506
  320.1 23.7 %collective-permute-start.45 = (f32[256,1280]{1,0:T(8,128)S(1)}, f32[256,1280]{1,0:T(8,128)S(1)}, u32[]{:S(2)}, u32[]{:S(2)}) collective-permute-start(f32[256,1280]{1,0:T(8,128)S(1)} %collective-permute-done.36.refs_1_.refs_37_), channel_id=1, source_target_pairs={{9,17},{11,19},{13,21},{15,23}} | collective-permute-start | bytes 3932168 | tf_op jit(solution)/shard_map/ppermute | solution.py:506
  321.8 22.0 %collective-permute-start.46 = (f32[256,768]{1,0:T(8,128)S(1)}, f32[256,768]{1,0:T(8,128)S(1)}, u32[]{:S(2)}, u32[]{:S(2)}) collective-permute-start(f32[256,768]{1,0:T(8,128)S(1)} %shard_map.61), channel_id=1, source_target_pairs={{8,10},{12,14},{16,18},{20,22}} | collective-permute-start | bytes 2359304 | tf_op jit(solution)/shard_map/ppermute | solution.py:506
  345.5 20.9 %collective-permute-start.53 = (f32[256,1280]{1,0:T(8,128)S(1)}, f32[256,1280]{1,0:T(8,128)S(1)}, u32[]{:S(2)}, u32[]{:S(2)}) collective-permute-start(f32[256,1280]{1,0:T(8,128)S(1)} %shard_map.64), channel_id=1, source_target_pairs={{9,8},{11,10},{13,12},{15,14},{17,16},{19,18},{21,20},{23,22},{5,4}} | collective-permute-start | bytes 3932168 | tf_op jit(solution)/shard_map/ppermute | solution.py:506
  (89 other events, 1745.6 us)

commit v6 on v4

--- a/solution.py
+++ b/solution.py
@@ -9,6 +9,7 @@
 BASE = 128
 BLOCK = 256
 STAGES = (6, 3)
+EDGE = 1
 FIRST = 2
 SECOND = (4, 6)
 THIRD = 8
@@ -627,6 +628,19 @@
     meta = jnp.array(plan, jnp.int32)[row, col]
     meta = meta.at[8].set(edge_live.astype(jnp.int32))
 
+    def fetch():
+        if routed:
+            e0 = move(near, [((edge, 1), (edge - 2, 2))], cols)
+            e1 = move(e0, [((edge - 2, 2), (edge - 4, 2))], cols)
+            e2 = move(e0 + e1, [((r, 2), (r + 1, 2)) for r in (2, 4)], cols)
+            return e0 + e1 + e2
+        total = jnp.zeros_like(near)
+        for r in workers:
+            total = total + move(near, [((edge, 1), (r, 2))], cols)
+        return total
+
+    edge_tile = lax.cond(edge_live, lambda _: fetch(), lambda _: unset(near), 0)
+
     pieces, copies, state = [], [], None
     drain = max(STAGES[0], steps + STAGES[1]) - steps if routed else 0
     for slot in range(count + drain):
@@ -685,7 +699,9 @@
                 ]
             arrived[p] = new
         late = []
-        if slot == FIRST:
+        if slot == EDGE:
+            late = [edge_tile]
+        elif slot == FIRST:
             late = [r2, r3, r4, tile11]
         elif slot == SECOND[0]:
             late = [r5, r6[0]]
@@ -701,7 +717,9 @@
             state = flowing[-1]
         for p, new in arrived.items():
             copies[p] += new
-        if slot == FIRST:
+        if slot == EDGE:
+            (edge_tile,) = late
+        elif slot == FIRST:
             r2, r3, r4, tile11 = late
             r5 = move(r2, both_ways([((r, 2), (r, 3)) for r in workers]), cols)
             across = both_ways(
@@ -731,17 +749,6 @@
         sets = [[got[0] for got in copies]]
         last_pieces = sets[0][steps:]
 
-    def fetch():
-        if routed:
-            e0 = move(near, [((edge, 1), (edge - 2, 2))], cols)
-            e1 = move(e0, [((edge - 2, 2), (edge - 4, 2))], cols)
-            e2 = move(e0 + e1, [((r, 2), (r + 1, 2)) for r in (2, 4)], cols)
-            return e0 + e1 + e2
-        total = jnp.zeros_like(near)
-        for r in workers:
-            total = total + move(near, [((edge, 1), (r, 2))], cols)
-        return total
-
     result, panel1 = finish(meta, tiles, raws, sets)
     at_edge = edge_live & (row == edge)
     flags = jnp.stack(
@@ -752,9 +759,9 @@
     ).astype(jnp.int32)
 
     def edge_parts(args):
-        panel1, last_pieces = args
+        panel1, edge_tile, last_pieces = args
         far = tiles[1]
-        last = eliminate_last(fetch(), last_pieces)
+        last = eliminate_last(edge_tile, last_pieces)
         column = far - dot(panel1, last, NT, lax.Precision.HIGH)
         sent = move(column, [((r, 2), (edge, r % cols)) for r in workers], cols).T
         solved = move(last, [((edge - 2, 2), (edge, 1)), ((edge - 1, 2), (edge, 2))], cols)
@@ -766,7 +773,7 @@
     def no_edge(args):
         return unset(near), unset(near)
 
-    parts = lax.cond(edge_live, edge_parts, no_edge, (panel1, last_pieces))
+    parts = lax.cond(edge_live, edge_parts, no_edge, (panel1, edge_tile, last_pieces))
     return patch(flags, result, parts).reshape(kernel_tiles.shape)
 
 

time: 458 us -> 826 us (1.80)
  the two profiles are of different devices: /device:TPU:12 before, /device:TPU:25 now
where the time goes in v6:
time: 826 us; the launch traced here: 814 us
  waiting for transfers between devices  567 us (69%)
  starting transfers between devices  81.3 us (10%)
  local copies, waits for them, and re-layouts  58.8 us (7%)
  Pallas kernels  47.9 us (6%)
  matrix products  42.5 us (5%)
  other arithmetic  13.6 us (2%)
    ppermute x62, waiting for transfers between devices, move(): return lax.ppermute(value, ('row', 'col'), flat)  567 us
    ppermute x62, starting transfers between devices, move(): return lax.ppermute(value, ('row', 'col'), flat)  81.3 us
    dot_general x9, matrix products, dot(): lax.dot_general(a, b, (dims, ((), ())), precision=precision, preferred_el...  42.5 us
  transfers between devices with their start and end apart: 62, of which 3 were waited for; matrix products, arithmetic and copies ran while one was open for 2% of the time, Pallas kernels for 3%

profile of v6, /device:TPU:25, one launch (start us, length us, event | category | flops | bytes accessed | tf_op | source)
XLA Modules:
  0.0 814.4 jit_solution(5967562810978910413)
XLA Ops:
  0.0 4.8 slice_bitcast_fusion.1
  4.8 2.7 collective-permute-start.5
  7.5 2.7 collective-permute-start.12
  10.2 2.7 collective-permute-start.11
  12.9 2.7 collective-permute-start.10
  17.7 54.7 %conditional.2 = (f32[1024,1024]{1,0:T(8,128)}) conditional(s32[]{:T(128)} %convert_element_type.10, () %tuple.33, f32[1024,1024]{1,0:T(8,128)} %slice_bitcast_fusion.1), branch_computations={%region_0.0_spmd, %region_1.0_spmd} | conditional | flops 2097152 | bytes 75497600 | solution.py:642
  20.2 45.5 %collective-permute-done = f32[1024,1024]{1,0:T(8,128)S(1)} collective-permute-done((f32[1024,1024]{1,0:T(8,128)}, f32[1024,1024]{1,0:T(8,128)S(1)}, u32[]{:S(2)}, u32[]{:S(2)}) %collective-permute-start) | collective-permute-done | bytes 4194336 | tf_op jit(solution)/shard_map/cond/branch_1_fun/ppermute | solution.py:507
  69.0 2.9 add.49
  87.3 2.7 collective-permute-start.20
  102.3 8.5 %shard_map.42 = (f32[256,1024]{1,0:T(8,128)}, f32[768,768]{1,0:T(8,128)}) custom-call(s32[1]{0:T(128)} %bitcast.12.refs_0_, f32[1024,1024]{1,0:T(8,128)} %collective-permute-done.12.refs_1_, f32[256,2048]{1,0:T(8,128)} %get-tuple-element.136.refs_2_.refs_10_, f32[256,1792]{1,0:T(8,128)} %get-tuple-element.141.refs_3_.refs_11_, ...), custom_call_target="tpu_custom_call" | custom-call | flops 2000000000 | bytes 8388608 | tf_op jit(solution)/shard_map/pallas_call | solution.py:190
  147.3 2.7 collective-permute-start.52
  179.6 13.3 %shard_map.68 = (f32[2,1024,1024]{2,1,0:T(8,128)}, f32[1024,1024]{1,0:T(8,128)}) custom-call(s32[17]{0:T(128)} %copy-done.40, f32[2,1024,1024]{2,1,0:T(8,128)} %bitcast.40, f32[1024,1024]{1,0:T(8,128)} %collective-permute-done.5.refs_2_, f32[1024,1024]{1,0:T(8,128)} %collective-permute-done.9.refs_0_.refs_3_, ...), custom_call_target="tpu_custom_call" | custom-call | flops 60000002048 | bytes 67108864 | tf_op jit(solution)/shard_map/pallas_call | solution.py:492
  192.9 612.3 %conditional.3 = (f32[1024,1024]{1,0:T(8,128)}, f32[1024,1024]{1,0:T(8,128)}) conditional(s32[]{:T(128)} %convert_element_type.10, () %tuple.44, (s32[]{:T(128)}, f32[256,1024]{1,0:T(8,128)}, f32[1024,1024]{1,0:T(8,128)}, f32[256,768]{1,0:T(8,128)}, f32[256,512]{1,0:T(8,128)S(1)}, /*index=5*/f32[256,256]{1,0:T(8,128)S(1)}, ...), branch_computations={%region_2.0_spmd, %region_3.0_spmd} | conditional | flops 16925853696 | bytes 174098656 | solution.py:776
  206.4 4.0 slice_subtract_fusion
  214.8 8.7 %copy.17 = f32[2,1024,1024]{1,2,0:T(8,128)} copy(f32[2,1024,1024]{2,1,0:T(8,128)} %get-tuple-element.237) | data formatting | bytes 16777216 | tf_op jit(solution)/shard_map
  225.3 17.7 %bitcast_subtract_fusion = f32[1024,1024]{0,1:T(8,128)} fusion(f32[2,1024,1024]{1,2,0:T(8,128)} %copy.17, f32[1024,1024]{1,0:T(8,128)} %get-tuple-element.46, f32[1024,256]{0,1:T(8,128)S(1)} %fusion.9, f32[1024,256]{0,1:T(8,128)S(1)} %fusion.1, f32[1024,256]{0,1:T(8,128)S(1)} %fusion.3, f32[1024,256]{0,1:T(8,128)S(1)} %bitcast.42), kind=kOutput, calls=%fused_computation.9 | convolution fusion | flops 6446645248 | bytes 16777216 | tf_op jit(solution)/shard_map/cond/branch_1_fun/dot_general | solution.py:26
  248.1 474.1 %collective-permute-done.4 = f32[1024,1024]{0,1:T(8,128)} collective-permute-done((f32[1024,1024]{0,1:T(8,128)}, f32[1024,1024]{0,1:T(8,128)}, u32[]{:S(2)}, u32[]{:S(2)}) %collective-permute-start.4) | collective-permute-done | bytes 4194336 | tf_op jit(solution)/shard_map/cond/branch_1_fun/ppermute | solution.py:507
  722.2 5.5 copy.15
  727.8 47.1 %collective-permute-done.3 = f32[1024,1024]{0,1:T(8,128)} collective-permute-done((f32[1024,1024]{0,1:T(8,128)}, f32[1024,1024]{0,1:T(8,128)}, u32[]{:S(2)}, u32[]{:S(2)}) %collective-permute-start.3) | collective-permute-done | bytes 4194336 | tf_op jit(solution)/shard_map/cond/branch_1_fun/ppermute | solution.py:507
  774.9 6.8 bitcast_select_fusion.1
  781.7 5.3 copy.23
  787.0 12.7 %fusion = f32[1024,1024]{0,1:T(8,128)} fusion(f32[1024,1024]{0,1:T(8,128)} %bitcast_subtract_fusion, f32[1024,1024]{1,0:T(8,128)} %copy.15, f32[2,1024,1024]{1,2,0:T(8,128)} %copy.17, pred[]{:T(512)S(6)} %eq.29, pred[]{:T(512)S(6)} %eq.28, f32[1024,1024]{0,1:T(8,128)} %collective-permute-done.3), kind=kOutput, calls=%fused_computation.8 | convolution fusion | flops 6445596672 | bytes 25165826 | tf_op jit(solution)/shard_map/cond/branch_1_fun/dot_general | solution.py:26
  799.7 5.4 copy.25
  805.2 9.0 %shard_map.69 = f32[2,1024,1024]{2,1,0:T(8,128)} custom-call(s32[2]{0:T(128)S(1)} %add_convert_fusion.flags_ref, f32[2,1024,1024]{2,1,0:T(8,128)} %get-tuple-element.213.result_ref, f32[1024,1024]{1,0:T(8,128)} %get-tuple-element.240.refs_0_, f32[1024,1024]{1,0:T(8,128)} %get-tuple-element.241.refs_1_), custom_call_target="tpu_custom_call", output_to_operand_aliasing={{}: (1, {})} | custom-call | tf_op jit(solution)/shard_map/pallas_call | solution.py:261
  (273 shorter events, 123.6 us)
Async XLA Ops:
  4.8 12.0 %collective-permute-start.5 = (f32[1024,1024]{1,0:T(8,128)}, f32[1024,1024]{1,0:T(8,128)}, u32[]{:S(2)}, u32[]{:S(2)}) collective-permute-start(f32[1024,1024]{1,0:T(8,128)} %slice_bitcast_fusion.1), channel_id=1, source_target_pairs={{0,1},{8,9},{12,13},{16,17},{20,21},{1,0},{9,8},{13,12},{17,16},{2... | collective-permute-start | bytes 12582920 | tf_op jit(solution)/shard_map/ppermute | solution.py:507
  7.5 71.4 %collective-permute-start.12 = (f32[1024,1024]{1,0:T(8,128)}, f32[1024,1024]{1,0:T(8,128)}, u32[]{:S(2)}, u32[]{:S(2)}) collective-permute-start(f32[1024,1024]{1,0:T(8,128)} %slice_bitcast_fusion.1), channel_id=1, source_target_pairs={{5,0}} | collective-permute-start | bytes 12582920 | tf_op jit(solution)/shard_map/ppermute | solution.py:507
  10.2 74.4 %collective-permute-start.11 = (f32[1024,1024]{1,0:T(8,128)}, f32[1024,1024]{1,0:T(8,128)}, u32[]{:S(2)}, u32[]{:S(2)}) collective-permute-start(f32[1024,1024]{1,0:T(8,128)} %slice_bitcast_fusion.1), channel_id=1, source_target_pairs={{16,8},{17,9},{20,12},{21,13}} | collective-permute-start | bytes 12582920 | tf_op jit(solution)/shard_map/ppermute | solution.py:507
  12.9 71.7 %collective-permute-start.10 = (f32[1024,1024]{1,0:T(8,128)}, f32[1024,1024]{1,0:T(8,128)}, u32[]{:S(2)}, u32[]{:S(2)}) collective-permute-start(f32[1024,1024]{1,0:T(8,128)} %slice_bitcast_fusion.1), channel_id=1, source_target_pairs={{16,20},{17,21},{20,16},{21,17},{2,18},{3,19},{6,22},{7,23}} | collective-permute-start | bytes 12582920 | tf_op jit(solution)/shard_map/ppermute | solution.py:507
  16.9 59.9 %collective-permute-start.6 = (f32[256,2048]{1,0:T(8,128)}, f32[256,2048]{1,0:T(8,128)S(1)}, u32[]{:S(2)}, u32[]{:S(2)}) collective-permute-start(f32[256,2048]{1,0:T(8,128)} %get-tuple-element.136.refs_2_.refs_10_), channel_id=1, source_target_pairs={{0,1}} | collective-permute-start | bytes 6291464 | tf_op jit(solution)/shard_map/ppermute | solution.py:507
  17.8 48.0 %collective-permute-start = (f32[1024,1024]{1,0:T(8,128)}, f32[1024,1024]{1,0:T(8,128)S(1)}, u32[]{:S(2)}, u32[]{:S(2)}) collective-permute-start(f32[1024,1024]{1,0:T(8,128)} %param.3), channel_id=1, source_target_pairs={{25,18}} | collective-permute-start | bytes 12582920 | tf_op jit(solution)/shard_map/cond/branch_1_fun/ppermute | solution.py:507
  72.4 12.1 %collective-permute-start.9 = (f32[1024,1024]{1,0:T(8,128)}, f32[1024,1024]{1,0:T(8,128)}, u32[]{:S(2)}, u32[]{:S(2)}) collective-permute-start(f32[1024,1024]{1,0:T(8,128)} %slice_bitcast_fusion.1), channel_id=1, source_target_pairs={{8,10},{9,11},{12,14},{13,15},{16,18},{17,19},{20,22},{21,23}} | collective-permute-start | bytes 12582920 | tf_op jit(solution)/shard_map/ppermute | solution.py:507
  87.3 23.6 %collective-permute-start.20 = (f32[1024,1024]{1,0:T(8,128)}, f32[1024,1024]{1,0:T(8,128)}, u32[]{:S(2)}, u32[]{:S(2)}) collective-permute-start(f32[1024,1024]{1,0:T(8,128)} %collective-permute-done.9.refs_0_.refs_3_), channel_id=1, source_target_pairs={{10,11},{14,15},{18,19},{22,23},{11,10},{15,14},{19,18},{23,22}} | collective-permute-start | bytes 12582920 | tf_op jit(solution)/shard_map/ppermute | solution.py:507
  95.6 15.2 %collective-permute-start.16 = (f32[256,2048]{1,0:T(8,128)}, f32[256,2048]{1,0:T(8,128)}, u32[]{:S(2)}, u32[]{:S(2)}) collective-permute-start(f32[256,2048]{1,0:T(8,128)} %shard_map.43), channel_id=1, source_target_pairs={{1,9},{3,11},{5,13},{7,15}} | collective-permute-start | bytes 6291464 | tf_op jit(solution)/shard_map/ppermute | solution.py:507
  98.4 12.4 %collective-permute-start.17 = (f32[256,1792]{1,0:T(8,128)S(1)}, f32[256,1792]{1,0:T(8,128)}, u32[]{:S(2)}, u32[]{:S(2)}) collective-permute-start(f32[256,1792]{1,0:T(8,128)S(1)} %shard_map.44), channel_id=1, source_target_pairs={{1,3},{5,7}} | collective-permute-start | bytes 5505032 | tf_op jit(solution)/shard_map/ppermute | solution.py:507
  100.4 10.5 %collective-permute-start.18 = (f32[256,1536]{1,0:T(8,128)}, f32[256,1536]{1,0:T(8,128)S(1)}, u32[]{:S(2)}, u32[]{:S(2)}) collective-permute-start(f32[256,1536]{1,0:T(8,128)} %collective-permute-done.15.refs_0_), channel_id=1, source_target_pairs={{1,5}} | collective-permute-start | bytes 4718600 | tf_op jit(solution)/shard_map/ppermute | solution.py:507
  101.1 9.7 %collective-permute-start.19 = (f32[256,1280]{1,0:T(8,128)S(1)}, f32[256,1280]{1,0:T(8,128)S(1)}, u32[]{:S(2)}, u32[]{:S(2)}) collective-permute-start(f32[256,1280]{1,0:T(8,128)S(1)} %copy-done.17), channel_id=1, source_target_pairs={{0,1}} | collective-permute-start | bytes 3932168 | tf_op jit(solution)/shard_map/ppermute | solution.py:507
  110.9 10.6 %collective-permute-start.26 = (f32[256,1024]{1,0:T(8,128)}, f32[256,1024]{1,0:T(8,128)S(1)}, u32[]{:S(2)}, u32[]{:S(2)}) collective-permute-start(f32[256,1024]{1,0:T(8,128)} %get-tuple-element.165.refs_0_.refs_14_), channel_id=1, source_target_pairs={{0,4}} | collective-permute-start | bytes 3145736 | tf_op jit(solution)/shard_map/ppermute | solution.py:507
  111.6 14.4 %collective-permute-start.22 = (f32[256,2048]{1,0:T(8,128)}, f32[256,2048]{1,0:T(8,128)}, u32[]{:S(2)}, u32[]{:S(2)}) collective-permute-start(f32[256,2048]{1,0:T(8,128)} %collective-permute-done.16.refs_1_.refs_34_), channel_id=1, source_target_pairs={{9,17},{11,19},{13,21},{15,23}} | collective-permute-start | bytes 6291464 | tf_op jit(solution)/shard_map/ppermute | solution.py:507
  114.4 11.6 %collective-permute-start.23 = (f32[256,1792]{1,0:T(8,128)}, f32[256,1792]{1,0:T(8,128)}, u32[]{:S(2)}, u32[]{:S(2)}) collective-permute-start(f32[256,1792]{1,0:T(8,128)} %shard_map.47), channel_id=1, source_target_pairs={{1,9},{3,11},{5,13},{7,15}} | collective-permute-start | bytes 5505032 | tf_op jit(solution)/shard_map/ppermute | solution.py:507
  119.5 13.4 %collective-permute-start.34 = (f32[512,1024]{1,0:T(8,128)}, f32[512,1024]{1,0:T(8,128)}, u32[]{:S(2)}, u32[]{:S(2)}) collective-permute-start(f32[512,1024]{1,0:T(8,128)} %shard_map.54), channel_id=1, source_target_pairs={{8,12},{9,13},{10,14},{11,15},{18,22},{19,23},{12,8},{13,9},{14,10... | collective-permute-start | bytes 6291464 | tf_op jit(solution)/shard_map/ppermute | solution.py:507
  127.1 10.2 %collective-permute-start.32 = (f32[256,1024]{1,0:T(8,128)}, f32[256,1024]{1,0:T(8,128)S(1)}, u32[]{:S(2)}, u32[]{:S(2)}) collective-permute-start(f32[256,1024]{1,0:T(8,128)} %shard_map.53), channel_id=1, source_target_pairs={{0,16},{4,20}} | collective-permute-start | bytes 3145736 | tf_op jit(solution)/shard_map/ppermute | solution.py:507
  129.2 10.8 %collective-permute-start.27 = (f32[256,2048]{1,0:T(8,128)S(1)}, f32[256,2048]{1,0:T(8,128)}, u32[]{:S(2)}, u32[]{:S(2)}) collective-permute-start(f32[256,2048]{1,0:T(8,128)S(1)} %shard_map.50), channel_id=1, source_target_pairs={{9,8},{11,10},{13,12},{15,14},{17,16},{19,18},{21,20},{23,22},{5,4}} | collective-permute-start | bytes 6291464 | tf_op jit(solution)/shard_map/ppermute | solution.py:507
  140.1 10.0 %collective-permute-start.43 = (f32[256,512]{1,0:T(8,128)}, f32[256,512]{1,0:T(8,128)S(1)}, u32[]{:S(2)}, u32[]{:S(2)}) collective-permute-start(f32[256,512]{1,0:T(8,128)} %get-tuple-element.183.refs_0_.refs_16_), channel_id=1, source_target_pairs={{0,4}} | collective-permute-start | bytes 1572872 | tf_op jit(solution)/shard_map/ppermute | solution.py:507
  142.0 9.5 %collective-permute-start.42 = (f32[256,768]{1,0:T(8,128)S(1)}, f32[256,768]{1,0:T(8,128)S(1)}, u32[]{:S(2)}, u32[]{:S(2)}) collective-permute-start(f32[256,768]{1,0:T(8,128)S(1)} %shard_map.59), channel_id=1, source_target_pairs={{0,16},{4,20}} | collective-permute-start | bytes 2359304 | tf_op jit(solution)/shard_map/ppermute | solution.py:507
  143.1 10.4 %collective-permute-start.41 = (f32[256,768]{1,0:T(8,128)S(1)}, f32[256,768]{1,0:T(8,128)S(1)}, u32[]{:S(2)}, u32[]{:S(2)}) collective-permute-start(f32[256,768]{1,0:T(8,128)S(1)} %shard_map.59), channel_id=1, source_target_pairs={{0,8},{4,12}} | collective-permute-start | bytes 2359304 | tf_op jit(solution)/shard_map/ppermute | solution.py:507
  147.3 20.8 %collective-permute-start.52 = (f32[1024,1024]{1,0:T(8,128)S(1)}, f32[1024,1024]{1,0:T(8,128)}, u32[]{:S(2)}, u32[]{:S(2)}) collective-permute-start(f32[1024,1024]{1,0:T(8,128)S(1)} %shard_map.63), channel_id=1, source_target_pairs={{16,17},{21,20},{9,8},{12,13},{8,9},{13,12},{10,11},{15,14}} | collective-permute-start | bytes 12582920 | tf_op jit(solution)/shard_map/ppermute | solution.py:507
  243.0 479.2 %collective-permute-start.4 = (f32[1024,1024]{0,1:T(8,128)}, f32[1024,1024]{0,1:T(8,128)}, u32[]{:S(2)}, u32[]{:S(2)}) collective-permute-start(f32[1024,1024]{0,1:T(8,128)} %bitcast_subtract_fusion), channel_id=1, source_target_pairs={{10,26},{14,27},{18,24},{22,25}} | collective-permute-start | bytes 12582920 | tf_op jit(solution)/shard_map/cond/branch_1_fun/ppermute | solution.py:507
  246.8 528.0 %collective-permute-start.3 = (f32[1024,1024]{0,1:T(8,128)}, f32[1024,1024]{0,1:T(8,128)}, u32[]{:S(2)}, u32[]{:S(2)}) collective-permute-start(f32[1024,1024]{0,1:T(8,128)} %pad_maximum_fusion), channel_id=1, source_target_pairs={{18,25},{22,26}} | collective-permute-start | bytes 12582920 | tf_op jit(solution)/shard_map/cond/branch_1_fun/ppermute | solution.py:507
  (89 other events, 573.7 us)
